TPU v7x, 128 devices: a whole 4x4x4 slice. The times are simulated.
128 devices in a mesh: dp: 8 (over z, x_hi), latent: 16 (over x_lo, y, core).
Axes of the slice: x: 4 (x_hi: 2, x_lo: 2; x = x_hi * 2 + x_lo), y: 4, z: 4, core: 2. Of those that a mesh axis runs over, the one named last changes fastest.
Arguments:
- tokens: bfloat16 [512, 4608], P(('dp', 'latent')), may hold values from -6 to 6
- batch_order: int32 [512], replicated, may hold values from 0 to 511, each once
- enc_weight: bfloat16 [4608, 65536], P(None, ('dp', 'latent')), may hold values from -0.09375 to 0.09375
- enc_bias: float32 [65536], P(('dp', 'latent')), may hold values from -0.5 to 0.5
- dec_weight: bfloat16 [65536, 4608], P(('dp', 'latent')), may hold values from -0.25 to 0.25
Outputs:
- recon_error: float32 [512, 4608], P(('dp', 'latent'))
- enc_grad: bfloat16 [4608, 65536], P(None, ('dp', 'latent'))
- dec_grad: bfloat16 [65536, 4608], P(('dp', 'latent'))
- bias_grad: float32 [65536], P(('dp', 'latent'))
Inputs may be any that keep to these rules, and one draw needn't show every extreme that they name: `batch_order`: each number from 0 to 511 appears once.
All inputs are finite; a program needn't handle non-finite values.
Results may differ from a plain program's by a relative error of at most 0.025.
Values may be sent and summed in bfloat16 or wider, within the bound.
No kernel may reach another device: no remote copies, remote signals or barrier semaphores. Data moves between devices by JAX's collectives and lax.ppermute only.
A program may use at most 128 MiB of HBM per device.

v0:
```python
import math

import jax
import jax.numpy as jnp
from jax import lax
from jax.sharding import PartitionSpec as P


def per_device(tokens, batch_order, enc_weight, enc_bias, dec_weight):
    rows_dev = tokens.shape[0]
    total_rows = batch_order.shape[0]
    lane_count = lax.axis_size("latent")
    row_scale = math.sqrt(total_rows)
    contract_rows = (((0,), (0,)), ((), ()))
    gathered = lax.all_gather(tokens, ("dp", "latent"), axis=0, tiled=True)
    positions = jnp.arange(total_rows, dtype=jnp.int32)
    row_first = (lax.axis_index("dp") * lane_count + lax.axis_index("latent")) * rows_dev
    local_order = jnp.take(batch_order, positions, axis=0)
    inputs = jnp.take(gathered, local_order, axis=0)
    preact = jnp.dot(inputs, enc_weight, preferred_element_type=jnp.float32) + enc_bias
    positive = jnp.maximum(preact, 0.0)
    activations = positive.astype(jnp.bfloat16)
    sliced = activations
    summed = lax.psum_scatter(
        jnp.dot(sliced, dec_weight, preferred_element_type=jnp.float32),
        ("dp", "latent"),
        scatter_dimension=0,
        tiled=True,
    )
    own_inputs = lax.dynamic_slice_in_dim(inputs, row_first, rows_dev, 0)
    recon_error = summed - own_inputs.astype(jnp.float32)
    err_grad = (recon_error / row_scale).astype(jnp.bfloat16)
    dec_wide = dec_weight.astype(jnp.float32)
    row_norms = jnp.sqrt(jnp.sum(dec_wide * dec_wide, axis=1) + 1e-06)
    act_total = jnp.sum(activations.astype(jnp.float32), axis=0) / row_scale
    piece = lax.all_gather(err_grad, ("dp", "latent"), axis=0, tiled=True)
    sliced = activations
    dec_accum = lax.dot_general(sliced, piece, contract_rows, preferred_element_type=jnp.float32)
    product = lax.dot_general(
        piece, dec_weight, (((1,), (1,)), ((), ())), preferred_element_type=jnp.float32
    )
    act_grad = product
    dec_accum, act_grad = (dec_accum, act_grad)
    act_grad = act_grad + row_norms / row_scale
    pre_grad = jnp.where(preact > 0.0, act_grad, jnp.zeros_like(act_grad)).astype(jnp.bfloat16)
    enc_grad = lax.dot_general(
        inputs, pre_grad, contract_rows, preferred_element_type=jnp.float32
    ).astype(jnp.bfloat16)
    bias_grad = jnp.sum(pre_grad.astype(jnp.float32), axis=0)
    dec_grad = (dec_accum + act_total[:, None] * dec_wide / row_norms[:, None]).astype(jnp.bfloat16)
    return (recon_error, enc_grad, dec_grad, bias_grad)


def solution(mesh):
    return jax.shard_map(
        per_device,
        mesh=mesh,
        in_specs=(
            P(("dp", "latent"), None),
            P(),
            P(None, ("dp", "latent")),
            P(("dp", "latent")),
            P(("dp", "latent"), None),
        ),
        out_specs=(
            P(("dp", "latent"), None),
            P(None, ("dp", "latent")),
            P(("dp", "latent"), None),
            P(("dp", "latent")),
        ),
        check_vma=False,
    )
```

profile of v0, /device:TPU:1, one launch (start us, length us, event | category | flops | bytes accessed | tf_op | source)
XLA Modules:
  0.0 379.5 jit_solution(9737593984599430941)
XLA Ops:
  7.2 0.0 copy-start
  7.2 0.0 all-gather.5.cloned.1.call-start
  7.2 0.7 all-gather.5.cloned.1.call-update
  7.9 0.0 all-reduce.3.cloned.1.call-start
  8.0 0.0 copy-done
  8.0 3.5 gather_fusion
  11.6 70.3 %all-gather.5.cloned.1.call-done = bf16[128,4,4608]{2,1,0:T(4,128)(2,1)} async-done(((bf16[1,4,4608]{2,1,0:T(4,128)(2,1)}), bf16[128,4,4608]{2,1,0:T(4,128)(2,1)}) %all-gather.5.cloned.1.call-update) | async-done | bytes 4718608 | tf_op jit(solution)/shard_map/all_gather | solution.py:15
  81.9 7.2 %reshape.70 = bf16[512,4608]{1,0:T(8,128)(2,1)} reshape(bf16[128,4,4608]{2,1,0:T(4,128)(2,1)} %all-gather.5.cloned.1.call-done) | data formatting | bytes 9437184
  89.1 12.6 %gather_fusion.1 = bf16[512,4608]{1,0:T(8,128)(2,1)} fusion(bf16[512,4608]{1,0:T(8,128)(2,1)} %reshape.70, s32[1024]{0:T(1024)S(1)} %pad_clamp_fusion), kind=kCustom, calls=%fused_computation.1 | custom fusion | bytes 9439232 | tf_op jit(solution)/shard_map/jit(_take)/gather | solution.py:19
  101.6 0.0 copy-start.4
  101.6 0.0 slice-start
  101.6 2.9 broadcast_select_fusion
  104.5 0.0 copy-done.4
  104.5 0.0 copy-start.2
  104.5 0.0 slice-start.1
  104.5 6.4 %convert_reduce_fusion.1 = (f32[512]{0:T(512)S(1)}, f32[512,512]{1,0:T(8,128)S(1)}) fusion(f32[512]{0:T(512)S(1)} %copy-done.4, bf16[512,4608]{1,0:T(8,128)(2,1)S(1)} %broadcast_select_fusion, bf16[4608,512]{1,0:T(8,128)(2,1)} %param.7), kind=kOutput, calls=%fused_computation.15 | convolution fusion | flops 2416967168 | bytes 10489856 | tf_op jit(solution)/shard_map/dot_general | solution.py:20
  110.9 0.0 copy-done.2
  110.9 0.0 slice-done
  110.9 0.0 slice-done.1
  110.9 5.1 %fusion.7 = f32[512,4608]{1,0:T(8,128)} fusion(bf16[512,4608]{1,0:T(8,128)(2,1)S(1)} %bitcast.14, f32[512,512]{1,0:T(8,128)S(1)} %get-tuple-element.9), kind=kOutput, calls=%fused_computation.30 | convolution fusion | flops 2416443392 | bytes 15204352 | tf_op jit(solution)/shard_map/dot_general | solution.py:25
  116.0 0.0 all-reduce.3.cloned.1.call-update
  116.1 0.2 all-gather.7.cloned.1.call-start
  116.3 160.8 %all-reduce.3.cloned.1.call-done = f32[512,4608]{1,0:T(8,128)} async-done(((f32[512,4608]{1,0:T(8,128)}), f32[512,4608]{1,0:T(8,128)}) %all-reduce.3.cloned.1.call-update) | async-done | bytes 9437200
  277.1 1.6 fusion.6
  278.7 0.0 all-gather.7.cloned.1.call-update
  278.8 3.3 fusion
  282.1 64.7 %all-gather.7.cloned.1.call-done = bf16[128,4,4608]{2,1,0:T(4,128)(2,1)} async-done(((bf16[1,4,4608]{2,1,0:T(4,128)(2,1)}), bf16[128,4,4608]{2,1,0:T(4,128)(2,1)}) %all-gather.7.cloned.1.call-update) | async-done | bytes 4718608 | tf_op jit(solution)/shard_map/all_gather | solution.py:36
  346.8 0.0 slice-start.2
  346.8 7.3 %reshape.72 = bf16[512,4608]{1,0:T(8,128)(2,1)} reshape(bf16[128,4,4608]{2,1,0:T(4,128)(2,1)} %all-gather.7.cloned.1.call-done) | data formatting | bytes 9437184
  354.1 0.0 slice-start.3
  354.1 7.1 %convert_reduce_fusion = (f32[512]{0:T(512)}, bf16[512,512]{1,0:T(8,128)(2,1)S(1)}) fusion(f32[512]{0:T(512)S(1)} %get-tuple-element.7, bf16[512,4608]{1,0:T(8,128)(2,1)} %reshape.72, bf16[512,4608]{1,0:T(8,128)(2,1)} %param.9, f32[512,512]{1,0:T(8,128)S(1)} %get-tuple-element.9), kind=kOutput, calls=%fused_computation.14 | convolution fusion | flops 2417491456 | bytes 11014144 | tf_op jit(solution)/shard_map/dot_general | solution.py:39
  361.2 0.0 copy-start.3
  361.2 6.8 %convolution_convert_fusion = bf16[4608,512]{1,0:T(8,128)(2,1)} fusion(bf16[512,4608]{1,0:T(8,128)(2,1)} %copy-done.2, bf16[512,512]{1,0:T(8,128)(2,1)S(1)} %get-tuple-element.11), kind=kOutput, calls=%fused_computation.8 | convolution fusion | flops 2418278400 | bytes 9961472 | tf_op jit(solution)/shard_map/dot_general | solution.py:46
  368.0 0.0 slice-done.2
  368.0 0.0 slice-done.3
  368.0 0.0 copy-done.3
  368.0 0.0 copy-start.1
  368.0 5.0 %fusion.3 = bf16[512,4608]{1,0:T(8,128)(2,1)} fusion(bf16[512,4608]{1,0:T(8,128)(2,1)S(1)} %bitcast.16, bf16[512,4608]{1,0:T(8,128)(2,1)S(1)} %copy-done.3, f32[512]{0:T(512)S(1)} %get-tuple-element.6, f32[512]{0:T(512)S(1)} %get-tuple-element.12, f32[512,512]{1,0:T(8,128)S(1)} %get-tuple-element.9), kind=kOutput, calls=%fused_computation.7 | convolution fusion | flops 2428239872 | bytes 15208448 | tf_op jit(solution)/shard_map/dot_general | solution.py:38
  373.0 0.0 copy-done.1
  (8 shorter events, 0.0 us)
Async XLA Ops:
  7.2 0.8 copy-start
  7.2 74.7 %all-gather.5.cloned.1.call-start = ((), (), s32[]{:S(2)}) async-start(), calls=%async_computation | async-start | bytes 4755456 | tf_op jit(solution)/shard_map/all_gather | solution.py:15
  7.9 269.2 %all-reduce.3.cloned.1.call-start = ((), (), s32[]{:S(2)}) async-start(), calls=%async_computation.2 | async-start | bytes 18874368
  101.6 2.9 copy-start.4
  101.6 9.3 %slice-start = ((s8[4718592]{0:T(1024)(128)(4,1)}), s8[524288]{0:T(1024)(128)(4,1)S(1)}, s32[]{:S(2)}) async-start(s8[4718592]{0:T(1024)(128)(4,1)} %bitcast.13), calls=%async_computation.3 | async-start | bytes 1048576
  104.5 6.4 %copy-start.2 = (bf16[512,4608]{1,0:T(8,128)(2,1)}, bf16[512,4608]{1,0:T(8,128)(2,1)S(1)}, u32[]{:S(2)}) copy-start(bf16[512,4608]{1,0:T(8,128)(2,1)S(1)} %broadcast_select_fusion) | copy-start | bytes 14155780
  104.5 6.4 %slice-start.1 = ((s8[4718592]{0:T(1024)(128)(4,1)}), s8[4194304]{0:T(1024)(128)(4,1)S(1)}, s32[]{:S(2)}) async-start(s8[4718592]{0:T(1024)(128)(4,1)} %bitcast.13), calls=%async_computation.4 | async-start | bytes 8388608
  116.1 230.7 %all-gather.7.cloned.1.call-start = ((), (), s32[]{:S(2)}) async-start(), calls=%async_computation.1 | async-start | bytes 4755456 | tf_op jit(solution)/shard_map/all_gather | solution.py:36
  346.8 21.2 %slice-start.2 = ((s8[4718592]{0:T(1024)(128)(4,1)}), s8[524288]{0:T(1024)(128)(4,1)S(1)}, s32[]{:S(2)}) async-start(s8[4718592]{0:T(1024)(128)(4,1)} %bitcast.15), calls=%async_computation.5 | async-start | bytes 1048576
  354.1 14.0 %slice-start.3 = ((s8[4718592]{0:T(1024)(128)(4,1)}), s8[4194304]{0:T(1024)(128)(4,1)S(1)}, s32[]{:S(2)}) async-start(s8[4718592]{0:T(1024)(128)(4,1)} %bitcast.15), calls=%async_computation.6 | async-start | bytes 8388608
  361.2 6.8 %copy-start.3 = (bf16[512,4608]{1,0:T(8,128)(2,1)S(1)}, bf16[512,4608]{1,0:T(8,128)(2,1)}, u32[]{:S(2)}) copy-start(bf16[512,4608]{1,0:T(8,128)(2,1)} %reshape.72) | copy-start | bytes 14155780
  368.0 5.0 %copy-start.1 = (s32[512]{0:T(512)S(1)}, s32[512]{0:T(512)}, u32[]{:S(2)}) copy-start(s32[512]{0:T(512)} %param.6) | copy-start | bytes 6148
Sparse Core Ops, SparseCore 0:
  11.1 70.7 all-gather.4
  116.2 160.8 all-reduce.2
  280.8 65.9 all-gather.6
where the time goes:
time: 380 us
  waiting for transfers between devices  297 us (78%)
  local copies, waits for them, and re-layouts  30.6 us (8%)
  matrix products  30.4 us (8%)
  between operations  13.9 us (4%)
  other arithmetic  7.88 us (2%)
    unnamed x4, waiting for transfers between devices  162 us
    all_gather x1, waiting for transfers between devices, per_device(): gathered = lax.all_gather(tokens, ('dp', 'latent'), axis=0, tiled=True)  70.3 us
    all_gather x1, waiting for transfers between devices, per_device(): piece = lax.all_gather(err_grad, ('dp', 'latent'), axis=0, tiled=True)  64.7 us
    unnamed x20, local copies, waits for them, and re-layouts  14.5 us
    gather x1, local copies, waits for them, and re-layouts, per_device(): inputs = jnp.take(gathered, local_order, axis=0)  12.6 us
  transfers between devices with their start and end apart: 3, of which 3 were waited for; matrix products, arithmetic and copies ran while one was open for 2% of the time, Pallas kernels for 0%

commit v1 on v0

v1 whole, which is shorter than its diff:
```python
import math

import jax
import jax.numpy as jnp
from jax import lax
from jax.sharding import Mesh, PartitionSpec as P

CHIPS = ("z", "xh", "xl", "y")
SWAP = [(0, 1), (1, 0)]


def gather_chips(block):
    chips = lax.axis_size(CHIPS)
    copies = jnp.broadcast_to(block[None], (chips,) + block.shape)
    out = lax.all_to_all(copies, CHIPS, 0, 0)
    return out.reshape(chips * block.shape[0], block.shape[1])


def per_device(tokens, batch_order, enc_weight, enc_bias, dec_weight):
    rows_dev, width = tokens.shape
    total_rows = batch_order.shape[0]
    row_scale = math.sqrt(total_rows)
    half = width // 2
    chips = lax.axis_size(CHIPS)
    contract_rows = (((0,), (0,)), ((), ()))
    core = lax.axis_index("c")
    own = core * half
    oth = (1 - core) * half

    def pick(a, start):
        return lax.dynamic_slice_in_dim(a, start, half, 1)

    got = lax.ppermute(pick(tokens, oth), "c", SWAP)
    mine = pick(tokens, own)
    block = jnp.where(core == 0, jnp.concatenate([mine, got]), jnp.concatenate([got, mine]))
    x_own = gather_chips(block)
    x_oth = lax.ppermute(x_own, "c", SWAP)
    inputs = jnp.where(core == 0, jnp.concatenate([x_own, x_oth], 1), jnp.concatenate([x_oth, x_own], 1))
    preact = jnp.dot(inputs, enc_weight, preferred_element_type=jnp.float32) + enc_bias
    activations = jnp.maximum(preact, 0.0).astype(jnp.bfloat16)

    part_oth = jnp.dot(activations, pick(dec_weight, oth), preferred_element_type=jnp.float32)
    part_got = lax.ppermute(part_oth.astype(jnp.bfloat16), "c", SWAP)
    part_own = jnp.dot(activations, pick(dec_weight, own), preferred_element_type=jnp.float32)
    part = (part_own + part_got.astype(jnp.float32)).astype(jnp.bfloat16)
    pieces = lax.all_to_all(part.reshape(chips, total_rows // chips, half), CHIPS, 0, 0)
    recon = jnp.sum(pieces.astype(jnp.float32), axis=0) - block.astype(jnp.float32)
    err_block = (recon / row_scale).astype(jnp.bfloat16)
    e_own = gather_chips(err_block)
    e_oth = lax.ppermute(e_own, "c", SWAP)
    err = jnp.where(core == 0, jnp.concatenate([e_own, e_oth], 1), jnp.concatenate([e_oth, e_own], 1))

    dec_wide = dec_weight.astype(jnp.float32)
    row_norms = jnp.sqrt(jnp.sum(dec_wide * dec_wide, axis=1) + 1e-06)
    act_total = jnp.sum(activations.astype(jnp.float32), axis=0) / row_scale
    dec_accum = lax.dot_general(activations, err, contract_rows, preferred_element_type=jnp.float32)
    dec_grad = (dec_accum + act_total[:, None] * dec_wide / row_norms[:, None]).astype(jnp.bfloat16)
    act_grad = lax.dot_general(err, dec_weight, (((1,), (1,)), ((), ())), preferred_element_type=jnp.float32)
    act_grad = act_grad + row_norms / row_scale
    pre_grad = jnp.where(preact > 0.0, act_grad, 0.0).astype(jnp.bfloat16)
    enc_grad = lax.dot_general(inputs, pre_grad, contract_rows, preferred_element_type=jnp.float32)
    bias_grad = jnp.sum(pre_grad.astype(jnp.float32), axis=0)

    first = lax.axis_index(CHIPS + ("c",)) * rows_dev
    wanted = lax.dynamic_slice_in_dim(batch_order, first, rows_dev)
    recon_error = jnp.take(err, wanted, axis=0).astype(jnp.float32) * row_scale
    return (recon_error, enc_grad.astype(jnp.bfloat16), dec_grad, bias_grad)


def solution(mesh):
    names = CHIPS + ("c",)
    split = Mesh(mesh.devices.reshape(4, 2, 2, 4, 2), names)
    return jax.shard_map(
        per_device,
        mesh=split,
        in_specs=(P(names, None), P(), P(None, names), P(names), P(names, None)),
        out_specs=(P(names, None), P(None, names), P(names, None), P(names)),
        check_vma=False,
    )
```

time: 380 us -> 177 us (0.47)
  waiting for transfers between devices: 297 us -> 9.33 us
  blocking collectives: 0 us -> 118 us
  local copies, waits for them, and re-layouts: 30.6 us -> 4.74 us
  between operations: 13.9 us -> 0.74 us
  starting transfers between devices: 0.3 us -> 6.16 us
    unnamed x4 -> x0, waiting for transfers between devices: 162 us -> none
    all_gather x2 -> x0, waiting for transfers between devices: 135 us -> none  [the longest x1 70.3 us: per_device(): gathered = lax.all_gather(tokens, ('dp', 'latent'), axis=0, tiled=True)]
    all_to_all x0 -> x3, blocking collectives: none -> 118 us  [the longest x2 80.5 us: gather_chips(): out = lax.all_to_all(copies, CHIPS, 0, 0)]
    unnamed x20, local copies, waits for them, and re-layouts: 14.5 us -> 0.04 us
    gather x2 -> x1, local copies, waits for them, and re-layouts: 16.1 us -> 3.63 us  [per_device(): recon_error = jnp.take(err, wanted, axis=0).astype(jnp.float32) * row_scale]
    ppermute x0 -> x4, waiting for transfers between devices: none -> 9.33 us  [the longest x1 4.16 us: per_device(): x_oth = lax.ppermute(x_own, 'c', SWAP)]
    ppermute x0 -> x4, starting transfers between devices: none -> 6.16 us  [the longest x1 2.61 us: per_device(): e_oth = lax.ppermute(e_own, 'c', SWAP)]
    dot_general x3 -> x4, matrix products: 17.2 us -> 16.7 us  [the longest x1 7.37 us: per_device(): lax.dot_general(err, dec_weight, (((1,), (1,)), ((), ())), preferred_elem...]
  transfers between devices with their start and end apart: 3 -> 4, of which waited for: 3 -> 4; matrix products, arithmetic and copies ran while one was open for 2% -> 2% of each run, Pallas kernels for 0% -> 0%
where the time goes in v1:
time: 177 us
  blocking collectives  118 us (67%)
  matrix products  27.5 us (16%)
  other arithmetic  10.2 us (6%)
  waiting for transfers between devices  9.33 us (5%)
  starting transfers between devices  6.16 us (3%)
  local copies, waits for them, and re-layouts  4.74 us (3%)
    all_to_all x2, blocking collectives, gather_chips(): out = lax.all_to_all(copies, CHIPS, 0, 0)  80.5 us
    all_to_all x1, blocking collectives, per_device(): lax.all_to_all(part.reshape(chips, total_rows // chips, half), CHIPS, 0, 0)  37.5 us
    dot_general x1, matrix products, per_device(): lax.dot_general(err, dec_weight, (((1,), (1,)), ((), ())), preferred_elem...  7.37 us
    dot_general x1, matrix products, per_device(): lax.dot_general(inputs, pre_grad, contract_rows, preferred_element_type=j...  7.16 us
    dot_general x1, matrix products, per_device(): lax.dot_general(activations, err, contract_rows, preferred_element_type=j...  6.53 us
    select_n x1, other arithmetic, per_device(): jnp.where(core == 0, jnp.concatenate([e_own, e_oth], 1), jnp.concatenate(...  4.96 us
    ppermute x1, waiting for transfers between devices, per_device(): x_oth = lax.ppermute(x_own, 'c', SWAP)  4.16 us
    ppermute x1, waiting for transfers between devices, per_device(): part_got = lax.ppermute(part_oth.astype(jnp.bfloat16), 'c', SWAP)  4.16 us
  transfers between devices with their start and end apart: 4, of which 4 were waited for; matrix products, arithmetic and copies ran while one was open for 2% of the time, Pallas kernels for 0%

profile of v1, /device:TPU:1, one launch (start us, length us, event | category | flops | bytes accessed | tf_op | source)
XLA Modules:
  0.0 176.7 jit_solution(15790394303514706301)
XLA Ops:
  0.6 0.0 copy-start.5
  0.6 0.8 constant_dynamic-slice_fusion.1
  1.4 1.5 collective-permute-start
  2.9 0.0 copy-start.2
  2.9 0.8 collective-permute-done
  3.8 0.2 broadcast_in_dim.16
  4.0 43.5 %all_to_all.15 = bf16[64,8,2304]{2,1,0:T(8,128)(2,1)S(1)} all-to-all(bf16[64,8,2304]{2,1,0:T(8,128)(2,1)S(1)} %broadcast_in_dim.16), channel_id=1, replica_groups=mesh['z'=4,'xh'=2,'xl'=2,'y'=4,'c'=2] {'z','xh','xl','y'}, dimensions={0} | all-to-all | bytes 4718592 | tf_op jit(solution)/shard_map/all_to_all | solution.py:15
  47.5 0.0 copy-start
  47.5 0.0 slice-start.2
  47.5 0.0 slice-start.3
  47.5 1.6 collective-permute-start.1
  49.1 4.2 %collective-permute-done.1 = bf16[512,2304]{1,0:T(8,128)(2,1)S(1)} collective-permute-done((bf16[512,2304]{1,0:T(8,128)(2,1)S(1)}, bf16[512,2304]{1,0:T(8,128)(2,1)S(1)}, u32[]{:S(2)}, u32[]{:S(2)}) %collective-permute-start.1) | collective-permute-done | bytes 2359328 | tf_op jit(solution)/shard_map/ppermute | solution.py:37
  53.3 0.0 copy-done.5
  53.3 0.0 copy-done.2
  53.3 0.0 copy-start.3
  53.3 3.7 %convert_reduce_fusion.2 = (f32[512]{0:T(512)S(1)}, bf16[512,512]{1,0:T(8,128)(2,1)S(1)}, f32[512,512]{1,0:T(8,128)}) fusion(f32[512]{0:T(512)S(1)} %copy-done.5, bf16[4608,512]{1,0:T(8,128)(2,1)S(1)} %copy-done.2, bf16[512,2304]{1,0:T(8,128)(2,1)S(1)} %collective-permute-done.1, bf16[512,2304]{1,0:T(8,128)(2,1)S(1)} %bitcast.19, pred[]{:T(512)S(6)} %eq.2), kind=kOutput, calls=%fused_computation.20 | convolution fusion | flops 2438462976 | bytes 11014145 | tf_op jit(solution)/shard_map/dot_general | solution.py:39
  56.9 0.0 copy-done
  56.9 0.0 copy-done.3
  56.9 0.0 slice-done.2
  57.0 0.0 slice-done.3
  57.0 1.4 convolution_convert_fusion.1
  58.4 0.5 collective-permute-start.2
  58.9 4.2 %collective-permute-done.2 = bf16[512,2304]{1,0:T(8,128)(2,1)S(1)} collective-permute-done((bf16[512,2304]{1,0:T(8,128)(2,1)S(1)}, bf16[512,2304]{1,0:T(8,128)(2,1)S(1)}, u32[]{:S(2)}, u32[]{:S(2)}) %collective-permute-start.2) | collective-permute-done | bytes 2359328 | tf_op jit(solution)/shard_map/ppermute | solution.py:43
  63.0 1.4 fusion.4
  64.4 37.5 %all_to_all.16 = bf16[64,8,2304]{2,1,0:T(8,128)(2,1)S(1)} all-to-all(bf16[64,8,2304]{2,1,0:T(8,128)(2,1)S(1)} %fusion.4), channel_id=1, replica_groups=mesh['z'=4,'xh'=2,'xl'=2,'y'=4,'c'=2] {'z','xh','xl','y'}, dimensions={0} | all-to-all | bytes 4718592 | tf_op jit(solution)/shard_map/all_to_all | solution.py:46
  101.9 0.4 convert_reduce_fusion
  102.3 0.2 broadcast_in_dim.32
  102.4 37.0 %all_to_all.17 = bf16[64,8,2304]{2,1,0:T(8,128)(2,1)S(1)} all-to-all(bf16[64,8,2304]{2,1,0:T(8,128)(2,1)S(1)} %broadcast_in_dim.32), channel_id=1, replica_groups=mesh['z'=4,'xh'=2,'xl'=2,'y'=4,'c'=2] {'z','xh','xl','y'}, dimensions={0} | all-to-all | bytes 4718592 | tf_op jit(solution)/shard_map/all_to_all | solution.py:15
  139.4 2.6 %collective-permute-start.3 = (bf16[512,2304]{1,0:T(8,128)(2,1)S(1)}, bf16[512,2304]{1,0:T(8,128)(2,1)}, u32[]{:S(2)}, u32[]{:S(2)}) collective-permute-start(bf16[512,2304]{1,0:T(8,128)(2,1)S(1)} %bitcast.12), channel_id=1, source_target_pairs={{0,1},{1,0},{2,3},{3,2},{4,5},{5,4},{6,7},{7,6},{8,9},{9,8},{10,11... | collective-permute-start | bytes 7077896 | tf_op jit(solution)/shard_map/ppermute | solution.py:50
  142.0 0.8 compare_and_fusion
  142.8 3.3 %fusion = f32[512]{0:T(512)S(1)} fusion(bf16[512,4608]{1,0:T(8,128)(2,1)} %param.9), kind=kLoop, calls=%fused_computation.3 | loop fusion | flops 7077376 | bytes 4720640 | tf_op jit(solution)/shard_map/reduce_sum | solution.py:54
  146.2 0.2 collective-permute-done.3
  146.3 5.0 %maximum_select_fusion.1 = bf16[512,4608]{1,0:T(8,128)(2,1)} fusion(bf16[512,2304]{1,0:T(8,128)(2,1)} %collective-permute-done.3, bf16[512,2304]{1,0:T(8,128)(2,1)S(1)} %bitcast.13, pred[]{:T(512)S(6)} %eq.2), kind=kLoop, calls=%fused_computation.9 | loop fusion | flops 21233664 | bytes 9437185 | tf_op jit(solution)/shard_map/jit(_where)/select_n | solution.py:51
  151.3 0.0 slice-start
  151.3 3.6 %gather_fusion = bf16[4,4608]{1,0:T(4,128)(2,1)S(1)} fusion(bf16[512,4608]{1,0:T(8,128)(2,1)} %maximum_select_fusion.1, s32[1024]{0:T(1024)S(1)} %pad_clamp_fusion), kind=kCustom, calls=%fused_computation | custom fusion | bytes 73744 | tf_op jit(solution)/shard_map/jit(_take)/gather | solution.py:66
  154.9 0.7 convert_multiply_fusion.2
  155.6 0.0 slice-start.1
  155.6 7.4 %convert_reduce_fusion.1 = (f32[512]{0:T(512)}, bf16[512,512]{1,0:T(8,128)(2,1)S(1)}) fusion(f32[512]{0:T(512)S(1)} %get-tuple-element.11, bf16[512,4608]{1,0:T(8,128)(2,1)} %maximum_select_fusion.1, bf16[512,4608]{1,0:T(8,128)(2,1)} %param.9, f32[512,512]{1,0:T(8,128)} %get-tuple-element.12), kind=kOutput, calls=%fused_computation.19 | convolution fusion | flops 2417491456 | bytes 11014144 | tf_op jit(solution)/shard_map/dot_general | solution.py:58
  163.0 0.0 slice-done
  163.0 0.0 slice-done.1
  163.0 0.0 copy-start.1
  163.0 0.0 copy-start.4
  163.0 6.5 %fusion.3 = bf16[512,4608]{1,0:T(8,128)(2,1)} fusion(bf16[512,4608]{1,0:T(8,128)(2,1)} %param.9, bf16[512,512]{1,0:T(8,128)(2,1)S(1)} %get-tuple-element.5, bf16[512,4608]{1,0:T(8,128)(2,1)S(1)} %bitcast.15, f32[512]{0:T(512)S(1)} %get-tuple-element.10, f32[512]{0:T(512)S(1)} %broadcast_multiply_fusion), kind=kOutput, calls=%fused_computation.6 | convolution fusion | flops 2427715584 | bytes 14684160 | tf_op jit(solution)/shard_map/dot_general | solution.py:56
  169.6 0.0 copy-done.1
  169.6 0.0 copy-done.4
  169.6 7.2 %convolution_convert_fusion = bf16[4608,512]{1,0:T(8,128)(2,1)} fusion(bf16[512,512]{1,0:T(8,128)(2,1)S(1)} %get-tuple-element.14, bf16[512,2304]{1,0:T(8,128)(2,1)S(1)} %copy-done.4, bf16[512,2304]{1,0:T(8,128)(2,1)S(1)} %bitcast.20, pred[]{:T(512)S(6)} %eq.2), kind=kOutput, calls=%fused_computation.7 | convolution fusion | flops 2439512064 | bytes 9961473 | tf_op jit(solution)/shard_map/dot_general | solution.py:61
  (7 shorter events, 0.1 us)
Async XLA Ops:
  0.6 52.6 %copy-start.5 = (f32[512]{0:T(512)S(1)}, f32[512]{0:T(512)}, u32[]{:S(2)}) copy-start(f32[512]{0:T(512)} %param.8) | copy-start | bytes 6148
  1.4 2.3 %collective-permute-start = (bf16[4,2304]{1,0:T(4,128)(2,1)S(1)}, bf16[4,2304]{1,0:T(4,128)(2,1)S(1)}, u32[]{:S(2)}, u32[]{:S(2)}) collective-permute-start(bf16[4,2304]{1,0:T(4,128)(2,1)S(1)} %get-tuple-element.9), channel_id=1, source_target_pairs={{0,1},{1,0},{2,3},{3,2},{4,5},{5,4},{6,7},{7,6},{8,9},{9,8},{10,11... | collective-permute-start | bytes 55304 | tf_op jit(solution)/shard_map/ppermute | solution.py:33
  2.9 50.3 %copy-start.2 = (bf16[4608,512]{1,0:T(8,128)(2,1)S(1)}, bf16[4608,512]{1,0:T(8,128)(2,1)}, u32[]{:S(2)}) copy-start(bf16[4608,512]{1,0:T(8,128)(2,1)} %param.7) | copy-start | bytes 14155780
  47.5 9.4 %copy-start = (bf16[64,8,2304]{2,1,0:T(8,128)(2,1)}, bf16[64,8,2304]{2,1,0:T(8,128)(2,1)S(1)}, u32[]{:S(2)}) copy-start(bf16[64,8,2304]{2,1,0:T(8,128)(2,1)S(1)} %all_to_all.15) | copy-start | bytes 7077892
  47.5 9.4 %slice-start.2 = ((s8[4718592]{0:T(1024)(128)(4,1)}), s8[4194304]{0:T(1024)(128)(4,1)S(1)}, s32[]{:S(2)}) async-start(s8[4718592]{0:T(1024)(128)(4,1)} %bitcast.16), calls=%async_computation.5 | async-start | bytes 8388608
  47.5 9.4 %slice-start.3 = ((s8[4718592]{0:T(1024)(128)(4,1)}), s8[524288]{0:T(1024)(128)(4,1)S(1)}, s32[]{:S(2)}) async-start(s8[4718592]{0:T(1024)(128)(4,1)} %bitcast.16), calls=%async_computation.6 | async-start | bytes 1048576
  47.5 5.7 %collective-permute-start.1 = (bf16[512,2304]{1,0:T(8,128)(2,1)S(1)}, bf16[512,2304]{1,0:T(8,128)(2,1)S(1)}, u32[]{:S(2)}, u32[]{:S(2)}) collective-permute-start(bf16[512,2304]{1,0:T(8,128)(2,1)S(1)} %bitcast.18), channel_id=1, source_target_pairs={{0,1},{1,0},{2,3},{3,2},{4,5},{5,4},{6,7},{7,6},{8,9},{9,8},{10,11... | collective-permute-start | bytes 7077896 | tf_op jit(solution)/shard_map/ppermute | solution.py:37
  53.3 3.7 %copy-start.3 = (bf16[512,2304]{1,0:T(8,128)(2,1)}, bf16[512,2304]{1,0:T(8,128)(2,1)S(1)}, u32[]{:S(2)}) copy-start(bf16[512,2304]{1,0:T(8,128)(2,1)S(1)} %collective-permute-done.1) | copy-start | bytes 7077892
  58.4 4.6 %collective-permute-start.2 = (bf16[512,2304]{1,0:T(8,128)(2,1)S(1)}, bf16[512,2304]{1,0:T(8,128)(2,1)S(1)}, u32[]{:S(2)}, u32[]{:S(2)}) collective-permute-start(bf16[512,2304]{1,0:T(8,128)(2,1)S(1)} %convolution_convert_fusion.1), channel_id=1, source_target_pairs={{0,1},{1,0},{2,3},{3,2},{4,5},{5,4},{6,7},{7,6},{8,9},{9,8},{10,11... | collective-permute-start | bytes 7077896 | tf_op jit(solution)/shard_map/ppermute | solution.py:43
  139.4 6.9 %collective-permute-start.3 = (bf16[512,2304]{1,0:T(8,128)(2,1)S(1)}, bf16[512,2304]{1,0:T(8,128)(2,1)}, u32[]{:S(2)}, u32[]{:S(2)}) collective-permute-start(bf16[512,2304]{1,0:T(8,128)(2,1)S(1)} %bitcast.12), channel_id=1, source_target_pairs={{0,1},{1,0},{2,3},{3,2},{4,5},{5,4},{6,7},{7,6},{8,9},{9,8},{10,11... | collective-permute-start | bytes 7077896 | tf_op jit(solution)/shard_map/ppermute | solution.py:50
  151.3 11.7 %slice-start = ((s8[4718592]{0:T(1024)(128)(4,1)}), s8[524288]{0:T(1024)(128)(4,1)S(1)}, s32[]{:S(2)}) async-start(s8[4718592]{0:T(1024)(128)(4,1)} %bitcast.14), calls=%async_computation.3 | async-start | bytes 1048576
  155.6 7.4 %slice-start.1 = ((s8[4718592]{0:T(1024)(128)(4,1)}), s8[4194304]{0:T(1024)(128)(4,1)S(1)}, s32[]{:S(2)}) async-start(s8[4718592]{0:T(1024)(128)(4,1)} %bitcast.14), calls=%async_computation.4 | async-start | bytes 8388608
  163.0 6.5 %copy-start.1 = (bf16[64,8,2304]{2,1,0:T(8,128)(2,1)S(1)}, bf16[64,8,2304]{2,1,0:T(8,128)(2,1)}, u32[]{:S(2)}) copy-start(bf16[64,8,2304]{2,1,0:T(8,128)(2,1)} %copy-done) | copy-start | bytes 7077892
  163.0 6.5 %copy-start.4 = (bf16[512,2304]{1,0:T(8,128)(2,1)S(1)}, bf16[512,2304]{1,0:T(8,128)(2,1)}, u32[]{:S(2)}) copy-start(bf16[512,2304]{1,0:T(8,128)(2,1)} %copy-done.3) | copy-start | bytes 7077892

commit v2 on v1

v2 whole, which is shorter than its diff:
```python
import functools
import itertools
import math

import jax
import jax.numpy as jnp
from jax import lax
from jax.experimental import pallas as pl
from jax.experimental.pallas import tpu as pltpu
from jax.sharding import Mesh, PartitionSpec as P

CHIPS = ("z", "xh", "xl", "y")
NAMES = CHIPS + ("c",)
SWAP = [(0, 1), (1, 0)]


def chip_index(z, x, y):
    return ((z % 4) * 4 + x % 4) * 4 + y % 4


def chip_classes():
    groups = []
    for b, a in itertools.product(range(2), range(2)):
        group = []
        for z, x, y in itertools.product(range(4), range(2), range(2)):
            group.append(chip_index(z, 2 * x + (a + z) % 2, 2 * y + (b + z) % 2))
        groups.append(group)
    return groups


def neighbour_shifts():
    shifts = []
    for step in ((0, 1, 0), (0, 0, 1), (1, 0, 0)):
        pairs = []
        for z, x, y in itertools.product(range(4), repeat=3):
            for c in range(2):
                s = 1 - 2 * c
                to = chip_index(z + s * step[0], x + s * step[1], y + s * step[2])
                pairs.append((chip_index(z, x, y) * 2 + c, to * 2 + c))
        shifts.append(pairs)
    return shifts


CLASSES = chip_classes()
SHIFTS = neighbour_shifts()


def gather_chips(block):
    copies = jnp.broadcast_to(block[None], (16,) + block.shape)
    near = lax.all_to_all(copies, CHIPS, 0, 0, axis_index_groups=CLASSES)
    near = near.reshape(16 * block.shape[0], block.shape[1])
    return [near] + [lax.ppermute(near, NAMES, pairs) for pairs in SHIFTS]


def reduce_chips(parts):
    got = [lax.ppermute(part, NAMES, pairs) for part, pairs in zip(parts[1:], SHIFTS)]
    total = parts[0].astype(jnp.float32)
    for part in got:
        total = total + part.astype(jnp.float32)
    total = total.astype(jnp.bfloat16)
    pieces = total.reshape(16, total.shape[0] // 16, total.shape[1])
    pieces = lax.all_to_all(pieces, CHIPS, 0, 0, axis_index_groups=CLASSES)
    return jnp.sum(pieces.astype(jnp.float32), axis=0)


def swap_cores(a):
    return lax.ppermute(a, "c", SWAP)


def column_block(n, step, core):
    return jnp.where(step < n, core * n + step, (1 - core) * n + step - n)


def front_kernel(n, core, bias_ref, enc_ref, *refs):
    x_own, x_oth = refs[:4], refs[4:8]
    preact_ref, act_ref, total = refs[8:]
    step = pl.program_id(0)

    def add(blocks):
        rows = jnp.concatenate([r[...] for r in blocks], axis=0)
        return jnp.dot(rows, enc_ref[...], preferred_element_type=jnp.float32)

    @pl.when(step == 0)
    def _():
        total[...] = add(x_own)

    @pl.when((step > 0) & (step < n))
    def _():
        total[...] += add(x_own)

    @pl.when((step >= n) & (step < 2 * n - 1))
    def _():
        total[...] += add(x_oth)

    @pl.when(step == 2 * n - 1)
    def _():
        preact = total[...] + add(x_oth) + bias_ref[...]
        preact_ref[...] = preact
        act_ref[...] = jnp.maximum(preact, 0.0).astype(jnp.bfloat16)


def front(core, x_own, x_oth, enc_weight, enc_bias, n):
    rows, half = x_own[0].shape
    latents = enc_weight.shape[1]
    total_rows = 4 * rows
    wide = half // n

    def whole(shape):
        return pl.BlockSpec(shape, lambda i, c: (0, 0))

    own = pl.BlockSpec((rows, wide), lambda i, c: (0, jnp.minimum(i, n - 1)))
    oth = pl.BlockSpec((rows, wide), lambda i, c: (0, jnp.maximum(i - n, 0)))
    return pl.pallas_call(
        functools.partial(front_kernel, n),
        out_shape=(
            jax.ShapeDtypeStruct((total_rows, latents), jnp.float32),
            jax.ShapeDtypeStruct((total_rows, latents), jnp.bfloat16),
        ),
        grid_spec=pltpu.PrefetchScalarGridSpec(
            num_scalar_prefetch=1,
            grid=(2 * n,),
            in_specs=[whole((1, latents)), pl.BlockSpec((wide, latents), lambda i, c: (column_block(n, i, c[0]), 0))]
            + [own] * 4
            + [oth] * 4,
            out_specs=(whole((total_rows, latents)), whole((total_rows, latents))),
            scratch_shapes=[pltpu.VMEM((total_rows, latents), jnp.float32)],
        ),
        compiler_params=pltpu.CompilerParams(vmem_limit_bytes=40 * 2**20),
        name="front",
    )(core, enc_bias[None], enc_weight, *x_own, *x_oth)


def tail_kernel(n, row_scale, core, left_ref, preact_ref, scale_ref, norm_ref, dec_ref, *refs):
    e_own, e_oth, x_own, x_oth = refs[:4], refs[4:8], refs[8:12], refs[12:16]
    dec_grad_ref, enc_grad_ref, bias_ref, recon_ref, total, pre = refs[16:]
    step = pl.program_id(0)
    latents = dec_ref.shape[0]
    out_rows = recon_ref.shape[0]

    @pl.when(step == 0)
    def _():
        total[...] = jnp.zeros_like(total)

    def stack(blocks):
        return jnp.concatenate([r[...] for r in blocks], axis=0)

    def first(blocks):
        err = stack(blocks)
        dec = dec_ref[...]
        both = jnp.dot(left_ref[...], err, preferred_element_type=jnp.float32)
        dec_grad_ref[...] = (both[:latents] + scale_ref[...] * dec.astype(jnp.float32)).astype(jnp.bfloat16)
        recon_ref[...] = both[latents : latents + out_rows] * row_scale
        total[...] += lax.dot_general(err, dec, (((1,), (1,)), ((), ())), preferred_element_type=jnp.float32)

    def second(blocks):
        enc_grad_ref[...] = lax.dot_general(
            stack(blocks), pre[...], (((0,), (0,)), ((), ())), preferred_element_type=jnp.float32
        ).astype(jnp.bfloat16)

    @pl.when(step < n)
    def _():
        first(e_own)

    @pl.when((step >= n) & (step < 2 * n))
    def _():
        first(e_oth)

    @pl.when(step == 2 * n)
    def _():
        rounded = jnp.where(preact_ref[...] > 0.0, total[...] + norm_ref[...], 0.0).astype(jnp.bfloat16)
        pre[...] = rounded
        bias_ref[...] = jnp.sum(rounded.astype(jnp.float32), axis=0, keepdims=True)

    @pl.when((step >= 2 * n) & (step < 3 * n))
    def _():
        second(x_own)

    @pl.when(step >= 3 * n)
    def _():
        second(x_oth)


def tail(core, left, preact, scale, norm, dec_weight, e_own, e_oth, x_own, x_oth, row_scale, out_rows, n):
    rows, half = x_own[0].shape
    latents, width = dec_weight.shape
    wide = half // n
    total_rows = 4 * rows

    def whole(shape):
        return pl.BlockSpec(shape, lambda i, c: (0, 0))

    def part(k):
        return pl.BlockSpec((rows, wide), lambda i, c: (0, jnp.clip(i - k * n, 0, n - 1)))

    def columns(height):
        return pl.BlockSpec((height, wide), lambda i, c: (0, column_block(n, jnp.minimum(i, 2 * n - 1), c[0])))

    return pl.pallas_call(
        functools.partial(tail_kernel, n, row_scale),
        out_shape=(
            jax.ShapeDtypeStruct((latents, width), jnp.bfloat16),
            jax.ShapeDtypeStruct((width, latents), jnp.bfloat16),
            jax.ShapeDtypeStruct((1, latents), jnp.float32),
            jax.ShapeDtypeStruct((out_rows, width), jnp.float32),
        ),
        grid_spec=pltpu.PrefetchScalarGridSpec(
            num_scalar_prefetch=1,
            grid=(4 * n,),
            in_specs=[
                whole(left.shape),
                whole(preact.shape),
                whole(scale.shape),
                whole(norm.shape),
                columns(latents),
            ]
            + [part(k) for k in range(4) for _ in range(4)],
            out_specs=(
                columns(latents),
                pl.BlockSpec((wide, latents), lambda i, c: (column_block(n, jnp.maximum(i - 2 * n, 0), c[0]), 0)),
                whole((1, latents)),
                columns(out_rows),
            ),
            scratch_shapes=[
                pltpu.VMEM((total_rows, latents), jnp.float32),
                pltpu.VMEM((total_rows, latents), jnp.bfloat16),
            ],
        ),
        compiler_params=pltpu.CompilerParams(vmem_limit_bytes=48 * 2**20),
        name="tail",
    )(core, left, preact, scale, norm, dec_weight, *e_own, *e_oth, *x_own, *x_oth)


def per_device(tokens, batch_order, enc_weight, enc_bias, dec_weight):
    rows_dev, width = tokens.shape
    total_rows = batch_order.shape[0]
    row_scale = math.sqrt(total_rows)
    half = width // 2
    block_rows = total_rows // 4
    core = lax.axis_index("c")
    core_arg = core[None].astype(jnp.int32)
    own = core * half
    oth = (1 - core) * half

    def pick(a, start):
        return lax.dynamic_slice_in_dim(a, start, half, 1)

    got = swap_cores(pick(tokens, oth))
    mine = pick(tokens, own)
    block = jnp.where(core == 0, jnp.concatenate([mine, got]), jnp.concatenate([got, mine]))
    x_own = gather_chips(block)
    x_oth = [swap_cores(a) for a in x_own]
    preact, activations = front(core_arg, x_own, x_oth, enc_weight, enc_bias, 3)

    part_oth = jnp.dot(activations, pick(dec_weight, oth), preferred_element_type=jnp.float32).astype(jnp.bfloat16)
    part_own = jnp.dot(activations, pick(dec_weight, own), preferred_element_type=jnp.float32)
    parts = []
    for k in range(4):
        rows = slice(k * block_rows, (k + 1) * block_rows)
        parts.append((part_own[rows] + swap_cores(part_oth[rows]).astype(jnp.float32)).astype(jnp.bfloat16))

    dec_wide = dec_weight.astype(jnp.float32)
    row_norms = jnp.sqrt(jnp.sum(dec_wide * dec_wide, axis=1) + 1e-06)
    act_total = jnp.sum(activations.astype(jnp.float32), axis=0) / row_scale
    z = lax.axis_index("z")
    x = lax.axis_index("xh") * 2 + lax.axis_index("xl")
    y = lax.axis_index("y")
    first = (chip_index(z, x, y) * 2 + core) * rows_dev
    wanted = lax.dynamic_slice_in_dim(batch_order, first, rows_dev)
    chip = wanted // (2 * rows_dev)
    tz, tx, ty = chip // 16, chip // 4 % 4, chip % 4
    a = (tx + tz + x + z) % 2
    b = (ty + tz + y + z) % 2
    place = (a + 2 * b) * block_rows + (tz * 4 + tx // 2 * 2 + ty // 2) * (2 * rows_dev) + wanted % (2 * rows_dev)
    place = jnp.concatenate([place, jnp.full((16 - rows_dev,), -1, place.dtype)])
    chosen = (place[:, None] == jnp.arange(total_rows, dtype=place.dtype)[None]).astype(jnp.bfloat16)
    left = jnp.concatenate([activations.T, chosen])
    scale = (act_total / row_norms)[:, None]
    norm = (row_norms / row_scale)[None]

    recon = reduce_chips(parts) - block.astype(jnp.float32)
    recon, left, scale, norm = lax.optimization_barrier((recon, left, scale, norm))
    err_block = (recon / row_scale).astype(jnp.bfloat16)
    e_own = gather_chips(err_block)
    e_oth = [swap_cores(a) for a in e_own]
    dec_grad, enc_grad, bias_grad, recon_error = tail(
        core_arg, left, preact, scale, norm, dec_weight, e_own, e_oth, x_own, x_oth, row_scale, rows_dev, 3
    )
    return (recon_error, enc_grad, dec_grad, bias_grad[0])


def solution(mesh):
    split = Mesh(mesh.devices.reshape(4, 2, 2, 4, 2), NAMES)
    return jax.shard_map(
        per_device,
        mesh=split,
        in_specs=(P(NAMES, None), P(), P(None, NAMES), P(NAMES), P(NAMES, None)),
        out_specs=(P(NAMES, None), P(None, NAMES), P(NAMES, None), P(NAMES)),
        check_vma=False,
    )
```

time: 177 us -> 144 us (0.81)
  blocking collectives: 118 us -> 40.3 us
  starting transfers between devices: 6.16 us -> 33.5 us
  matrix products: 27.5 us -> 2.79 us
  waiting for transfers between devices: 9.33 us -> 31.2 us
  Pallas kernels: 0 us -> 21.2 us
    all_to_all x3 -> x2, blocking collectives: 118 us -> 40.3 us  [gather_chips(): near = lax.all_to_all(copies, CHIPS, 0, 0, axis_index_groups=CLASSES)]
    dot_general x4 -> x0, matrix products: 24.7 us -> none  [the longest x1 7.37 us: per_device(): lax.dot_general(err, dec_weight, (((1,), (1,)), ((), ())), preferred_elem...]
    ppermute x4 -> x22, starting transfers between devices: 6.16 us -> 29.4 us  [the longest x13 19.1 us: swap_cores(): return lax.ppermute(a, 'c', SWAP)]
    pallas_call x0 -> x2, Pallas kernels: none -> 21.2 us  [the longest x1 17.1 us: tail(): pl.pallas_call(functools.partial(tail_kernel, n, row_scale), out_shape=(j...]
    all_to_all x0 -> x1, waiting for transfers between devices: none -> 11.1 us  [reduce_chips(): pieces = lax.all_to_all(pieces, CHIPS, 0, 0, axis_index_groups=CLASSES)]
    ppermute x4 -> x22, waiting for transfers between devices: 9.33 us -> 20 us  [the longest x13 8.55 us: swap_cores(): return lax.ppermute(a, 'c', SWAP)]
    select_n x1 -> x0, other arithmetic: 4.96 us -> none  [per_device(): jnp.where(core == 0, jnp.concatenate([e_own, e_oth], 1), jnp.concatenate(...]
    all_to_all x0 -> x1, starting transfers between devices: none -> 4.1 us  [reduce_chips(): pieces = lax.all_to_all(pieces, CHIPS, 0, 0, axis_index_groups=CLASSES)]
  transfers between devices with their start and end apart: 4 -> 23, of which waited for: 4 -> 15; matrix products, arithmetic and copies ran while one was open for 2% -> 5% of each run, Pallas kernels for 0% -> 0%
where the time goes in v2:
time: 144 us
  blocking collectives  40.3 us (28%)
  starting transfers between devices  33.5 us (23%)
  waiting for transfers between devices  31.2 us (22%)
  Pallas kernels  21.2 us (15%)
  other arithmetic  8.81 us (6%)
  local copies, waits for them, and re-layouts  4.69 us (3%)
  matrix products  2.79 us (2%)
    all_to_all x2, blocking collectives, gather_chips(): near = lax.all_to_all(copies, CHIPS, 0, 0, axis_index_groups=CLASSES)  40.3 us
    ppermute x13, starting transfers between devices, swap_cores(): return lax.ppermute(a, 'c', SWAP)  19.1 us
    pallas_call x1, Pallas kernels, tail(): pl.pallas_call(functools.partial(tail_kernel, n, row_scale), out_shape=(j...  17.1 us
    all_to_all x1, waiting for transfers between devices, reduce_chips(): pieces = lax.all_to_all(pieces, CHIPS, 0, 0, axis_index_groups=CLASSES)  11.1 us
    ppermute x13, waiting for transfers between devices, swap_cores(): return lax.ppermute(a, 'c', SWAP)  8.55 us
    ppermute x6, waiting for transfers between devices, gather_chips(): return [near] + [lax.ppermute(near, NAMES, pairs) for pairs in SHIFTS]  7.68 us
    ppermute x6, starting transfers between devices, gather_chips(): return [near] + [lax.ppermute(near, NAMES, pairs) for pairs in SHIFTS]  5.79 us
    ppermute x3, starting transfers between devices, reduce_chips(): lax.ppermute(part, NAMES, pairs)  4.52 us
  transfers between devices with their start and end apart: 23, of which 15 were waited for; matrix products, arithmetic and copies ran while one was open for 5% of the time, Pallas kernels for 0%

profile of v2, /device:TPU:1, one launch (start us, length us, event | category | flops | bytes accessed | tf_op | source)
XLA Modules:
  0.0 143.6 jit_solution(14650789439973150791)
XLA Ops:
  0.7 0.8 constant_dynamic-slice_fusion.1
  1.5 1.5 %collective-permute-start = (bf16[4,2304]{1,0:T(4,128)(2,1)S(1)}, bf16[4,2304]{1,0:T(4,128)(2,1)S(1)}, u32[]{:S(2)}, u32[]{:S(2)}) collective-permute-start(bf16[4,2304]{1,0:T(4,128)(2,1)S(1)} %get-tuple-element.32), channel_id=1, source_target_pairs={{0,1},{1,0},{2,3},{3,2},{4,5},{5,4},{6,7},{7,6},{8,9},{9,8},{10,11... | collective-permute-start | bytes 55304 | tf_op jit(solution)/shard_map/ppermute | solution.py:67
  3.0 0.8 collective-permute-done
  3.9 24.1 %all_to_all.15 = bf16[16,8,2304]{2,1,0:T(8,128)(2,1)S(1)} all-to-all(bf16[16,8,2304]{2,1,0:T(8,128)(2,1)S(1)} %broadcast_in_dim.10), channel_id=1, replica_groups={{0,4,16,20,42,46,58,62,64,68,80,84,106,110,122,126},{8,12,24,28,34,38,5..., dimensions={0} | all-to-all | bytes 1179648 | tf_op jit(solution)/shard_map/all_to_all | solution.py:50
  28.0 0.9 collective-permute-start.2
  29.0 2.3 %collective-permute-start.1 = (bf16[128,2304]{1,0:T(8,128)(2,1)S(1)}, bf16[128,2304]{1,0:T(8,128)(2,1)S(1)}, u32[]{:S(2)}, u32[]{:S(2)}) collective-permute-start(bf16[128,2304]{1,0:T(8,128)(2,1)S(1)} %bitcast.14), channel_id=1, source_target_pairs={{0,8},{1,25},{2,10},{3,27},{4,12},{5,29},{6,14},{7,31},{8,16},{9,1... | collective-permute-start | bytes 1769480 | tf_op jit(solution)/shard_map/ppermute | solution.py:52
  31.3 5.8 %collective-permute-done.3.refs_3_.refs_11_ = bf16[128,2304]{1,0:T(8,128)(2,1)S(1)} collective-permute-done((bf16[128,2304]{1,0:T(8,128)(2,1)S(1)}, bf16[128,2304]{1,0:T(8,128)(2,1)S(1)}, u32[]{:S(2)}, u32[]{:S(2)}) %collective-permute-start.3) | collective-permute-done | bytes 589856 | tf_op jit(solution)/shard_map/ppermute | solution.py:52
  37.1 3.6 %collective-permute-start.7 = (bf16[128,2304]{1,0:T(8,128)(2,1)S(1)}, bf16[128,2304]{1,0:T(8,128)(2,1)S(1)}, u32[]{:S(2)}, u32[]{:S(2)}) collective-permute-start(bf16[128,2304]{1,0:T(8,128)(2,1)S(1)} %collective-permute-done.3.refs_3_.refs_11_), channel_id=1, source_target_pairs={{0,1},{1,0},{2,3},{3,2},{4,5},{5,4},{6,7},{7,6},{8,9},{9,8},{10,11... | collective-permute-start | bytes 1769480 | tf_op jit(solution)/shard_map/ppermute | solution.py:67
  40.8 0.6 collective-permute-start.5
  41.4 0.9 collective-permute-done.7.refs_7_.refs_15_
  42.3 0.8 collective-permute-done.6.refs_6_.refs_14_
  43.2 0.8 collective-permute-done.5.refs_5_.refs_13_
  44.0 2.5 %copy-done = bf16[4608,512]{1,0:T(8,128)(2,1)S(1)} copy-done((bf16[4608,512]{1,0:T(8,128)(2,1)S(1)}, bf16[4608,512]{1,0:T(8,128)(2,1)}, u32[]{:S(2)}) %copy-start) | copy-done | bytes 4718616
  46.6 0.7 copy-done.9
  47.3 4.2 %front.1 = (f32[512,512]{1,0:T(8,128)S(1)}, bf16[512,512]{1,0:T(8,128)(2,1)S(1)}) custom-call(s32[1]{0:T(128)} %bitcast.core, f32[1,512]{1,0:T(1,128)S(1)} %bitcast.24, bf16[4608,512]{1,0:T(8,128)(2,1)S(1)} %copy-done, bf16[128,2304]{1,0:T(8,128)(2,1)S(1)} %bitcast.16, bf16[128,2304]{1,0:T(8,128)(2,1)S(1)} %collective-permute-done.1.refs_1_.refs_9_, ...), custom_call_target="tpu_custom_call" | custom-call | tf_op jit(solution)/shard_map/front/pallas_call | solution.py:113
  51.5 1.4 convolution_convert_fusion
  52.9 0.2 fusion.17
  53.1 0.5 collective-permute-start.13
  53.7 0.4 collective-permute-start.9
  54.1 0.1 collective-permute-start.8
  54.2 1.4 fusion.1
  55.6 1.3 collective-permute-done.11
  56.9 0.8 collective-permute-done.9
  57.7 1.2 fusion.5
  58.9 1.5 %collective-permute-start.10 = (bf16[128,2304]{1,0:T(8,128)(2,1)}, bf16[128,2304]{1,0:T(8,128)(2,1)}, u32[]{:S(2)}, u32[]{:S(2)}) collective-permute-start(bf16[128,2304]{1,0:T(8,128)(2,1)} %get-tuple-element.24), channel_id=1, source_target_pairs={{0,8},{1,25},{2,10},{3,27},{4,12},{5,29},{6,14},{7,31},{8,16},{9,1... | collective-permute-start | bytes 1769480 | tf_op jit(solution)/shard_map/ppermute | solution.py:56
  60.4 2.1 %collective-permute-start.14 = (bf16[128,2304]{1,0:T(8,128)(2,1)S(1)}, bf16[128,2304]{1,0:T(8,128)(2,1)}, u32[]{:S(2)}, u32[]{:S(2)}) collective-permute-start(bf16[128,2304]{1,0:T(8,128)(2,1)S(1)} %get-tuple-element.25), channel_id=1, source_target_pairs={{0,32},{1,97},{2,34},{3,99},{4,36},{5,101},{6,38},{7,103},{8,40},{... | collective-permute-start | bytes 1769480 | tf_op jit(solution)/shard_map/ppermute | solution.py:56
  62.5 0.9 collective-permute-start.12
  63.4 0.8 fusion.12
  64.2 3.3 %multiply_reduce_fusion = f32[512]{0:T(512)S(1)} fusion(bf16[512,4608]{1,0:T(8,128)(2,1)} %dec_ref.1), kind=kLoop, calls=%fused_computation | loop fusion | flops 7077376 | bytes 4720640 | tf_op jit(solution)/shard_map/reduce_sum | solution.py:262
  67.6 0.7 collective-permute-done.10
  68.3 1.3 collective-permute-done.14
  69.6 1.8 %collective-permute-done.12 = bf16[128,2304]{1,0:T(8,128)(2,1)} collective-permute-done((bf16[128,2304]{1,0:T(8,128)(2,1)S(1)}, bf16[128,2304]{1,0:T(8,128)(2,1)}, u32[]{:S(2)}, u32[]{:S(2)}) %collective-permute-start.12) | collective-permute-done | bytes 589856 | tf_op jit(solution)/shard_map/ppermute | solution.py:56
  71.4 3.1 %fusion.7 = bf16[16,8,2304]{2,1,0:T(8,128)(2,1)} fusion(bf16[128,2304]{1,0:T(8,128)(2,1)} %collective-permute-done.14, bf16[128,2304]{1,0:T(8,128)(2,1)} %collective-permute-done.12, bf16[128,2304]{1,0:T(8,128)(2,1)} %collective-permute-done.10, bf16[128,2304]{1,0:T(8,128)(2,1)} %collective-permute-done.8, f32[512,2304]{1,0:T(8,128)} %copy-done.10), kind=kLoop, calls=%fused_computation.16 | loop fusion | flops 3244032 | bytes 4128768 | tf_op jit(solution)/shard_map/reshape | solution.py:61
  74.5 4.1 %all-to-all-start.1 = ((bf16[16,8,2304]{2,1,0:T(8,128)(2,1)}), bf16[16,8,2304]{2,1,0:T(8,128)(2,1)S(1)}, u32[]{:S(2)}, u32[]{:S(2)}) async-start(bf16[16,8,2304]{2,1,0:T(8,128)(2,1)} %fusion.7), calls=%async_computation.1 | async-start | bytes 1179648 | tf_op jit(solution)/shard_map/all_to_all | solution.py:62
  78.7 0.2 copy.10
  79.1 11.1 %all-to-all-done.1 = bf16[16,8,2304]{2,1,0:T(8,128)(2,1)S(1)} async-done(((bf16[16,8,2304]{2,1,0:T(8,128)(2,1)}), bf16[16,8,2304]{2,1,0:T(8,128)(2,1)S(1)}, u32[]{:S(2)}, u32[]{:S(2)}) %all-to-all-start.1) | async-done | bytes 589856 | tf_op jit(solution)/shard_map/all_to_all | solution.py:62
  90.4 16.2 %all_to_all.16 = bf16[16,8,2304]{2,1,0:T(8,128)(2,1)S(1)} all-to-all(bf16[16,8,2304]{2,1,0:T(8,128)(2,1)S(1)} %broadcast_in_dim.11), channel_id=1, replica_groups={{0,4,16,20,42,46,58,62,64,68,80,84,106,110,122,126},{8,12,24,28,34,38,5..., dimensions={0} | all-to-all | bytes 1179648 | tf_op jit(solution)/shard_map/all_to_all | solution.py:50
  106.6 2.1 %collective-permute-start.16 = (bf16[128,2304]{1,0:T(8,128)(2,1)S(1)}, bf16[128,2304]{1,0:T(8,128)(2,1)S(1)}, u32[]{:S(2)}, u32[]{:S(2)}) collective-permute-start(bf16[128,2304]{1,0:T(8,128)(2,1)S(1)} %bitcast.19), channel_id=1, source_target_pairs={{0,2},{1,7},{2,4},{3,1},{4,6},{5,3},{6,0},{7,5},{8,10},{9,15},{10,... | collective-permute-start | bytes 1769480 | tf_op jit(solution)/shard_map/ppermute | solution.py:52
  108.7 0.5 collective-permute-start.15
  109.1 4.3 %collective-permute-start.18 = (bf16[128,2304]{1,0:T(8,128)(2,1)S(1)}, bf16[128,2304]{1,0:T(8,128)(2,1)}, u32[]{:S(2)}, u32[]{:S(2)}) collective-permute-start(bf16[128,2304]{1,0:T(8,128)(2,1)S(1)} %bitcast.21), channel_id=1, source_target_pairs={{0,1},{1,0},{2,3},{3,2},{4,5},{5,4},{6,7},{7,6},{8,9},{9,8},{10,11... | collective-permute-start | bytes 1769480 | tf_op jit(solution)/shard_map/ppermute | solution.py:67
  113.4 1.9 %collective-permute-done.17.refs_3_ = bf16[128,2304]{1,0:T(8,128)(2,1)S(1)} collective-permute-done((bf16[128,2304]{1,0:T(8,128)(2,1)S(1)}, bf16[128,2304]{1,0:T(8,128)(2,1)S(1)}, u32[]{:S(2)}, u32[]{:S(2)}) %collective-permute-start.17) | collective-permute-done | bytes 589856 | tf_op jit(solution)/shard_map/ppermute | solution.py:52
  115.3 7.4 %collective-permute-start.21 = (bf16[128,2304]{1,0:T(8,128)(2,1)S(1)}, bf16[128,2304]{1,0:T(8,128)(2,1)}, u32[]{:S(2)}, u32[]{:S(2)}) collective-permute-start(bf16[128,2304]{1,0:T(8,128)(2,1)S(1)} %collective-permute-done.17.refs_3_), channel_id=1, source_target_pairs={{0,1},{1,0},{2,3},{3,2},{4,5},{5,4},{6,7},{7,6},{8,9},{9,8},{10,11... | collective-permute-start | bytes 1769480 | tf_op jit(solution)/shard_map/ppermute | solution.py:67
  122.7 0.5 collective-permute-start.19
  123.2 0.1 copy.11.scale_ref
  123.4 1.1 collective-permute-done.21.refs_7_
  124.5 1.7 %collective-permute-done.20.refs_6_ = bf16[128,2304]{1,0:T(8,128)(2,1)} collective-permute-done((bf16[128,2304]{1,0:T(8,128)(2,1)S(1)}, bf16[128,2304]{1,0:T(8,128)(2,1)}, u32[]{:S(2)}, u32[]{:S(2)}) %collective-permute-start.20) | collective-permute-done | bytes 589856 | tf_op jit(solution)/shard_map/ppermute | solution.py:67
  126.2 0.2 collective-permute-done.19.refs_5_
  126.4 17.1 %tail.1 = (bf16[512,4608]{1,0:T(8,128)(2,1)}, bf16[4608,512]{1,0:T(8,128)(2,1)}, f32[1,512]{1,0:T(1,128)}, f32[4,4608]{1,0:T(4,128)}) custom-call(s32[1]{0:T(128)} %bitcast.core, bf16[528,512]{1,0:T(8,128)(2,1)S(1)} %pad_maximum_fusion.left_ref, f32[512,512]{1,0:T(8,128)} %copy-done.8, f32[512,1]{1,0:T(8,128)S(1)} %copy.11.scale_ref, f32[1,512]{1,0:T(1,128)S(1)} %bitcast.23, ...), custom_call_target="tpu_custom_call" | custom-call | tf_op jit(solution)/shard_map/tail/pallas_call | solution.py:198
  (50 shorter events, 0.8 us)
Async XLA Ops:
  0.6 50.9 %slice-start = ((s8[4718592]{0:T(1024)(128)(4,1)}), s8[524288]{0:T(1024)(128)(4,1)S(1)}, s32[]{:S(2)}) async-start(s8[4718592]{0:T(1024)(128)(4,1)} %bitcast.25), calls=%async_computation.3 | async-start | bytes 1048576
  1.5 2.3 %collective-permute-start = (bf16[4,2304]{1,0:T(4,128)(2,1)S(1)}, bf16[4,2304]{1,0:T(4,128)(2,1)S(1)}, u32[]{:S(2)}, u32[]{:S(2)}) collective-permute-start(bf16[4,2304]{1,0:T(4,128)(2,1)S(1)} %get-tuple-element.32), channel_id=1, source_target_pairs={{0,1},{1,0},{2,3},{3,2},{4,5},{5,4},{6,7},{7,6},{8,9},{9,8},{10,11... | collective-permute-start | bytes 55304 | tf_op jit(solution)/shard_map/ppermute | solution.py:67
  28.0 9.0 %collective-permute-start.3 = (bf16[128,2304]{1,0:T(8,128)(2,1)S(1)}, bf16[128,2304]{1,0:T(8,128)(2,1)S(1)}, u32[]{:S(2)}, u32[]{:S(2)}) collective-permute-start(bf16[128,2304]{1,0:T(8,128)(2,1)S(1)} %bitcast.12), channel_id=1, source_target_pairs={{0,32},{1,97},{2,34},{3,99},{4,36},{5,101},{6,38},{7,103},{8,40},{... | collective-permute-start | bytes 1769480 | tf_op jit(solution)/shard_map/ppermute | solution.py:52
  28.0 12.7 %collective-permute-start.2 = (bf16[128,2304]{1,0:T(8,128)(2,1)S(1)}, bf16[128,2304]{1,0:T(8,128)(2,1)S(1)}, u32[]{:S(2)}, u32[]{:S(2)}) collective-permute-start(bf16[128,2304]{1,0:T(8,128)(2,1)S(1)} %bitcast.13), channel_id=1, source_target_pairs={{0,2},{1,7},{2,4},{3,1},{4,6},{5,3},{6,0},{7,5},{8,10},{9,15},{10,... | collective-permute-start | bytes 1769480 | tf_op jit(solution)/shard_map/ppermute | solution.py:52
  29.0 11.8 %collective-permute-start.1 = (bf16[128,2304]{1,0:T(8,128)(2,1)S(1)}, bf16[128,2304]{1,0:T(8,128)(2,1)S(1)}, u32[]{:S(2)}, u32[]{:S(2)}) collective-permute-start(bf16[128,2304]{1,0:T(8,128)(2,1)S(1)} %bitcast.14), channel_id=1, source_target_pairs={{0,8},{1,25},{2,10},{3,27},{4,12},{5,29},{6,14},{7,31},{8,16},{9,1... | collective-permute-start | bytes 1769480 | tf_op jit(solution)/shard_map/ppermute | solution.py:52
  31.3 10.1 %collective-permute-start.4 = (bf16[128,2304]{1,0:T(8,128)(2,1)S(1)}, bf16[128,2304]{1,0:T(8,128)(2,1)S(1)}, u32[]{:S(2)}, u32[]{:S(2)}) collective-permute-start(bf16[128,2304]{1,0:T(8,128)(2,1)S(1)} %bitcast.15), channel_id=1, source_target_pairs={{0,1},{1,0},{2,3},{3,2},{4,5},{5,4},{6,7},{7,6},{8,9},{9,8},{10,11... | collective-permute-start | bytes 1769480 | tf_op jit(solution)/shard_map/ppermute | solution.py:67
  37.1 14.4 %copy-start.1 = (bf16[128,2304]{1,0:T(8,128)(2,1)}, bf16[128,2304]{1,0:T(8,128)(2,1)S(1)}, u32[]{:S(2)}) copy-start(bf16[128,2304]{1,0:T(8,128)(2,1)S(1)} %collective-permute-done.3.refs_3_.refs_11_) | copy-start | bytes 1769476
  37.1 5.3 %collective-permute-start.7 = (bf16[128,2304]{1,0:T(8,128)(2,1)S(1)}, bf16[128,2304]{1,0:T(8,128)(2,1)S(1)}, u32[]{:S(2)}, u32[]{:S(2)}) collective-permute-start(bf16[128,2304]{1,0:T(8,128)(2,1)S(1)} %collective-permute-done.3.refs_3_.refs_11_), channel_id=1, source_target_pairs={{0,1},{1,0},{2,3},{3,2},{4,5},{5,4},{6,7},{7,6},{8,9},{9,8},{10,11... | collective-permute-start | bytes 1769480 | tf_op jit(solution)/shard_map/ppermute | solution.py:67
  40.7 10.7 %copy-start.2 = (bf16[128,2304]{1,0:T(8,128)(2,1)}, bf16[128,2304]{1,0:T(8,128)(2,1)S(1)}, u32[]{:S(2)}) copy-start(bf16[128,2304]{1,0:T(8,128)(2,1)S(1)} %collective-permute-done.2.refs_2_.refs_10_) | copy-start | bytes 1769476
  40.7 2.5 %collective-permute-start.6 = (bf16[128,2304]{1,0:T(8,128)(2,1)S(1)}, bf16[128,2304]{1,0:T(8,128)(2,1)S(1)}, u32[]{:S(2)}, u32[]{:S(2)}) collective-permute-start(bf16[128,2304]{1,0:T(8,128)(2,1)S(1)} %collective-permute-done.2.refs_2_.refs_10_), channel_id=1, source_target_pairs={{0,1},{1,0},{2,3},{3,2},{4,5},{5,4},{6,7},{7,6},{8,9},{9,8},{10,11... | collective-permute-start | bytes 1769480 | tf_op jit(solution)/shard_map/ppermute | solution.py:67
  40.8 10.6 %copy-start.3 = (bf16[128,2304]{1,0:T(8,128)(2,1)}, bf16[128,2304]{1,0:T(8,128)(2,1)S(1)}, u32[]{:S(2)}) copy-start(bf16[128,2304]{1,0:T(8,128)(2,1)S(1)} %collective-permute-done.1.refs_1_.refs_9_) | copy-start | bytes 1769476
  40.8 3.2 %collective-permute-start.5 = (bf16[128,2304]{1,0:T(8,128)(2,1)S(1)}, bf16[128,2304]{1,0:T(8,128)(2,1)S(1)}, u32[]{:S(2)}, u32[]{:S(2)}) collective-permute-start(bf16[128,2304]{1,0:T(8,128)(2,1)S(1)} %collective-permute-done.1.refs_1_.refs_9_), channel_id=1, source_target_pairs={{0,1},{1,0},{2,3},{3,2},{4,5},{5,4},{6,7},{7,6},{8,9},{9,8},{10,11... | collective-permute-start | bytes 1769480 | tf_op jit(solution)/shard_map/ppermute | solution.py:67
  41.4 10.1 %copy-start.4 = (bf16[128,2304]{1,0:T(8,128)(2,1)}, bf16[128,2304]{1,0:T(8,128)(2,1)S(1)}, u32[]{:S(2)}) copy-start(bf16[128,2304]{1,0:T(8,128)(2,1)S(1)} %collective-permute-done.4.refs_4_.refs_12_) | copy-start | bytes 1769476
  42.3 9.1 %copy-start.5 = (bf16[128,2304]{1,0:T(8,128)(2,1)}, bf16[128,2304]{1,0:T(8,128)(2,1)S(1)}, u32[]{:S(2)}) copy-start(bf16[128,2304]{1,0:T(8,128)(2,1)S(1)} %collective-permute-done.7.refs_7_.refs_15_) | copy-start | bytes 1769476
  43.2 8.3 %copy-start.6 = (bf16[128,2304]{1,0:T(8,128)(2,1)}, bf16[128,2304]{1,0:T(8,128)(2,1)S(1)}, u32[]{:S(2)}) copy-start(bf16[128,2304]{1,0:T(8,128)(2,1)S(1)} %collective-permute-done.6.refs_6_.refs_14_) | copy-start | bytes 1769476
  44.0 7.5 %copy-start.7 = (bf16[128,2304]{1,0:T(8,128)(2,1)}, bf16[128,2304]{1,0:T(8,128)(2,1)S(1)}, u32[]{:S(2)}) copy-start(bf16[128,2304]{1,0:T(8,128)(2,1)S(1)} %collective-permute-done.5.refs_5_.refs_13_) | copy-start | bytes 1769476
  44.0 2.5 %copy-start = (bf16[4608,512]{1,0:T(8,128)(2,1)S(1)}, bf16[4608,512]{1,0:T(8,128)(2,1)}, u32[]{:S(2)}) copy-start(bf16[4608,512]{1,0:T(8,128)(2,1)} %enc_ref.1) | copy-start | bytes 14155780
  46.6 0.7 copy-start.9
  47.3 4.3 %slice-start.1 = ((s8[4718592]{0:T(1024)(128)(4,1)}), s8[4194304]{0:T(1024)(128)(4,1)S(1)}, s32[]{:S(2)}) async-start(s8[4718592]{0:T(1024)(128)(4,1)} %bitcast.25), calls=%async_computation.4 | async-start | bytes 8388608
  51.5 1.4 %copy-start.8 = (f32[512,512]{1,0:T(8,128)}, f32[512,512]{1,0:T(8,128)S(1)}, u32[]{:S(2)}) copy-start(f32[512,512]{1,0:T(8,128)S(1)} %get-tuple-element.16.preact_ref) | copy-start | bytes 3145732
  53.1 2.5 %collective-permute-start.13 = (bf16[128,2304]{1,0:T(8,128)(2,1)S(1)}, bf16[128,2304]{1,0:T(8,128)(2,1)S(1)}, u32[]{:S(2)}, u32[]{:S(2)}) collective-permute-start(bf16[128,2304]{1,0:T(8,128)(2,1)S(1)} %get-tuple-element.28), channel_id=1, source_target_pairs={{0,1},{1,0},{2,3},{3,2},{4,5},{5,4},{6,7},{7,6},{8,9},{9,8},{10,11... | collective-permute-start | bytes 1769480 | tf_op jit(solution)/shard_map/ppermute | solution.py:67
  53.6 3.3 %collective-permute-start.11 = (bf16[128,2304]{1,0:T(8,128)(2,1)S(1)}, bf16[128,2304]{1,0:T(8,128)(2,1)S(1)}, u32[]{:S(2)}, u32[]{:S(2)}) collective-permute-start(bf16[128,2304]{1,0:T(8,128)(2,1)S(1)} %get-tuple-element.29), channel_id=1, source_target_pairs={{0,1},{1,0},{2,3},{3,2},{4,5},{5,4},{6,7},{7,6},{8,9},{9,8},{10,11... | collective-permute-start | bytes 1769480 | tf_op jit(solution)/shard_map/ppermute | solution.py:67
  53.7 4.0 %collective-permute-start.9 = (bf16[128,2304]{1,0:T(8,128)(2,1)S(1)}, bf16[128,2304]{1,0:T(8,128)(2,1)S(1)}, u32[]{:S(2)}, u32[]{:S(2)}) collective-permute-start(bf16[128,2304]{1,0:T(8,128)(2,1)S(1)} %get-tuple-element.30), channel_id=1, source_target_pairs={{0,1},{1,0},{2,3},{3,2},{4,5},{5,4},{6,7},{7,6},{8,9},{9,8},{10,11... | collective-permute-start | bytes 1769480 | tf_op jit(solution)/shard_map/ppermute | solution.py:67
  54.1 13.5 %collective-permute-start.8 = (bf16[128,2304]{1,0:T(8,128)(2,1)S(1)}, bf16[128,2304]{1,0:T(8,128)(2,1)}, u32[]{:S(2)}, u32[]{:S(2)}) collective-permute-start(bf16[128,2304]{1,0:T(8,128)(2,1)S(1)} %get-tuple-element.27), channel_id=1, source_target_pairs={{0,1},{1,0},{2,3},{3,2},{4,5},{5,4},{6,7},{7,6},{8,9},{9,8},{10,11... | collective-permute-start | bytes 1769480 | tf_op jit(solution)/shard_map/ppermute | solution.py:67
  55.6 3.3 %copy-start.10 = (f32[512,2304]{1,0:T(8,128)}, f32[512,2304]{1,0:T(8,128)S(1)}, u32[]{:S(2)}) copy-start(f32[512,2304]{1,0:T(8,128)S(1)} %fusion.1) | copy-start | bytes 14155780
  58.9 9.3 %collective-permute-start.10 = (bf16[128,2304]{1,0:T(8,128)(2,1)}, bf16[128,2304]{1,0:T(8,128)(2,1)}, u32[]{:S(2)}, u32[]{:S(2)}) collective-permute-start(bf16[128,2304]{1,0:T(8,128)(2,1)} %get-tuple-element.24), channel_id=1, source_target_pairs={{0,8},{1,25},{2,10},{3,27},{4,12},{5,29},{6,14},{7,31},{8,16},{9,1... | collective-permute-start | bytes 1769480 | tf_op jit(solution)/shard_map/ppermute | solution.py:56
  60.4 9.1 %collective-permute-start.14 = (bf16[128,2304]{1,0:T(8,128)(2,1)S(1)}, bf16[128,2304]{1,0:T(8,128)(2,1)}, u32[]{:S(2)}, u32[]{:S(2)}) collective-permute-start(bf16[128,2304]{1,0:T(8,128)(2,1)S(1)} %get-tuple-element.25), channel_id=1, source_target_pairs={{0,32},{1,97},{2,34},{3,99},{4,36},{5,101},{6,38},{7,103},{8,40},{... | collective-permute-start | bytes 1769480 | tf_op jit(solution)/shard_map/ppermute | solution.py:56
  62.5 8.8 %collective-permute-start.12 = (bf16[128,2304]{1,0:T(8,128)(2,1)S(1)}, bf16[128,2304]{1,0:T(8,128)(2,1)}, u32[]{:S(2)}, u32[]{:S(2)}) collective-permute-start(bf16[128,2304]{1,0:T(8,128)(2,1)S(1)} %get-tuple-element.26), channel_id=1, source_target_pairs={{0,2},{1,7},{2,4},{3,1},{4,6},{5,3},{6,0},{7,5},{8,10},{9,15},{10,... | collective-permute-start | bytes 1769480 | tf_op jit(solution)/shard_map/ppermute | solution.py:56
  74.5 15.7 %all-to-all-start.1 = ((bf16[16,8,2304]{2,1,0:T(8,128)(2,1)}), bf16[16,8,2304]{2,1,0:T(8,128)(2,1)S(1)}, u32[]{:S(2)}, u32[]{:S(2)}) async-start(bf16[16,8,2304]{2,1,0:T(8,128)(2,1)} %fusion.7), calls=%async_computation.1 | async-start | bytes 1179648 | tf_op jit(solution)/shard_map/all_to_all | solution.py:62
  106.6 8.7 %collective-permute-start.17 = (bf16[128,2304]{1,0:T(8,128)(2,1)S(1)}, bf16[128,2304]{1,0:T(8,128)(2,1)S(1)}, u32[]{:S(2)}, u32[]{:S(2)}) collective-permute-start(bf16[128,2304]{1,0:T(8,128)(2,1)S(1)} %bitcast.18), channel_id=1, source_target_pairs={{0,32},{1,97},{2,34},{3,99},{4,36},{5,101},{6,38},{7,103},{8,40},{... | collective-permute-start | bytes 1769480 | tf_op jit(solution)/shard_map/ppermute | solution.py:52
  106.6 16.1 %collective-permute-start.16 = (bf16[128,2304]{1,0:T(8,128)(2,1)S(1)}, bf16[128,2304]{1,0:T(8,128)(2,1)S(1)}, u32[]{:S(2)}, u32[]{:S(2)}) collective-permute-start(bf16[128,2304]{1,0:T(8,128)(2,1)S(1)} %bitcast.19), channel_id=1, source_target_pairs={{0,2},{1,7},{2,4},{3,1},{4,6},{5,3},{6,0},{7,5},{8,10},{9,15},{10,... | collective-permute-start | bytes 1769480 | tf_op jit(solution)/shard_map/ppermute | solution.py:52
  108.7 14.0 %collective-permute-start.15 = (bf16[128,2304]{1,0:T(8,128)(2,1)S(1)}, bf16[128,2304]{1,0:T(8,128)(2,1)}, u32[]{:S(2)}, u32[]{:S(2)}) collective-permute-start(bf16[128,2304]{1,0:T(8,128)(2,1)S(1)} %bitcast.20), channel_id=1, source_target_pairs={{0,8},{1,25},{2,10},{3,27},{4,12},{5,29},{6,14},{7,31},{8,16},{9,1... | collective-permute-start | bytes 1769480 | tf_op jit(solution)/shard_map/ppermute | solution.py:52
  109.1 14.2 %collective-permute-start.18 = (bf16[128,2304]{1,0:T(8,128)(2,1)S(1)}, bf16[128,2304]{1,0:T(8,128)(2,1)}, u32[]{:S(2)}, u32[]{:S(2)}) collective-permute-start(bf16[128,2304]{1,0:T(8,128)(2,1)S(1)} %bitcast.21), channel_id=1, source_target_pairs={{0,1},{1,0},{2,3},{3,2},{4,5},{5,4},{6,7},{7,6},{8,9},{9,8},{10,11... | collective-permute-start | bytes 1769480 | tf_op jit(solution)/shard_map/ppermute | solution.py:67
  115.3 9.1 %collective-permute-start.21 = (bf16[128,2304]{1,0:T(8,128)(2,1)S(1)}, bf16[128,2304]{1,0:T(8,128)(2,1)}, u32[]{:S(2)}, u32[]{:S(2)}) collective-permute-start(bf16[128,2304]{1,0:T(8,128)(2,1)S(1)} %collective-permute-done.17.refs_3_), channel_id=1, source_target_pairs={{0,1},{1,0},{2,3},{3,2},{4,5},{5,4},{6,7},{7,6},{8,9},{9,8},{10,11... | collective-permute-start | bytes 1769480 | tf_op jit(solution)/shard_map/ppermute | solution.py:67
  122.7 3.4 %collective-permute-start.20 = (bf16[128,2304]{1,0:T(8,128)(2,1)S(1)}, bf16[128,2304]{1,0:T(8,128)(2,1)}, u32[]{:S(2)}, u32[]{:S(2)}) collective-permute-start(bf16[128,2304]{1,0:T(8,128)(2,1)S(1)} %collective-permute-done.16.refs_2_), channel_id=1, source_target_pairs={{0,1},{1,0},{2,3},{3,2},{4,5},{5,4},{6,7},{7,6},{8,9},{9,8},{10,11... | collective-permute-start | bytes 1769480 | tf_op jit(solution)/shard_map/ppermute | solution.py:67
  122.7 3.6 %collective-permute-start.19 = (bf16[128,2304]{1,0:T(8,128)(2,1)}, bf16[128,2304]{1,0:T(8,128)(2,1)}, u32[]{:S(2)}, u32[]{:S(2)}) collective-permute-start(bf16[128,2304]{1,0:T(8,128)(2,1)} %collective-permute-done.15.refs_1_), channel_id=1, source_target_pairs={{0,1},{1,0},{2,3},{3,2},{4,5},{5,4},{6,7},{7,6},{8,9},{9,8},{10,11... | collective-permute-start | bytes 1769480 | tf_op jit(solution)/shard_map/ppermute | solution.py:67

commit v3 on v1

v3 whole, which is shorter than its diff:
```python
import functools
import itertools
import math

import jax
import jax.numpy as jnp
from jax import lax
from jax.experimental import pallas as pl
from jax.experimental.pallas import tpu as pltpu
from jax.sharding import Mesh, PartitionSpec as P

CHIPS = ("z", "xh", "xl", "y")
NAMES = CHIPS + ("c",)
SWAP = [(0, 1), (1, 0)]
SMALL_VMEM = 12 * 2**20
TAIL_VMEM = 20 * 2**20
SMEM = pl.BlockSpec(memory_space=pltpu.SMEM)
VMEM = pl.BlockSpec(memory_space=pltpu.VMEM)
ANY = pl.BlockSpec(memory_space=pl.ANY)
HBM = pl.BlockSpec(memory_space=pltpu.HBM)


def chip_index(z, x, y):
    return ((z % 4) * 4 + x % 4) * 4 + y % 4


def chip_classes():
    groups = []
    for b, a in itertools.product(range(2), range(2)):
        group = []
        for z, x, y in itertools.product(range(4), range(2), range(2)):
            group.append(chip_index(z, 2 * x + (a + z) % 2, 2 * y + (b + z) % 2))
        groups.append(group)
    return groups


def neighbour_shifts():
    shifts = []
    for step in ((0, 1, 0), (0, 0, 1), (1, 0, 0)):
        pairs = []
        for z, x, y in itertools.product(range(4), repeat=3):
            for c in range(2):
                s = 1 - 2 * c
                to = chip_index(z + s * step[0], x + s * step[1], y + s * step[2])
                pairs.append((chip_index(z, x, y) * 2 + c, to * 2 + c))
        shifts.append(pairs)
    return shifts


CLASSES = chip_classes()
SHIFTS = neighbour_shifts()


def gather_chips(block):
    copies = jnp.broadcast_to(block[None], (16,) + block.shape)
    near = lax.all_to_all(copies, CHIPS, 0, 0, axis_index_groups=CLASSES)
    near = near.reshape(16 * block.shape[0], block.shape[1])
    return [near] + [lax.ppermute(near, NAMES, pairs) for pairs in SHIFTS]


def swap_cores(a):
    return lax.ppermute(a, "c", SWAP)


def stack(blocks):
    return jnp.concatenate([ref[...] for ref in blocks], axis=0)


def estimate(flops, moved):
    return pl.CostEstimate(flops=flops, bytes_accessed=moved, transcendentals=0)


def load_kernel(core_ref, near_ref, enc_ref, dec_ref, enc_own, enc_oth, dec_own, dec_oth, sems):
    half = enc_own.shape[0]
    copies = []
    for k, (enc, dec) in enumerate(((enc_own, dec_own), (enc_oth, dec_oth))):
        base = pl.multiple_of(jnp.where(core_ref[0] == k, 0, half), 128)
        copies.append(pltpu.make_async_copy(enc_ref.at[pl.ds(base, half), :], enc, sems.at[k, 0]))
        copies.append(pltpu.make_async_copy(dec_ref.at[:, pl.ds(base, half)], dec, sems.at[k, 1]))
    for copy in copies:
        copy.start()
    for copy in copies:
        copy.wait()


def load(core, near, enc_weight, dec_weight):
    width, latents = enc_weight.shape
    half = width // 2
    enc_half = jax.ShapeDtypeStruct((half, latents), jnp.bfloat16)
    dec_half = jax.ShapeDtypeStruct((latents, half), jnp.bfloat16)
    return pl.pallas_call(
        load_kernel,
        out_shape=(enc_half, enc_half, dec_half, dec_half),
        in_specs=[SMEM, ANY, HBM, HBM],
        out_specs=(VMEM,) * 4,
        scratch_shapes=[pltpu.SemaphoreType.DMA((2, 2))],
        compiler_params=pltpu.CompilerParams(vmem_limit_bytes=SMALL_VMEM),
        cost_estimate=estimate(0, 8 * width * latents),
        name="load",
    )(core, near, enc_weight, dec_weight)


def pre_kernel(enc_ref, x0, x1, x2, x3, total_ref):
    total_ref[...] = jnp.dot(stack((x0, x1, x2, x3)), enc_ref[...], preferred_element_type=jnp.float32)


def pre(x_own, enc_own):
    rows, half = x_own[0].shape
    latents = enc_own.shape[1]
    return pl.pallas_call(
        pre_kernel,
        out_shape=jax.ShapeDtypeStruct((4 * rows, latents), jnp.float32),
        in_specs=[VMEM] * 5,
        out_specs=VMEM,
        compiler_params=pltpu.CompilerParams(vmem_limit_bytes=SMALL_VMEM),
        cost_estimate=estimate(8 * rows * half * latents, 4 * rows * half),
        name="pre",
    )(enc_own, *x_own)


def front_kernel(n, bias_ref, total_ref, enc_ref, dec_ref, x0, x1, x2, x3, preact_ref, act_ref, *part_refs):
    rows, half = x0.shape
    wide = half // n
    product = jnp.dot(stack((x0, x1, x2, x3)), enc_ref[...], preferred_element_type=jnp.float32)
    preact = total_ref[...] + product + bias_ref[...]
    preact_ref[...] = preact
    act_ref[...] = jnp.maximum(preact, 0.0).astype(jnp.bfloat16)
    for k in range(n):
        cols = slice(k * wide, (k + 1) * wide)
        product = jnp.dot(act_ref[...], dec_ref[:, cols], preferred_element_type=jnp.float32).astype(jnp.bfloat16)
        for b, ref in enumerate(part_refs):
            ref[:, cols] = product[b * rows : (b + 1) * rows]


def front(total, x_oth, enc_oth, enc_bias, dec_oth, n):
    rows, half = x_oth[0].shape
    total_rows, latents = total.shape
    out = pl.pallas_call(
        functools.partial(front_kernel, n),
        out_shape=[
            jax.ShapeDtypeStruct((total_rows, latents), jnp.float32),
            jax.ShapeDtypeStruct((total_rows, latents), jnp.bfloat16),
        ]
        + [jax.ShapeDtypeStruct((rows, half), jnp.bfloat16)] * 4,
        in_specs=[VMEM] * 8,
        out_specs=[VMEM] * 6,
        compiler_params=pltpu.CompilerParams(vmem_limit_bytes=SMALL_VMEM),
        cost_estimate=estimate(4 * total_rows * latents * half, 8 * latents * half),
        name="front",
    )(enc_bias[None], total, enc_oth, dec_oth, *x_oth)
    return out[0], out[1], out[2:]


def own_kernel(n, act_ref, dec_ref, *part_refs):
    rows, half = part_refs[0].shape
    wide = half // n
    for k in range(n):
        cols = slice(k * wide, (k + 1) * wide)
        product = jnp.dot(act_ref[...], dec_ref[:, cols], preferred_element_type=jnp.float32).astype(jnp.bfloat16)
        for b, ref in enumerate(part_refs):
            ref[:, cols] = product[b * rows : (b + 1) * rows]


def own_parts(act, dec_own, n):
    total_rows, latents = act.shape
    half = dec_own.shape[1]
    return pl.pallas_call(
        functools.partial(own_kernel, n),
        out_shape=[jax.ShapeDtypeStruct((total_rows // 4, half), jnp.bfloat16)] * 4,
        in_specs=[VMEM] * 2,
        out_specs=[VMEM] * 4,
        compiler_params=pltpu.CompilerParams(vmem_limit_bytes=SMALL_VMEM),
        cost_estimate=estimate(2 * total_rows * latents * half, 6 * latents * half),
        name="own_parts",
    )(act, dec_own)


def side_kernel(row_scale, place_ref, act_ref, dec_own, dec_oth, left_ref, scale_ref, norm_ref):
    latents, half = dec_own.shape
    total_rows = act_ref.shape[0]
    act = act_ref[...]
    left_ref[:latents] = act.T
    spot = lax.broadcasted_iota(jnp.int32, (16, total_rows), 0)
    target = jnp.full((16, total_rows), -1, jnp.int32)
    for r in range(place_ref.shape[0]):
        target = jnp.where(spot == r, place_ref[r], target)
    chosen = lax.broadcasted_iota(jnp.int32, (16, total_rows), 1) == target
    left_ref[latents:] = jnp.where(chosen, 1.0, 0.0).astype(jnp.bfloat16)
    total = jnp.sum(act.astype(jnp.float32), axis=0, keepdims=True) / row_scale
    total = jnp.broadcast_to(total, (128, latents)).T[:, :1]
    squares = jnp.zeros((latents, 128), jnp.float32)
    for dec in (dec_own, dec_oth):
        for c in range(half // 128):
            wide = dec[:, c * 128 : (c + 1) * 128].astype(jnp.float32)
            squares = squares + wide * wide
    norms = jnp.sqrt(jnp.sum(squares, axis=1, keepdims=True) + 1e-06)
    scale_ref[...] = total / norms
    norm_ref[...] = jnp.broadcast_to(norms / row_scale, (latents, 128)).T[:1]


def side(place, act, dec_own, dec_oth, row_scale):
    total_rows, latents = act.shape
    width = 2 * dec_own.shape[1]
    return pl.pallas_call(
        functools.partial(side_kernel, row_scale),
        out_shape=(
            jax.ShapeDtypeStruct((latents + 16, total_rows), jnp.bfloat16),
            jax.ShapeDtypeStruct((latents, 1), jnp.float32),
            jax.ShapeDtypeStruct((1, latents), jnp.float32),
        ),
        in_specs=[SMEM] + [VMEM] * 3,
        out_specs=(VMEM, VMEM, VMEM),
        compiler_params=pltpu.CompilerParams(vmem_limit_bytes=SMALL_VMEM),
        cost_estimate=estimate(4 * latents * width, 2 * latents * width),
        name="side",
    )(place, act, dec_own, dec_oth)


def decoder_half(n, base, row_scale, left_ref, scale_ref, dec_ref, err, dec_out, dec_grad_ref, recon_ref, sems):
    latents, half = dec_ref.shape
    wide = half // n
    outs = []
    for k in range(n):
        cols = slice(k * wide, (k + 1) * wide)
        both = jnp.dot(left_ref[...], err[:, cols], preferred_element_type=jnp.float32)
        grad = both[:latents] + scale_ref[...] * dec_ref[:, cols].astype(jnp.float32)
        dec_out[k] = grad.astype(jnp.bfloat16)
        start = pl.multiple_of(base + k * wide, 128)
        out = pltpu.make_async_copy(dec_out.at[k], dec_grad_ref.at[:, pl.ds(start, wide)], sems.at[k])
        out.start()
        outs.append(out)
        recon_ref[k] = both[latents : latents + recon_ref.shape[1]] * row_scale
    return outs


def grad_own_kernel(n, row_scale, core_ref, left_ref, scale_ref, dec_ref, *refs):
    blocks = refs[:4]
    total_ref, recon_ref, dec_grad_ref, dec_out, sems = refs[4:]
    half = dec_ref.shape[1]
    err = stack(blocks)
    outs = decoder_half(
        n, core_ref[0] * half, row_scale, left_ref, scale_ref, dec_ref, err, dec_out, dec_grad_ref, recon_ref, sems
    )
    total_ref[...] = lax.dot_general(err, dec_ref[...], (((1,), (1,)), ((), ())), preferred_element_type=jnp.float32)
    for out in outs:
        out.wait()


def grad_own(core, left, scale, dec_own, e_own, row_scale, out_rows, n):
    rows, half = e_own[0].shape
    latents = dec_own.shape[0]
    wide = half // n
    return pl.pallas_call(
        functools.partial(grad_own_kernel, n, row_scale),
        out_shape=(
            jax.ShapeDtypeStruct((4 * rows, latents), jnp.float32),
            jax.ShapeDtypeStruct((n, out_rows, wide), jnp.float32),
            jax.ShapeDtypeStruct((latents, 2 * half), jnp.bfloat16),
        ),
        in_specs=[SMEM] + [VMEM] * 7,
        out_specs=(VMEM, VMEM, HBM),
        scratch_shapes=[pltpu.VMEM((n, latents, wide), jnp.bfloat16), pltpu.SemaphoreType.DMA((n,))],
        compiler_params=pltpu.CompilerParams(vmem_limit_bytes=SMALL_VMEM),
        cost_estimate=estimate(16 * rows * latents * half, 4 * latents * half),
        name="grad_own",
    )(core, left, scale, dec_own, *e_own)


def tail_kernel(n, row_scale, core_ref, left_ref, preact_ref, scale_ref, norm_ref, total_ref, recon_own, dec_ref, *refs):
    e_oth, x_blocks = refs[:4], (refs[4:8], refs[8:12])
    dec_grad_ref, enc_grad_ref, bias_ref, recon_ref = refs[13:17]
    dec_out, enc_out, recon_oth, pre_ref, dec_sems, enc_sems = refs[17:]
    core = core_ref[0]
    half = dec_ref.shape[1]
    wide = half // n
    bases = (core * half, (1 - core) * half)
    err = stack(e_oth)
    outs = decoder_half(
        n, bases[1], row_scale, left_ref, scale_ref, dec_ref, err, dec_out, dec_grad_ref, recon_oth, dec_sems
    )
    for side_index, held in enumerate((recon_own, recon_oth)):
        for k in range(n):
            recon_ref[:, pl.ds(pl.multiple_of(bases[side_index] + k * wide, 128), wide)] = held[k]
    product = lax.dot_general(err, dec_ref[...], (((1,), (1,)), ((), ())), preferred_element_type=jnp.float32)
    act_grad = total_ref[...] + product + norm_ref[...]
    rounded = jnp.where(preact_ref[...] > 0.0, act_grad, 0.0).astype(jnp.bfloat16)
    pre_ref[...] = rounded
    bias_ref[...] = jnp.sum(rounded.astype(jnp.float32), axis=0, keepdims=True)
    for side_index in range(2):
        for k in range(n):
            spot = side_index * n + k
            mine = jnp.concatenate([ref[:, k * wide : (k + 1) * wide] for ref in x_blocks[side_index]], axis=0)
            grad = lax.dot_general(mine, pre_ref[...], (((0,), (0,)), ((), ())), preferred_element_type=jnp.float32)
            enc_out[spot] = grad.astype(jnp.bfloat16)
            start = pl.multiple_of(bases[side_index] + k * wide, 128)
            out = pltpu.make_async_copy(enc_out.at[spot], enc_grad_ref.at[pl.ds(start, wide), :], enc_sems.at[spot])
            out.start()
            outs.append(out)
    for out in outs:
        out.wait()


def tail(core, left, preact, scale, norm, total, recon_own, dec_oth, e_oth, x_own, x_oth, dec_grad, row_scale, n):
    rows, half = x_own[0].shape
    latents = dec_oth.shape[0]
    width = 2 * half
    wide = half // n
    total_rows = 4 * rows
    out_rows = recon_own.shape[1]
    return pl.pallas_call(
        functools.partial(tail_kernel, n, row_scale),
        out_shape=(
            jax.ShapeDtypeStruct((latents, width), jnp.bfloat16),
            jax.ShapeDtypeStruct((width, latents), jnp.bfloat16),
            jax.ShapeDtypeStruct((1, latents), jnp.float32),
            jax.ShapeDtypeStruct((out_rows, width), jnp.float32),
        ),
        in_specs=[SMEM] + [VMEM] * 19 + [HBM],
        out_specs=(HBM, HBM, VMEM, VMEM),
        scratch_shapes=[
            pltpu.VMEM((n, latents, wide), jnp.bfloat16),
            pltpu.VMEM((2 * n, wide, latents), jnp.bfloat16),
            pltpu.VMEM((n, out_rows, wide), jnp.float32),
            pltpu.VMEM((total_rows, latents), jnp.bfloat16),
            pltpu.SemaphoreType.DMA((n,)),
            pltpu.SemaphoreType.DMA((2 * n,)),
        ],
        input_output_aliases={20: 0},
        compiler_params=pltpu.CompilerParams(vmem_limit_bytes=TAIL_VMEM),
        cost_estimate=estimate(32 * rows * latents * half, 8 * latents * half),
        name="tail",
    )(core, left, preact, scale, norm, total, recon_own, dec_oth, *e_oth, *x_own, *x_oth, dec_grad)


def per_device(tokens, batch_order, enc_weight, enc_bias, dec_weight):
    rows_dev, width = tokens.shape
    total_rows = batch_order.shape[0]
    row_scale = math.sqrt(total_rows)
    half = width // 2
    block_rows = total_rows // 4
    core = lax.axis_index("c")
    core_arg = core[None].astype(jnp.int32)

    z = lax.axis_index("z")
    x = lax.axis_index("xh") * 2 + lax.axis_index("xl")
    y = lax.axis_index("y")
    first = (chip_index(z, x, y) * 2 + core) * rows_dev
    wanted = lax.dynamic_slice_in_dim(batch_order, first, rows_dev)
    chip = wanted // (2 * rows_dev)
    tz, tx, ty = chip // 16, chip // 4 % 4, chip % 4
    a = (tx + tz + x + z) % 2
    b = (ty + tz + y + z) % 2
    place = (a + 2 * b) * block_rows + (tz * 4 + tx // 2 * 2 + ty // 2) * (2 * rows_dev) + wanted % (2 * rows_dev)

    def pick(a, start):
        return lax.dynamic_slice_in_dim(a, start, half, 1)

    got = swap_cores(pick(tokens, (1 - core) * half))
    mine = pick(tokens, core * half)
    block = jnp.where(core == 0, jnp.concatenate([mine, got]), jnp.concatenate([got, mine]))
    block, place = lax.optimization_barrier((block, place))
    x_own = gather_chips(block)
    halves = load(core_arg, x_own[0], enc_weight, dec_weight)
    x_own[1:], halves = lax.optimization_barrier((x_own[1:], halves))
    enc_own, enc_oth, dec_own, dec_oth = halves
    x_oth = [swap_cores(a) for a in x_own]
    partial = pre(x_own, enc_own)
    preact, activations, part_oth = front(partial, x_oth, enc_oth, enc_bias, dec_oth, 3)

    part_got = [swap_cores(part_oth[k]) for k in (1, 2, 3, 0)]
    part_own = own_parts(activations, dec_own, 3)
    sent = [(part_own[k + 1].astype(jnp.float32) + part_got[k].astype(jnp.float32)).astype(jnp.bfloat16) for k in range(3)]
    got = [lax.ppermute(part, NAMES, pairs) for part, pairs in zip(sent, SHIFTS)]
    left, scale, norm = side(place, activations, dec_own, dec_oth, row_scale)
    total = part_own[0].astype(jnp.float32) + part_got[3].astype(jnp.float32)
    for part in got:
        total = total + part.astype(jnp.float32)
    total = total.astype(jnp.bfloat16).reshape(16, block_rows // 16, half)
    total, left, scale, norm = lax.optimization_barrier((total, left, scale, norm))
    pieces = lax.all_to_all(total, CHIPS, 0, 0, axis_index_groups=CLASSES)
    recon = jnp.sum(pieces.astype(jnp.float32), axis=0) - block.astype(jnp.float32)
    err_block = (recon / row_scale).astype(jnp.bfloat16)
    e_own = gather_chips(err_block)
    e_oth = [swap_cores(a) for a in e_own]
    act_part, recon_own, dec_grad = grad_own(core_arg, left, scale, dec_own, e_own, row_scale, rows_dev, 3)
    dec_grad, enc_grad, bias_grad, recon_error = tail(
        core_arg, left, preact, scale, norm, act_part, recon_own, dec_oth, e_oth, x_own, x_oth, dec_grad, row_scale, 3
    )
    return (recon_error, enc_grad, dec_grad, bias_grad[0])


def solution(mesh):
    split = Mesh(mesh.devices.reshape(4, 2, 2, 4, 2), NAMES)
    return jax.shard_map(
        per_device,
        mesh=split,
        in_specs=(P(NAMES, None), P(), P(None, NAMES), P(NAMES), P(NAMES, None)),
        out_specs=(P(NAMES, None), P(None, NAMES), P(NAMES, None), P(NAMES)),
        check_vma=False,
    )
```

time: 177 us -> 125 us (0.71)
  blocking collectives: 118 us -> 57.1 us
  matrix products: 27.5 us -> 0 us
  starting transfers between devices: 6.16 us -> 30.1 us
  Pallas kernels: 0 us -> 18.6 us
  other arithmetic: 10.2 us -> 1.83 us
    all_to_all x3, blocking collectives: 118 us -> 57.1 us  [the longest x2 39.8 us: gather_chips(): near = lax.all_to_all(copies, CHIPS, 0, 0, axis_index_groups=CLASSES)]
    dot_general x6 -> x0, matrix products: 27.5 us -> none  [the longest x1 7.37 us: per_device(): lax.dot_general(err, dec_weight, (((1,), (1,)), ((), ())), preferred_elem...]
    ppermute x4 -> x22, starting transfers between devices: 6.16 us -> 30.1 us  [the longest x13 16 us: swap_cores(): return lax.ppermute(a, 'c', SWAP)]
    pallas_call x0 -> x7, Pallas kernels: none -> 18.6 us  [the longest x1 7.37 us: tail(): pl.pallas_call(functools.partial(tail_kernel, n, row_scale), out_shape=(j...]
    select_n x1 -> x0, other arithmetic: 4.96 us -> none  [per_device(): jnp.where(core == 0, jnp.concatenate([e_own, e_oth], 1), jnp.concatenate(...]
    unnamed x20 -> x6, local copies, waits for them, and re-layouts: 0.04 us -> 4.68 us
    gather x1 -> x0, local copies, waits for them, and re-layouts: 3.63 us -> none  [per_device(): recon_error = jnp.take(err, wanted, axis=0).astype(jnp.float32) * row_scale]
    reduce_sum x1 -> x0, other arithmetic: 3.34 us -> none  [per_device(): row_norms = jnp.sqrt(jnp.sum(dec_wide * dec_wide, axis=1) + 1e-06)]
  transfers between devices with their start and end apart: 4 -> 22, of which waited for: 4 -> 9; matrix products, arithmetic and copies ran while one was open for 2% -> 1% of each run, Pallas kernels for 0% -> 7%
where the time goes in v3:
time: 125 us
  blocking collectives  57.1 us (46%)
  starting transfers between devices  30.1 us (24%)
  Pallas kernels  18.6 us (15%)
  waiting for transfers between devices  10.4 us (8%)
  local copies, waits for them, and re-layouts  5.52 us (4%)
  other arithmetic  1.83 us (1%)
    all_to_all x2, blocking collectives, gather_chips(): near = lax.all_to_all(copies, CHIPS, 0, 0, axis_index_groups=CLASSES)  39.8 us
    all_to_all x1, blocking collectives, per_device(): pieces = lax.all_to_all(total, CHIPS, 0, 0, axis_index_groups=CLASSES)  17.3 us
    ppermute x13, starting transfers between devices, swap_cores(): return lax.ppermute(a, 'c', SWAP)  16 us
    ppermute x6, starting transfers between devices, gather_chips(): return [near] + [lax.ppermute(near, NAMES, pairs) for pairs in SHIFTS]  7.77 us
    pallas_call x1, Pallas kernels, tail(): pl.pallas_call(functools.partial(tail_kernel, n, row_scale), out_shape=(j...  7.37 us
    ppermute x3, starting transfers between devices, per_device(): lax.ppermute(part, NAMES, pairs)  6.35 us
    ppermute x3, waiting for transfers between devices, per_device(): lax.ppermute(part, NAMES, pairs)  4.97 us
    unnamed x6, local copies, waits for them, and re-layouts  4.68 us
  transfers between devices with their start and end apart: 22, of which 9 were waited for; matrix products, arithmetic and copies ran while one was open for 1% of the time, Pallas kernels for 7%

profile of v3, /device:TPU:1, one launch (start us, length us, event | category | flops | bytes accessed | tf_op | source)
XLA Modules:
  0.0 124.5 jit_solution(8930798335678319381)
XLA Ops:
  0.6 0.8 constant_dynamic-slice_fusion.1
  1.4 1.5 %collective-permute-start = (bf16[4,2304]{1,0:T(4,128)(2,1)S(1)}, bf16[4,2304]{1,0:T(4,128)(2,1)S(1)}, u32[]{:S(2)}, u32[]{:S(2)}) collective-permute-start(bf16[4,2304]{1,0:T(4,128)(2,1)S(1)} %get-tuple-element.79), channel_id=1, source_target_pairs={{0,1},{1,0},{2,3},{3,2},{4,5},{5,4},{6,7},{7,6},{8,9},{9,8},{10,11... | collective-permute-start | bytes 55304 | tf_op jit(solution)/shard_map/ppermute | solution.py:62
  2.9 0.8 fusion.2.place_ref
  3.7 0.0 collective-permute-done
  3.8 24.1 %all_to_all.15 = bf16[16,8,2304]{2,1,0:T(8,128)(2,1)S(1)} all-to-all(bf16[16,8,2304]{2,1,0:T(8,128)(2,1)S(1)} %broadcast_in_dim.20), channel_id=1, replica_groups={{0,4,16,20,42,46,58,62,64,68,80,84,106,110,122,126},{8,12,24,28,34,38,5..., dimensions={0} | all-to-all | bytes 1179648 | tf_op jit(solution)/shard_map/all_to_all | solution.py:56
  28.0 0.9 collective-permute-start.2
  28.9 2.3 %collective-permute-start.1 = (bf16[128,2304]{1,0:T(8,128)(2,1)S(1)}, bf16[128,2304]{1,0:T(8,128)(2,1)S(1)}, u32[]{:S(2)}, u32[]{:S(2)}) collective-permute-start(bf16[128,2304]{1,0:T(8,128)(2,1)S(1)} %bitcast.9), channel_id=1, source_target_pairs={{0,8},{1,25},{2,10},{3,27},{4,12},{5,29},{6,14},{7,31},{8,16},{9,1... | collective-permute-start | bytes 1769480 | tf_op jit(solution)/shard_map/ppermute | solution.py:58
  31.2 0.0 collective-permute-start.4
  31.2 2.3 %copy-done = bf16[4608,512]{1,0:T(8,128)(2,1)S(1)} copy-done((bf16[4608,512]{1,0:T(8,128)(2,1)S(1)}, bf16[4608,512]{1,0:T(8,128)(2,1)}, u32[]{:S(2)}) %copy-start) | copy-done | bytes 4718616
  33.6 2.3 %copy-done.1 = bf16[512,4608]{1,0:T(8,128)(2,1)S(1)} copy-done((bf16[512,4608]{1,0:T(8,128)(2,1)S(1)}, bf16[512,4608]{1,0:T(8,128)(2,1)}, u32[]{:S(2)}) %copy-start.1) | copy-done | bytes 4718616
  35.9 0.7 load.1
  36.6 0.4 collective-permute-done.3.x3.refs_7_
  37.0 1.1 collective-permute-done.1.x1.refs_5_
  38.0 3.3 %collective-permute-start.5 = (bf16[128,2304]{1,0:T(8,128)(2,1)S(1)}, bf16[128,2304]{1,0:T(8,128)(2,1)S(1)}, u32[]{:S(2)}, u32[]{:S(2)}) collective-permute-start(bf16[128,2304]{1,0:T(8,128)(2,1)S(1)} %collective-permute-done.1.x1.refs_5_), channel_id=1, source_target_pairs={{0,1},{1,0},{2,3},{3,2},{4,5},{5,4},{6,7},{7,6},{8,9},{9,8},{10,11... | collective-permute-start | bytes 1769480 | tf_op jit(solution)/shard_map/ppermute | solution.py:62
  41.3 0.5 collective-permute-start.7
  41.8 1.4 %pre.1.total_ref = f32[512,512]{1,0:T(8,128)S(1)} custom-call(bf16[2304,512]{1,0:T(8,128)(2,1)S(1)} %get-tuple-element.46.enc_ref, bf16[128,2304]{1,0:T(8,128)(2,1)S(1)} %bitcast.12, bf16[128,2304]{1,0:T(8,128)(2,1)S(1)} %collective-permute-done.1.x1.refs_5_, bf16[128,2304]{1,0:T(8,128)(2,1)S(1)} %collective-permute-done.2.x2.refs_6_, ...), custom_call_target="tpu_custom_call" | custom-call | flops 1207959552 | bytes 1179648 | tf_op jit(solution)/shard_map/pre/pallas_call | solution.py:110
  43.2 0.6 collective-permute-done.6.x2.refs_10_
  43.8 0.8 collective-permute-done.7.x3.refs_11_
  44.6 2.7 %front.1 = (f32[512,512]{1,0:T(8,128)S(1)}, bf16[512,512]{1,0:T(8,128)(2,1)S(1)}, bf16[128,2304]{1,0:T(8,128)(2,1)S(1)}, bf16[128,2304]{1,0:T(8,128)(2,1)S(1)}, ...) custom-call(f32[1,512]{1,0:T(1,128)S(1)} %bitcast.19, f32[512,512]{1,0:T(8,128)S(1)} %pre.1.total_ref, ...), custom_call_target="tpu_custom_call" | custom-call | flops 2415919104 | bytes 9437184 | tf_op jit(solution)/shard_map/front/pallas_call | solution.py:138
  47.4 0.5 collective-permute-start.9
  47.8 0.1 collective-permute-start.8
  48.0 0.4 collective-permute-start.11
  48.4 0.1 collective-permute-start.13
  48.5 1.4 %own_parts.1 = (bf16[128,2304]{1,0:T(8,128)(2,1)S(1)}, bf16[128,2304]{1,0:T(8,128)(2,1)S(1)}, bf16[128,2304]{1,0:T(8,128)(2,1)S(1)}, bf16[128,2304]{1,0:T(8,128)(2,1)S(1)}) custom-call(bf16[512,512]{1,0:T(8,128)(2,1)S(1)} %get-tuple-element.52.act_ref, bf16[512,2304]{1,0:T(8,128)(2,1)S(1)} %get-tuple-element.53.dec_ref.dec_own), custom_call_target="tpu_custom_call" | custom-call | flops 1207959552 | bytes 7077888 | tf_op jit(solution)/shard_map/own_parts/pallas_call | solution.py:167
  49.9 0.1 add_convert_fusion.3
  50.0 1.0 collective-permute-start.10
  51.0 0.1 collective-permute-done.11
  51.2 0.2 add_convert_fusion.2
  51.4 2.3 %collective-permute-start.12 = (bf16[128,2304]{1,0:T(8,128)(2,1)S(1)}, bf16[128,2304]{1,0:T(8,128)(2,1)S(1)}, u32[]{:S(2)}, u32[]{:S(2)}) collective-permute-start(bf16[128,2304]{1,0:T(8,128)(2,1)S(1)} %add_convert_fusion.2), channel_id=1, source_target_pairs={{0,2},{1,7},{2,4},{3,1},{4,6},{5,3},{6,0},{7,5},{8,10},{9,15},{10,... | collective-permute-start | bytes 1769480 | tf_op jit(solution)/shard_map/ppermute | solution.py:373
  53.7 0.2 add_convert_fusion.1
  53.9 3.0 %collective-permute-start.14 = (bf16[128,2304]{1,0:T(8,128)(2,1)S(1)}, bf16[128,2304]{1,0:T(8,128)(2,1)S(1)}, u32[]{:S(2)}, u32[]{:S(2)}) collective-permute-start(bf16[128,2304]{1,0:T(8,128)(2,1)S(1)} %add_convert_fusion.1), channel_id=1, source_target_pairs={{0,32},{1,97},{2,34},{3,99},{4,36},{5,101},{6,38},{7,103},{8,40},{... | collective-permute-start | bytes 1769480 | tf_op jit(solution)/shard_map/ppermute | solution.py:373
  56.9 1.9 %side.1 = (bf16[528,512]{1,0:T(8,128)(2,1)S(1)}, f32[512,1]{1,0:T(8,128)S(1)}, f32[1,512]{1,0:T(1,128)S(1)}) custom-call(s32[4]{0:T(128)S(1)} %fusion.2.place_ref, bf16[512,512]{1,0:T(8,128)(2,1)S(1)} %get-tuple-element.52.act_ref, bf16[512,2304]{1,0:T(8,128)(2,1)S(1)} %get-tuple-element.53.dec_ref.dec_own, ...), custom_call_target="tpu_custom_call" | custom-call | flops 9437184 | bytes 4718592 | tf_op jit(solution)/shard_map/side/pallas_call | solution.py:204
  58.8 0.4 collective-permute-done.10
  59.1 1.4 %collective-permute-done.12 = bf16[128,2304]{1,0:T(8,128)(2,1)S(1)} collective-permute-done((bf16[128,2304]{1,0:T(8,128)(2,1)S(1)}, bf16[128,2304]{1,0:T(8,128)(2,1)S(1)}, u32[]{:S(2)}, u32[]{:S(2)}) %collective-permute-start.12) | collective-permute-done | bytes 589856 | tf_op jit(solution)/shard_map/ppermute | solution.py:373
  60.5 3.2 %collective-permute-done.14 = bf16[128,2304]{1,0:T(8,128)(2,1)S(1)} collective-permute-done((bf16[128,2304]{1,0:T(8,128)(2,1)S(1)}, bf16[128,2304]{1,0:T(8,128)(2,1)S(1)}, u32[]{:S(2)}, u32[]{:S(2)}) %collective-permute-start.14) | collective-permute-done | bytes 589856 | tf_op jit(solution)/shard_map/ppermute | solution.py:373
  63.7 0.4 fusion
  64.1 17.3 %all_to_all.16 = bf16[16,8,2304]{2,1,0:T(8,128)(2,1)S(1)} all-to-all(bf16[16,8,2304]{2,1,0:T(8,128)(2,1)S(1)} %fusion), channel_id=1, replica_groups={{0,4,16,20,42,46,58,62,64,68,80,84,106,110,122,126},{8,12,24,28,34,38,5..., dimensions={0} | all-to-all | bytes 1179648 | tf_op jit(solution)/shard_map/all_to_all | solution.py:380
  81.5 0.1 convert_reduce_fusion
  81.6 15.6 %all_to_all.17 = bf16[16,8,2304]{2,1,0:T(8,128)(2,1)S(1)} all-to-all(bf16[16,8,2304]{2,1,0:T(8,128)(2,1)S(1)} %broadcast_in_dim.21), channel_id=1, replica_groups={{0,4,16,20,42,46,58,62,64,68,80,84,106,110,122,126},{8,12,24,28,34,38,5..., dimensions={0} | all-to-all | bytes 1179648 | tf_op jit(solution)/shard_map/all_to_all | solution.py:56
  97.3 2.8 %collective-permute-start.17 = (bf16[128,2304]{1,0:T(8,128)(2,1)S(1)}, bf16[128,2304]{1,0:T(8,128)(2,1)S(1)}, u32[]{:S(2)}, u32[]{:S(2)}) collective-permute-start(bf16[128,2304]{1,0:T(8,128)(2,1)S(1)} %bitcast.14), channel_id=1, source_target_pairs={{0,32},{1,97},{2,34},{3,99},{4,36},{5,101},{6,38},{7,103},{8,40},{... | collective-permute-start | bytes 1769480 | tf_op jit(solution)/shard_map/ppermute | solution.py:58
  100.1 1.7 %collective-permute-start.15 = (bf16[128,2304]{1,0:T(8,128)(2,1)S(1)}, bf16[128,2304]{1,0:T(8,128)(2,1)S(1)}, u32[]{:S(2)}, u32[]{:S(2)}) collective-permute-start(bf16[128,2304]{1,0:T(8,128)(2,1)S(1)} %bitcast.16), channel_id=1, source_target_pairs={{0,8},{1,25},{2,10},{3,27},{4,12},{5,29},{6,14},{7,31},{8,16},{9,1... | collective-permute-start | bytes 1769480 | tf_op jit(solution)/shard_map/ppermute | solution.py:58
  101.8 2.9 %collective-permute-start.18 = (bf16[128,2304]{1,0:T(8,128)(2,1)S(1)}, bf16[128,2304]{1,0:T(8,128)(2,1)S(1)}, u32[]{:S(2)}, u32[]{:S(2)}) collective-permute-start(bf16[128,2304]{1,0:T(8,128)(2,1)S(1)} %bitcast.17), channel_id=1, source_target_pairs={{0,1},{1,0},{2,3},{3,2},{4,5},{5,4},{6,7},{7,6},{8,9},{9,8},{10,11... | collective-permute-start | bytes 1769480 | tf_op jit(solution)/shard_map/ppermute | solution.py:62
  104.7 2.4 %collective-permute-done.17.refs_3_ = bf16[128,2304]{1,0:T(8,128)(2,1)S(1)} collective-permute-done((bf16[128,2304]{1,0:T(8,128)(2,1)S(1)}, bf16[128,2304]{1,0:T(8,128)(2,1)S(1)}, u32[]{:S(2)}, u32[]{:S(2)}) %collective-permute-start.17) | collective-permute-done | bytes 589856 | tf_op jit(solution)/shard_map/ppermute | solution.py:58
  107.0 5.8 %collective-permute-start.21 = (bf16[128,2304]{1,0:T(8,128)(2,1)S(1)}, bf16[128,2304]{1,0:T(8,128)(2,1)S(1)}, u32[]{:S(2)}, u32[]{:S(2)}) collective-permute-start(bf16[128,2304]{1,0:T(8,128)(2,1)S(1)} %collective-permute-done.17.refs_3_), channel_id=1, source_target_pairs={{0,1},{1,0},{2,3},{3,2},{4,5},{5,4},{6,7},{7,6},{8,9},{9,8},{10,11... | collective-permute-start | bytes 1769480 | tf_op jit(solution)/shard_map/ppermute | solution.py:62
  112.9 0.5 collective-permute-start.20
  113.4 0.3 collective-permute-start.19
  113.7 3.2 %grad_own.1 = (f32[512,512]{1,0:T(8,128)S(1)}, f32[3,4,768]{2,1,0:T(4,128)S(1)}, bf16[512,4608]{1,0:T(8,128)(2,1)}) custom-call(s32[1]{0:T(128)} %bitcast.core_ref, bf16[528,512]{1,0:T(8,128)(2,1)S(1)} %get-tuple-element.66.left_ref, f32[512,1]{1,0:T(8,128)S(1)} %get-tuple-element.68.scale_ref, bf16[512,2304]{1,0:T(8,128)(2,1)S(1)} %get-tuple-element.53.dec_ref.dec_own, ...), custom_call_target="tpu_custom_call" | custom-call | flops 2415919104 | bytes 4718592 | tf_op jit(solution)/shard_map/grad_own/pallas_call | solution.py:253
  117.0 7.4 %tail.1 = (bf16[512,4608]{1,0:T(8,128)(2,1)}, bf16[4608,512]{1,0:T(8,128)(2,1)}, f32[1,512]{1,0:T(1,128)}, f32[4,4608]{1,0:T(4,128)}) custom-call(s32[1]{0:T(128)} %bitcast.core_ref, bf16[528,512]{1,0:T(8,128)(2,1)S(1)} %get-tuple-element.66.left_ref, f32[512,512]{1,0:T(8,128)S(1)} %get-tuple-element.67.preact_ref, ...), custom_call_target="tpu_custom_call", output_to_operand_aliasing={{0}: (20, {})} | custom-call | flops 4831838208 | bytes 9437184 | tf_op jit(solution)/shard_map/tail/pallas_call | solution.py:310
  (23 shorter events, 0.2 us)
Async XLA Ops:
  1.4 2.3 %collective-permute-start = (bf16[4,2304]{1,0:T(4,128)(2,1)S(1)}, bf16[4,2304]{1,0:T(4,128)(2,1)S(1)}, u32[]{:S(2)}, u32[]{:S(2)}) collective-permute-start(bf16[4,2304]{1,0:T(4,128)(2,1)S(1)} %get-tuple-element.79), channel_id=1, source_target_pairs={{0,1},{1,0},{2,3},{3,2},{4,5},{5,4},{6,7},{7,6},{8,9},{9,8},{10,11... | collective-permute-start | bytes 55304 | tf_op jit(solution)/shard_map/ppermute | solution.py:62
  28.0 9.0 %collective-permute-start.3 = (bf16[128,2304]{1,0:T(8,128)(2,1)S(1)}, bf16[128,2304]{1,0:T(8,128)(2,1)S(1)}, u32[]{:S(2)}, u32[]{:S(2)}) collective-permute-start(bf16[128,2304]{1,0:T(8,128)(2,1)S(1)} %bitcast.7), channel_id=1, source_target_pairs={{0,32},{1,97},{2,34},{3,99},{4,36},{5,101},{6,38},{7,103},{8,40},{... | collective-permute-start | bytes 1769480 | tf_op jit(solution)/shard_map/ppermute | solution.py:58
  28.0 9.0 %collective-permute-start.2 = (bf16[128,2304]{1,0:T(8,128)(2,1)S(1)}, bf16[128,2304]{1,0:T(8,128)(2,1)S(1)}, u32[]{:S(2)}, u32[]{:S(2)}) collective-permute-start(bf16[128,2304]{1,0:T(8,128)(2,1)S(1)} %bitcast.8), channel_id=1, source_target_pairs={{0,2},{1,7},{2,4},{3,1},{4,6},{5,3},{6,0},{7,5},{8,10},{9,15},{10,... | collective-permute-start | bytes 1769480 | tf_op jit(solution)/shard_map/ppermute | solution.py:58
  28.9 9.2 %collective-permute-start.1 = (bf16[128,2304]{1,0:T(8,128)(2,1)S(1)}, bf16[128,2304]{1,0:T(8,128)(2,1)S(1)}, u32[]{:S(2)}, u32[]{:S(2)}) collective-permute-start(bf16[128,2304]{1,0:T(8,128)(2,1)S(1)} %bitcast.9), channel_id=1, source_target_pairs={{0,8},{1,25},{2,10},{3,27},{4,12},{5,29},{6,14},{7,31},{8,16},{9,1... | collective-permute-start | bytes 1769480 | tf_op jit(solution)/shard_map/ppermute | solution.py:58
  31.2 12.0 %collective-permute-start.4 = (bf16[128,2304]{1,0:T(8,128)(2,1)S(1)}, bf16[128,2304]{1,0:T(8,128)(2,1)S(1)}, u32[]{:S(2)}, u32[]{:S(2)}) collective-permute-start(bf16[128,2304]{1,0:T(8,128)(2,1)S(1)} %bitcast.10), channel_id=1, source_target_pairs={{0,1},{1,0},{2,3},{3,2},{4,5},{5,4},{6,7},{7,6},{8,9},{9,8},{10,11... | collective-permute-start | bytes 1769480 | tf_op jit(solution)/shard_map/ppermute | solution.py:62
  31.2 2.3 %copy-start = (bf16[4608,512]{1,0:T(8,128)(2,1)S(1)}, bf16[4608,512]{1,0:T(8,128)(2,1)}, u32[]{:S(2)}) copy-start(bf16[4608,512]{1,0:T(8,128)(2,1)} %enc_ref.1) | copy-start | bytes 14155780
  33.6 2.3 %copy-start.1 = (bf16[512,4608]{1,0:T(8,128)(2,1)S(1)}, bf16[512,4608]{1,0:T(8,128)(2,1)}, u32[]{:S(2)}) copy-start(bf16[512,4608]{1,0:T(8,128)(2,1)} %dec_ref.1) | copy-start | bytes 14155780
  38.0 6.6 %copy-start.2 = (f32[512]{0:T(512)S(1)}, f32[512]{0:T(512)}, u32[]{:S(2)}) copy-start(f32[512]{0:T(512)} %param.8) | copy-start | bytes 6148
  38.0 5.2 %collective-permute-start.5 = (bf16[128,2304]{1,0:T(8,128)(2,1)S(1)}, bf16[128,2304]{1,0:T(8,128)(2,1)S(1)}, u32[]{:S(2)}, u32[]{:S(2)}) collective-permute-start(bf16[128,2304]{1,0:T(8,128)(2,1)S(1)} %collective-permute-done.1.x1.refs_5_), channel_id=1, source_target_pairs={{0,1},{1,0},{2,3},{3,2},{4,5},{5,4},{6,7},{7,6},{8,9},{9,8},{10,11... | collective-permute-start | bytes 1769480 | tf_op jit(solution)/shard_map/ppermute | solution.py:62
  41.3 2.5 %collective-permute-start.6 = (bf16[128,2304]{1,0:T(8,128)(2,1)S(1)}, bf16[128,2304]{1,0:T(8,128)(2,1)S(1)}, u32[]{:S(2)}, u32[]{:S(2)}) collective-permute-start(bf16[128,2304]{1,0:T(8,128)(2,1)S(1)} %collective-permute-done.2.x2.refs_6_), channel_id=1, source_target_pairs={{0,1},{1,0},{2,3},{3,2},{4,5},{5,4},{6,7},{7,6},{8,9},{9,8},{10,11... | collective-permute-start | bytes 1769480 | tf_op jit(solution)/shard_map/ppermute | solution.py:62
  41.3 3.3 %collective-permute-start.7 = (bf16[128,2304]{1,0:T(8,128)(2,1)S(1)}, bf16[128,2304]{1,0:T(8,128)(2,1)S(1)}, u32[]{:S(2)}, u32[]{:S(2)}) collective-permute-start(bf16[128,2304]{1,0:T(8,128)(2,1)S(1)} %collective-permute-done.3.x3.refs_7_), channel_id=1, source_target_pairs={{0,1},{1,0},{2,3},{3,2},{4,5},{5,4},{6,7},{7,6},{8,9},{9,8},{10,11... | collective-permute-start | bytes 1769480 | tf_op jit(solution)/shard_map/ppermute | solution.py:62
  47.4 2.5 %collective-permute-start.9 = (bf16[128,2304]{1,0:T(8,128)(2,1)S(1)}, bf16[128,2304]{1,0:T(8,128)(2,1)S(1)}, u32[]{:S(2)}, u32[]{:S(2)}) collective-permute-start(bf16[128,2304]{1,0:T(8,128)(2,1)S(1)} %get-tuple-element.57), channel_id=1, source_target_pairs={{0,1},{1,0},{2,3},{3,2},{4,5},{5,4},{6,7},{7,6},{8,9},{9,8},{10,11... | collective-permute-start | bytes 1769480 | tf_op jit(solution)/shard_map/ppermute | solution.py:62
  47.8 10.9 %collective-permute-start.8 = (bf16[128,2304]{1,0:T(8,128)(2,1)S(1)}, bf16[128,2304]{1,0:T(8,128)(2,1)S(1)}, u32[]{:S(2)}, u32[]{:S(2)}) collective-permute-start(bf16[128,2304]{1,0:T(8,128)(2,1)S(1)} %get-tuple-element.55), channel_id=1, source_target_pairs={{0,1},{1,0},{2,3},{3,2},{4,5},{5,4},{6,7},{7,6},{8,9},{9,8},{10,11... | collective-permute-start | bytes 1769480 | tf_op jit(solution)/shard_map/ppermute | solution.py:62
  48.0 3.2 %collective-permute-start.11 = (bf16[128,2304]{1,0:T(8,128)(2,1)S(1)}, bf16[128,2304]{1,0:T(8,128)(2,1)S(1)}, u32[]{:S(2)}, u32[]{:S(2)}) collective-permute-start(bf16[128,2304]{1,0:T(8,128)(2,1)S(1)} %get-tuple-element.59), channel_id=1, source_target_pairs={{0,1},{1,0},{2,3},{3,2},{4,5},{5,4},{6,7},{7,6},{8,9},{9,8},{10,11... | collective-permute-start | bytes 1769480 | tf_op jit(solution)/shard_map/ppermute | solution.py:62
  48.4 5.3 %collective-permute-start.13 = (bf16[128,2304]{1,0:T(8,128)(2,1)S(1)}, bf16[128,2304]{1,0:T(8,128)(2,1)S(1)}, u32[]{:S(2)}, u32[]{:S(2)}) collective-permute-start(bf16[128,2304]{1,0:T(8,128)(2,1)S(1)} %get-tuple-element.61), channel_id=1, source_target_pairs={{0,1},{1,0},{2,3},{3,2},{4,5},{5,4},{6,7},{7,6},{8,9},{9,8},{10,11... | collective-permute-start | bytes 1769480 | tf_op jit(solution)/shard_map/ppermute | solution.py:62
  50.0 9.1 %collective-permute-start.10 = (bf16[128,2304]{1,0:T(8,128)(2,1)S(1)}, bf16[128,2304]{1,0:T(8,128)(2,1)S(1)}, u32[]{:S(2)}, u32[]{:S(2)}) collective-permute-start(bf16[128,2304]{1,0:T(8,128)(2,1)S(1)} %add_convert_fusion.3), channel_id=1, source_target_pairs={{0,8},{1,25},{2,10},{3,27},{4,12},{5,29},{6,14},{7,31},{8,16},{9,1... | collective-permute-start | bytes 1769480 | tf_op jit(solution)/shard_map/ppermute | solution.py:373
  51.4 9.2 %collective-permute-start.12 = (bf16[128,2304]{1,0:T(8,128)(2,1)S(1)}, bf16[128,2304]{1,0:T(8,128)(2,1)S(1)}, u32[]{:S(2)}, u32[]{:S(2)}) collective-permute-start(bf16[128,2304]{1,0:T(8,128)(2,1)S(1)} %add_convert_fusion.2), channel_id=1, source_target_pairs={{0,2},{1,7},{2,4},{3,1},{4,6},{5,3},{6,0},{7,5},{8,10},{9,15},{10,... | collective-permute-start | bytes 1769480 | tf_op jit(solution)/shard_map/ppermute | solution.py:373
  53.9 9.8 %collective-permute-start.14 = (bf16[128,2304]{1,0:T(8,128)(2,1)S(1)}, bf16[128,2304]{1,0:T(8,128)(2,1)S(1)}, u32[]{:S(2)}, u32[]{:S(2)}) collective-permute-start(bf16[128,2304]{1,0:T(8,128)(2,1)S(1)} %add_convert_fusion.1), channel_id=1, source_target_pairs={{0,32},{1,97},{2,34},{3,99},{4,36},{5,101},{6,38},{7,103},{8,40},{... | collective-permute-start | bytes 1769480 | tf_op jit(solution)/shard_map/ppermute | solution.py:373
  97.3 9.8 %collective-permute-start.17 = (bf16[128,2304]{1,0:T(8,128)(2,1)S(1)}, bf16[128,2304]{1,0:T(8,128)(2,1)S(1)}, u32[]{:S(2)}, u32[]{:S(2)}) collective-permute-start(bf16[128,2304]{1,0:T(8,128)(2,1)S(1)} %bitcast.14), channel_id=1, source_target_pairs={{0,32},{1,97},{2,34},{3,99},{4,36},{5,101},{6,38},{7,103},{8,40},{... | collective-permute-start | bytes 1769480 | tf_op jit(solution)/shard_map/ppermute | solution.py:58
  100.1 12.8 %collective-permute-start.16 = (bf16[128,2304]{1,0:T(8,128)(2,1)S(1)}, bf16[128,2304]{1,0:T(8,128)(2,1)S(1)}, u32[]{:S(2)}, u32[]{:S(2)}) collective-permute-start(bf16[128,2304]{1,0:T(8,128)(2,1)S(1)} %bitcast.15), channel_id=1, source_target_pairs={{0,2},{1,7},{2,4},{3,1},{4,6},{5,3},{6,0},{7,5},{8,10},{9,15},{10,... | collective-permute-start | bytes 1769480 | tf_op jit(solution)/shard_map/ppermute | solution.py:58
  100.1 13.3 %collective-permute-start.15 = (bf16[128,2304]{1,0:T(8,128)(2,1)S(1)}, bf16[128,2304]{1,0:T(8,128)(2,1)S(1)}, u32[]{:S(2)}, u32[]{:S(2)}) collective-permute-start(bf16[128,2304]{1,0:T(8,128)(2,1)S(1)} %bitcast.16), channel_id=1, source_target_pairs={{0,8},{1,25},{2,10},{3,27},{4,12},{5,29},{6,14},{7,31},{8,16},{9,1... | collective-permute-start | bytes 1769480 | tf_op jit(solution)/shard_map/ppermute | solution.py:58
  101.8 15.2 %collective-permute-start.18 = (bf16[128,2304]{1,0:T(8,128)(2,1)S(1)}, bf16[128,2304]{1,0:T(8,128)(2,1)S(1)}, u32[]{:S(2)}, u32[]{:S(2)}) collective-permute-start(bf16[128,2304]{1,0:T(8,128)(2,1)S(1)} %bitcast.17), channel_id=1, source_target_pairs={{0,1},{1,0},{2,3},{3,2},{4,5},{5,4},{6,7},{7,6},{8,9},{9,8},{10,11... | collective-permute-start | bytes 1769480 | tf_op jit(solution)/shard_map/ppermute | solution.py:62
  107.0 9.9 %collective-permute-start.21 = (bf16[128,2304]{1,0:T(8,128)(2,1)S(1)}, bf16[128,2304]{1,0:T(8,128)(2,1)S(1)}, u32[]{:S(2)}, u32[]{:S(2)}) collective-permute-start(bf16[128,2304]{1,0:T(8,128)(2,1)S(1)} %collective-permute-done.17.refs_3_), channel_id=1, source_target_pairs={{0,1},{1,0},{2,3},{3,2},{4,5},{5,4},{6,7},{7,6},{8,9},{9,8},{10,11... | collective-permute-start | bytes 1769480 | tf_op jit(solution)/shard_map/ppermute | solution.py:62
  112.9 4.1 %collective-permute-start.20 = (bf16[128,2304]{1,0:T(8,128)(2,1)S(1)}, bf16[128,2304]{1,0:T(8,128)(2,1)S(1)}, u32[]{:S(2)}, u32[]{:S(2)}) collective-permute-start(bf16[128,2304]{1,0:T(8,128)(2,1)S(1)} %collective-permute-done.16.refs_2_), channel_id=1, source_target_pairs={{0,1},{1,0},{2,3},{3,2},{4,5},{5,4},{6,7},{7,6},{8,9},{9,8},{10,11... | collective-permute-start | bytes 1769480 | tf_op jit(solution)/shard_map/ppermute | solution.py:62
  113.4 3.6 %collective-permute-start.19 = (bf16[128,2304]{1,0:T(8,128)(2,1)S(1)}, bf16[128,2304]{1,0:T(8,128)(2,1)S(1)}, u32[]{:S(2)}, u32[]{:S(2)}) collective-permute-start(bf16[128,2304]{1,0:T(8,128)(2,1)S(1)} %collective-permute-done.15.refs_1_), channel_id=1, source_target_pairs={{0,1},{1,0},{2,3},{3,2},{4,5},{5,4},{6,7},{7,6},{8,9},{9,8},{10,11... | collective-permute-start | bytes 1769480 | tf_op jit(solution)/shard_map/ppermute | solution.py:62

commit v4 on v1

v4 whole, which is shorter than its diff:
```python
import functools
import itertools
import math

import jax
import jax.numpy as jnp
from jax import lax
from jax.experimental import pallas as pl
from jax.experimental.pallas import tpu as pltpu
from jax.sharding import Mesh, PartitionSpec as P

CHIPS = ("z", "xh", "xl", "y")
NAMES = CHIPS + ("c",)
SWAP = [(0, 1), (1, 0)]
SMALL_VMEM = 12 * 2**20
TAIL_VMEM = 20 * 2**20
SMEM = pl.BlockSpec(memory_space=pltpu.SMEM)
VMEM = pl.BlockSpec(memory_space=pltpu.VMEM)
ANY = pl.BlockSpec(memory_space=pl.ANY)
HBM = pl.BlockSpec(memory_space=pltpu.HBM)


def chip_index(z, x, y):
    return ((z % 4) * 4 + x % 4) * 4 + y % 4


def chip_classes():
    groups = []
    for b, a in itertools.product(range(2), range(2)):
        group = []
        for z, x, y in itertools.product(range(4), range(2), range(2)):
            group.append(chip_index(z, 2 * x + (a + z) % 2, 2 * y + (b + z) % 2))
        groups.append(group)
    return groups


def neighbour_shifts():
    shifts = []
    for step in ((0, 1, 0), (0, 0, 1), (1, 0, 0)):
        pairs = []
        for z, x, y in itertools.product(range(4), repeat=3):
            for c in range(2):
                s = 1 - 2 * c
                to = chip_index(z + s * step[0], x + s * step[1], y + s * step[2])
                pairs.append((chip_index(z, x, y) * 2 + c, to * 2 + c))
        shifts.append(pairs)
    return shifts


CLASSES = chip_classes()
SHIFTS = neighbour_shifts()
GROUPS = ((0,), (1,), (2,), (3,))


def near_copies(block):
    copies = jnp.broadcast_to(block[None], (16,) + block.shape)
    near = lax.all_to_all(copies, CHIPS, 0, 0, axis_index_groups=CLASSES)
    return near.reshape(16 * block.shape[0], block.shape[1])


def spread(near):
    return [near] + [lax.ppermute(near, NAMES, pairs) for pairs in SHIFTS]


def swap_cores(a):
    return lax.ppermute(a, "c", SWAP)


def stack(blocks):
    return jnp.concatenate([ref[...] for ref in blocks], axis=0)


def estimate(flops, moved):
    return pl.CostEstimate(flops=flops, bytes_accessed=moved, transcendentals=0)


def params(limit):
    return pltpu.CompilerParams(vmem_limit_bytes=limit)


def chunks(width):
    found, at = [], 0
    while at < width:
        step = min(768, width - at)
        if width - at == 1024:
            step = 512
        found.append((at, step))
        at += step
    return found


def load_kernel(widths, core_ref, near_ref, enc_ref, dec_ref, *refs):
    pieces = 2 * len(widths)
    enc_refs, dec_refs, sems = refs[:pieces], refs[pieces : 2 * pieces], refs[2 * pieces]
    half = sum(widths)
    copies = []
    for k in range(pieces):
        side_index, q = divmod(k, len(widths))
        base = jnp.where(core_ref[0] == side_index, 0, half) + sum(widths[:q])
        base = pl.multiple_of(base, 128)
        cut = pl.ds(base, widths[q])
        copies.append(pltpu.make_async_copy(enc_ref.at[cut, :], enc_refs[k], sems.at[k, 0]))
        copies.append(pltpu.make_async_copy(dec_ref.at[:, cut], dec_refs[k], sems.at[k, 1]))
    for copy in copies:
        copy.start()
    for copy in copies:
        copy.wait()


def load(core, near, enc_weight, dec_weight, widths):
    width, latents = enc_weight.shape
    both = list(widths) * 2
    out = pl.pallas_call(
        functools.partial(load_kernel, widths),
        out_shape=[jax.ShapeDtypeStruct((w, latents), jnp.bfloat16) for w in both]
        + [jax.ShapeDtypeStruct((latents, w), jnp.bfloat16) for w in both],
        in_specs=[SMEM, ANY, HBM, HBM],
        out_specs=[VMEM] * (2 * len(both)),
        scratch_shapes=[pltpu.SemaphoreType.DMA((len(both), 2))],
        compiler_params=params(SMALL_VMEM),
        cost_estimate=estimate(0, 8 * width * latents),
        name="load",
    )(core, near, enc_weight, dec_weight)
    return out[: len(both)], out[len(both) :]


def pipelined(tasks):
    held = None
    for product, use in tasks:
        result = product()
        if held is not None:
            held[0](held[1])
        held = (use, result)
    held[0](held[1])


def part_tasks(act_ref, dec_ref, part_refs):
    rows = part_refs[0].shape[0]

    def task(cols):
        def product():
            return jnp.dot(act_ref[...], dec_ref[:, cols], preferred_element_type=jnp.float32)

        def use(result):
            result = result.astype(jnp.bfloat16)
            for b, ref in enumerate(part_refs):
                ref[:, cols] = result[b * rows : (b + 1) * rows]

        return product, use

    return [task(slice(at, at + step)) for at, step in chunks(dec_ref.shape[1])]


def front_kernel(count, bias_ref, enc_own, enc_oth, dec_ref, *refs):
    x_own, x_oth = refs[:count], refs[count : 2 * count]
    preact_ref, act_ref = refs[2 * count : 2 * count + 2]
    preact = jnp.dot(stack(x_own), enc_own[...], preferred_element_type=jnp.float32)
    preact = preact + jnp.dot(stack(x_oth), enc_oth[...], preferred_element_type=jnp.float32) + bias_ref[...]
    preact_ref[...] = preact
    act_ref[...] = jnp.maximum(preact, 0.0).astype(jnp.bfloat16)
    pipelined(part_tasks(act_ref, dec_ref, refs[2 * count + 2 :]))


def front(x_own, x_oth, encs, enc_bias, dec):
    count = len(x_own)
    rows, half = x_own[0].shape
    latents = dec.shape[0]
    out = pl.pallas_call(
        functools.partial(front_kernel, count),
        out_shape=[
            jax.ShapeDtypeStruct((count * rows, latents), jnp.float32),
            jax.ShapeDtypeStruct((count * rows, latents), jnp.bfloat16),
        ]
        + [jax.ShapeDtypeStruct((rows, half), jnp.bfloat16)] * count,
        in_specs=[VMEM] * (4 + 2 * count),
        out_specs=[VMEM] * (2 + count),
        compiler_params=params(SMALL_VMEM),
        cost_estimate=estimate(6 * count * rows * latents * half, 8 * latents * half),
        name="front",
    )(enc_bias[None], *encs, dec, *x_own, *x_oth)
    return out[0], out[1], out[2:]


def parts_kernel(act_ref, dec_ref, *part_refs):
    pipelined(part_tasks(act_ref, dec_ref, part_refs))


def parts(act, dec, count):
    total_rows, latents = act.shape
    wide = dec.shape[1]
    return pl.pallas_call(
        parts_kernel,
        out_shape=[jax.ShapeDtypeStruct((total_rows // count, wide), jnp.bfloat16)] * count,
        in_specs=[VMEM] * 2,
        out_specs=[VMEM] * count,
        compiler_params=params(SMALL_VMEM),
        cost_estimate=estimate(2 * total_rows * latents * wide, 4 * latents * wide),
        name="parts",
    )(act, dec)


def side_kernel(row_scale, rows_dev, groups, order_ref, *refs):
    acts, decs, (left_ref, scale_ref, norm_ref) = refs[:groups], refs[groups:-3], refs[-3:]
    act = stack(acts)
    total_rows, latents = act.shape
    left_ref[:latents] = act.T
    spot = lax.broadcasted_iota(jnp.int32, (16, total_rows), 0)
    target = jnp.full((16, total_rows), -1, jnp.int32)
    z = lax.axis_index("z")
    x = lax.axis_index("xh") * 2 + lax.axis_index("xl")
    y = lax.axis_index("y")
    first = (((z * 4 + x) * 4 + y) * 2 + lax.axis_index("c")) * rows_dev
    chip_rows = 2 * rows_dev
    for r in range(rows_dev):
        wanted = order_ref[first + r]
        chip = wanted // chip_rows
        tz, tx, ty = chip // 16, chip // 4 % 4, chip % 4
        kind = (tx + tz + x + z) % 2 + 2 * ((ty + tz + y + z) % 2)
        place = (kind * 16 + tz * 4 + tx // 2 * 2 + ty // 2) * chip_rows + wanted % chip_rows
        target = jnp.where(spot == r, place, target)
    chosen = lax.broadcasted_iota(jnp.int32, (16, total_rows), 1) == target
    left_ref[latents:] = jnp.where(chosen, 1.0, 0.0).astype(jnp.bfloat16)
    total = jnp.sum(act.astype(jnp.float32), axis=0, keepdims=True) / row_scale
    total = jnp.broadcast_to(total, (128, latents)).T[:, :1]
    squares = jnp.zeros((latents, 128), jnp.float32)
    for dec in decs:
        for c in range(dec.shape[1] // 128):
            wide = dec[:, c * 128 : (c + 1) * 128].astype(jnp.float32)
            squares = squares + wide * wide
    norms = jnp.sqrt(jnp.sum(squares, axis=1, keepdims=True) + 1e-06)
    scale_ref[...] = total / norms
    norm_ref[...] = jnp.broadcast_to(norms / row_scale, (latents, 128)).T[:1]


def side(order, acts, decs, row_scale, rows_dev):
    total_rows, latents = sum(act.shape[0] for act in acts), acts[0].shape[1]
    width = sum(dec.shape[1] for dec in decs)
    return pl.pallas_call(
        functools.partial(side_kernel, row_scale, rows_dev, len(acts)),
        out_shape=(
            jax.ShapeDtypeStruct((latents + 16, total_rows), jnp.bfloat16),
            jax.ShapeDtypeStruct((latents, 1), jnp.float32),
            jax.ShapeDtypeStruct((1, latents), jnp.float32),
        ),
        in_specs=[SMEM] + [VMEM] * (len(acts) + len(decs)),
        out_specs=(VMEM, VMEM, VMEM),
        compiler_params=params(SMALL_VMEM),
        cost_estimate=estimate(4 * latents * width, 2 * latents * width),
        name="side",
    )(order, *acts, *decs)


def decoder_tasks(base, row_scale, left_ref, scale_ref, dec_ref, err, dec_out, dec_grad_ref, recon_ref, sems, outs):
    latents, wide = dec_ref.shape

    def task(spot, at, step):
        cols = slice(at, at + step)

        def product():
            return jnp.dot(left_ref[...], err[:, cols], preferred_element_type=jnp.float32)

        def use(both):
            grad = both[:latents] + scale_ref[...] * dec_ref[:, cols].astype(jnp.float32)
            dec_out[:, cols] = grad.astype(jnp.bfloat16)
            recon_ref[:, cols] = both[latents : latents + recon_ref.shape[0]] * row_scale
            start = pl.multiple_of(base + at, 128)
            out = pltpu.make_async_copy(dec_out.at[:, cols], dec_grad_ref.at[:, pl.ds(start, step)], sems.at[spot])
            out.start()
            outs.append(out)

        return product, use

    return [task(spot, at, step) for spot, (at, step) in enumerate(chunks(wide))]


def piece_base(core, half, side_index, offset):
    return jnp.where(core == side_index, 0, half) + offset


def grad_kernel(later, side_index, offset, half, row_scale, core_ref, left_ref, scale_ref, dec_ref, *refs):
    blocks, refs = refs[:4], refs[4:]
    before, refs = (refs[0], refs[2:]) if later else (None, refs)
    total_ref, recon_ref, dec_grad_ref, dec_out, sems = refs
    base = piece_base(core_ref[0], half, side_index, offset)
    err = stack(blocks)
    outs = []

    def product():
        return lax.dot_general(err, dec_ref[...], (((1,), (1,)), ((), ())), preferred_element_type=jnp.float32)

    def use(result):
        total_ref[...] = before[...] + result if later else result

    pipelined(
        decoder_tasks(base, row_scale, left_ref, scale_ref, dec_ref, err, dec_out, dec_grad_ref, recon_ref, sems, outs)
        + [(product, use)]
    )
    for out in outs:
        out.wait()


def grad(core, left, scale, dec, blocks, held, side_index, offset, half, row_scale, out_rows):
    rows, wide = blocks[0].shape
    latents = dec.shape[0]
    later = held is not None
    return pl.pallas_call(
        functools.partial(grad_kernel, later, side_index, offset, half, row_scale),
        out_shape=(
            jax.ShapeDtypeStruct((4 * rows, latents), jnp.float32),
            jax.ShapeDtypeStruct((out_rows, wide), jnp.float32),
            jax.ShapeDtypeStruct((latents, 2 * half), jnp.bfloat16),
        ),
        in_specs=[SMEM] + [VMEM] * 7 + ([VMEM, HBM] if later else []),
        out_specs=(VMEM, VMEM, HBM),
        scratch_shapes=[
            pltpu.VMEM((latents, wide), jnp.bfloat16),
            pltpu.SemaphoreType.DMA((len(chunks(wide)),)),
        ],
        input_output_aliases={9: 2} if later else {},
        compiler_params=params(SMALL_VMEM),
        cost_estimate=estimate(16 * rows * latents * wide, 4 * latents * wide),
        name="grad",
    )(core, left, scale, dec, *blocks, *(held if later else ()))


def tail_kernel(widths, row_scale, groups, core_ref, left_ref, scale_ref, norm_ref, total_ref, dec_ref, *refs):
    count = len(widths)
    preacts, refs = refs[:groups], refs[groups:]
    recons, refs = refs[: 2 * count - 1], refs[2 * count - 1 :]
    e_blocks, refs = refs[:4], refs[4:]
    x_blocks, refs = [refs[4 * k : 4 * k + 4] for k in range(2 * count)], refs[8 * count + 1 :]
    dec_grad_ref, enc_grad_ref, bias_ref, recon_ref = refs[:4]
    dec_out, enc_out, recon_last, pre_ref, dec_sems, enc_sems = refs[4:]
    core = core_ref[0]
    half = sum(widths)
    bases = []
    for k in range(2 * count):
        side_index, q = divmod(k, count)
        bases.append(piece_base(core, half, side_index, sum(widths[:q])))
    err = stack(e_blocks)
    outs = []

    def product():
        return lax.dot_general(err, dec_ref[...], (((1,), (1,)), ((), ())), preferred_element_type=jnp.float32)

    def use(result):
        act_grad = total_ref[...] + result + norm_ref[...]
        rounded = jnp.where(stack(preacts) > 0.0, act_grad, 0.0).astype(jnp.bfloat16)
        pre_ref[...] = rounded
        bias_ref[...] = jnp.sum(rounded.astype(jnp.float32), axis=0, keepdims=True)

    def encoder_task(spot, row, k, at, step):
        def product():
            mine = jnp.concatenate([ref[:, at : at + step] for ref in x_blocks[k]], axis=0)
            return lax.dot_general(mine, pre_ref[...], (((0,), (0,)), ((), ())), preferred_element_type=jnp.float32)

        def use(piece):
            enc_out[row : row + step] = piece.astype(jnp.bfloat16)
            start = pl.multiple_of(bases[k] + at, 128)
            out = pltpu.make_async_copy(
                enc_out.at[pl.ds(row, step), :], enc_grad_ref.at[pl.ds(start, step), :], enc_sems.at[spot]
            )
            out.start()
            outs.append(out)

        return product, use

    decoder = decoder_tasks(
        bases[-1], row_scale, left_ref, scale_ref, dec_ref, err, dec_out, dec_grad_ref, recon_last, dec_sems, outs
    )
    encoder = []
    row = 0
    for k in range(2 * count):
        for at, step in chunks(widths[k % count]):
            encoder.append(encoder_task(len(encoder), row, k, at, step))
            row += step
    tasks = [(product, use), decoder.pop(0)]
    for spot, task in enumerate(encoder):
        tasks.append(task)
        if decoder and spot % 2 == 1:
            tasks.append(decoder.pop(0))
    pipelined(tasks)
    for k, held in enumerate(list(recons) + [recon_last]):
        recon_ref[:, pl.ds(pl.multiple_of(bases[k], 128), widths[k % count])] = held[...]
    for out in outs:
        out.wait()


def tail(core, left, preacts, scale, norm, total, dec, recons, e_blocks, x_blocks, dec_grad, row_scale, widths):
    rows = e_blocks[0].shape[0]
    latents = dec.shape[0]
    half = sum(widths)
    out_rows = recons[0].shape[0]
    spots = 2 * sum(len(chunks(w)) for w in widths)
    vmem_args = [left, scale, norm, total, dec, *preacts, *recons, *e_blocks, *[b for blocks in x_blocks for b in blocks]]
    return pl.pallas_call(
        functools.partial(tail_kernel, widths, row_scale, len(preacts)),
        out_shape=(
            jax.ShapeDtypeStruct((latents, 2 * half), jnp.bfloat16),
            jax.ShapeDtypeStruct((2 * half, latents), jnp.bfloat16),
            jax.ShapeDtypeStruct((1, latents), jnp.float32),
            jax.ShapeDtypeStruct((out_rows, 2 * half), jnp.float32),
        ),
        in_specs=[SMEM] + [VMEM] * len(vmem_args) + [HBM],
        out_specs=(HBM, HBM, VMEM, VMEM),
        scratch_shapes=[
            pltpu.VMEM((latents, widths[-1]), jnp.bfloat16),
            pltpu.VMEM((2 * half, latents), jnp.bfloat16),
            pltpu.VMEM((out_rows, widths[-1]), jnp.float32),
            pltpu.VMEM((4 * rows, latents), jnp.bfloat16),
            pltpu.SemaphoreType.DMA((len(chunks(widths[-1])),)),
            pltpu.SemaphoreType.DMA((spots,)),
        ],
        input_output_aliases={1 + len(vmem_args): 0},
        compiler_params=params(TAIL_VMEM),
        cost_estimate=estimate(24 * rows * latents * half, 8 * latents * half),
        name="tail",
    )(core, *vmem_args, dec_grad)


def per_device(tokens, batch_order, enc_weight, enc_bias, dec_weight):
    rows_dev, width = tokens.shape
    total_rows = batch_order.shape[0]
    row_scale = math.sqrt(total_rows)
    half = width // 2
    widths = (half,)
    block_rows = total_rows // 4
    core = lax.axis_index("c")
    core_arg = core[None].astype(jnp.int32)

    got = swap_cores(tokens)
    low = jnp.concatenate([tokens[:, :half], got[:, :half]])
    high = jnp.concatenate([got[:, half:], tokens[:, half:]])
    block = jnp.where(core == 0, low, high)
    near = near_copies(block)
    x_own = spread(near)
    encs, decs = load(core_arg, near, enc_weight, dec_weight, widths)
    done = []

    def work(group):
        oth = [swap_cores(x_own[k]) for k in group]
        pre_part, act, sibling = front([x_own[k] for k in group], oth, encs, enc_bias, decs[1])
        own = parts(act, decs[0], len(group))
        done.append((oth, pre_part, act, sibling, own))

    work(GROUPS[0])
    x_own[1:], encs, decs, done[0] = lax.optimization_barrier((x_own[1:], encs, decs, done[0]))
    for group in GROUPS[1:]:
        work(group)
    preacts, acts = [item[1] for item in done], [item[2] for item in done]
    x_oth, parts_oth, parts_own = [[a for item in done for a in item[k]] for k in (0, 3, 4)]
    got = [swap_cores(part) for part in parts_oth]
    total = parts_own[0].astype(jnp.float32) + got[0].astype(jnp.float32)
    for k in range(1, 4):
        sent = (parts_own[k].astype(jnp.float32) + got[k].astype(jnp.float32)).astype(jnp.bfloat16)
        total = total + lax.ppermute(sent, NAMES, SHIFTS[k - 1]).astype(jnp.float32)
    left, scale, norm = side(batch_order, acts, decs, row_scale, rows_dev)
    total = total.astype(jnp.bfloat16).reshape(16, block_rows // 16, half)
    total, left, scale, norm = lax.optimization_barrier((total, left, scale, norm))
    pieces = lax.all_to_all(total, CHIPS, 0, 0, axis_index_groups=CLASSES)
    recon = jnp.sum(pieces.astype(jnp.float32), axis=0) - block.astype(jnp.float32)
    err_block = (recon / row_scale).astype(jnp.bfloat16)
    near = near_copies(err_block)
    e_own = spread(near)
    e_oth = [swap_cores(a) for a in e_own]
    act_part, recon_own, dec_grad = grad(core_arg, left, scale, decs[0], e_own, None, 0, 0, half, row_scale, rows_dev)
    dec_grad, enc_grad, bias_grad, recon_error = tail(
        core_arg, left, preacts, scale, norm, act_part, decs[1], [recon_own], e_oth, [x_own, x_oth], dec_grad, row_scale,
        widths,
    )
    return (recon_error, enc_grad, dec_grad, bias_grad[0])


def solution(mesh):
    split = Mesh(mesh.devices.reshape(4, 2, 2, 4, 2), NAMES)
    return jax.shard_map(
        per_device,
        mesh=split,
        in_specs=(P(NAMES, None), P(), P(None, NAMES), P(NAMES), P(NAMES, None)),
        out_specs=(P(NAMES, None), P(None, NAMES), P(NAMES, None), P(NAMES)),
        check_vma=False,
    )
```

time: 177 us -> 123 us (0.69)
  blocking collectives: 118 us -> 54.3 us
  matrix products: 27.5 us -> 0 us
  starting transfers between devices: 6.16 us -> 32.9 us
  Pallas kernels: 0 us -> 19.8 us
  other arithmetic: 10.2 us -> 0.96 us
    all_to_all x3, blocking collectives: 118 us -> 54.3 us  [the longest x2 39.3 us: near_copies(): near = lax.all_to_all(copies, CHIPS, 0, 0, axis_index_groups=CLASSES)]
    dot_general x6 -> x0, matrix products: 27.5 us -> none  [the longest x1 7.37 us: per_device(): lax.dot_general(err, dec_weight, (((1,), (1,)), ((), ())), preferred_elem...]
    ppermute x4 -> x22, starting transfers between devices: 6.16 us -> 32.9 us  [the longest x13 22 us: swap_cores(): return lax.ppermute(a, 'c', SWAP)]
    pallas_call x0 -> x12, Pallas kernels: none -> 19.8 us  [the longest x1 7.07 us: tail(): pl.pallas_call(functools.partial(tail_kernel, widths, row_scale, len(prea...]
    select_n x2 -> x1, other arithmetic: 5 us -> 0.04 us  [per_device(): block = jnp.where(core == 0, low, high)]
    unnamed x20 -> x8, local copies, waits for them, and re-layouts: 0.04 us -> 4.68 us
    gather x1 -> x0, local copies, waits for them, and re-layouts: 3.63 us -> none  [per_device(): recon_error = jnp.take(err, wanted, axis=0).astype(jnp.float32) * row_scale]
    reduce_sum x1 -> x0, other arithmetic: 3.34 us -> none  [per_device(): row_norms = jnp.sqrt(jnp.sum(dec_wide * dec_wide, axis=1) + 1e-06)]
  transfers between devices with their start and end apart: 4 -> 22, of which waited for: 4 -> 7; matrix products, arithmetic and copies ran while one was open for 2% -> 1% of each run, Pallas kernels for 0% -> 10%
where the time goes in v4:
time: 123 us
  blocking collectives  54.3 us (44%)
  starting transfers between devices  32.9 us (27%)
  Pallas kernels  19.8 us (16%)
  waiting for transfers between devices  8.35 us (7%)
  local copies, waits for them, and re-layouts  5.53 us (4%)
    all_to_all x2, blocking collectives, near_copies(): near = lax.all_to_all(copies, CHIPS, 0, 0, axis_index_groups=CLASSES)  39.3 us
    ppermute x13, starting transfers between devices, swap_cores(): return lax.ppermute(a, 'c', SWAP)  22 us
    all_to_all x1, blocking collectives, per_device(): pieces = lax.all_to_all(total, CHIPS, 0, 0, axis_index_groups=CLASSES)  15 us
    pallas_call x1, Pallas kernels, tail(): pl.pallas_call(functools.partial(tail_kernel, widths, row_scale, len(prea...  7.07 us
    ppermute x3, waiting for transfers between devices, per_device(): total = total + lax.ppermute(sent, NAMES, SHIFTS[k - 1]).astype(jnp.float32)  6.48 us
    ppermute x3, starting transfers between devices, per_device(): total = total + lax.ppermute(sent, NAMES, SHIFTS[k - 1]).astype(jnp.float32)  5.91 us
    ppermute x6, starting transfers between devices, spread(): return [near] + [lax.ppermute(near, NAMES, pairs) for pairs in SHIFTS]  4.98 us
    pallas_call x4, Pallas kernels, front(): pl.pallas_call(functools.partial(front_kernel, count), out_shape=[jax.Sha...  4.92 us
  transfers between devices with their start and end apart: 22, of which 7 were waited for; matrix products, arithmetic and copies ran while one was open for 1% of the time, Pallas kernels for 10%

profile of v4, /device:TPU:1, one launch (start us, length us, event | category | flops | bytes accessed | tf_op | source)
XLA Modules:
  0.0 123.0 jit_solution(6775873833846553444)
XLA Ops:
  0.6 1.5 %collective-permute-start = (bf16[4,4608]{1,0:T(4,128)(2,1)}, bf16[4,4608]{1,0:T(4,128)(2,1)S(1)}, u32[]{:S(2)}, u32[]{:S(2)}) collective-permute-start(bf16[4,4608]{1,0:T(4,128)(2,1)} %param.5), channel_id=1, source_target_pairs={{0,1},{1,0},{2,3},{3,2},{4,5},{5,4},{6,7},{7,6},{8,9},{9,8},{10,11... | collective-permute-start | bytes 110600 | tf_op jit(solution)/shard_map/ppermute | solution.py:66
  2.1 0.8 fusion.2
  2.9 0.3 collective-permute-done
  3.3 24.1 %all_to_all.15 = bf16[16,8,2304]{2,1,0:T(8,128)(2,1)S(1)} all-to-all(bf16[16,8,2304]{2,1,0:T(8,128)(2,1)S(1)} %broadcast_in_dim.9), channel_id=1, replica_groups={{0,4,16,20,42,46,58,62,64,68,80,84,106,110,122,126},{8,12,24,28,34,38,5..., dimensions={0} | all-to-all | bytes 1179648 | tf_op jit(solution)/shard_map/all_to_all | solution.py:57
  27.4 1.6 %collective-permute-start.4 = (bf16[128,2304]{1,0:T(8,128)(2,1)S(1)}, bf16[128,2304]{1,0:T(8,128)(2,1)S(1)}, u32[]{:S(2)}, u32[]{:S(2)}) collective-permute-start(bf16[128,2304]{1,0:T(8,128)(2,1)S(1)} %bitcast.7), channel_id=1, source_target_pairs={{0,1},{1,0},{2,3},{3,2},{4,5},{5,4},{6,7},{7,6},{8,9},{9,8},{10,11... | collective-permute-start | bytes 1769480 | tf_op jit(solution)/shard_map/ppermute | solution.py:66
  29.0 0.9 collective-permute-start.2
  29.9 1.8 %collective-permute-start.1 = (bf16[128,2304]{1,0:T(8,128)(2,1)S(1)}, bf16[128,2304]{1,0:T(8,128)(2,1)S(1)}, u32[]{:S(2)}, u32[]{:S(2)}) collective-permute-start(bf16[128,2304]{1,0:T(8,128)(2,1)S(1)} %bitcast.10), channel_id=1, source_target_pairs={{0,8},{1,25},{2,10},{3,27},{4,12},{5,29},{6,14},{7,31},{8,16},{9,1... | collective-permute-start | bytes 1769480 | tf_op jit(solution)/shard_map/ppermute | solution.py:62
  31.7 2.3 %copy-done = bf16[4608,512]{1,0:T(8,128)(2,1)S(1)} copy-done((bf16[4608,512]{1,0:T(8,128)(2,1)S(1)}, bf16[4608,512]{1,0:T(8,128)(2,1)}, u32[]{:S(2)}) %copy-start) | copy-done | bytes 4718616
  34.0 2.3 %copy-done.1 = bf16[512,4608]{1,0:T(8,128)(2,1)S(1)} copy-done((bf16[512,4608]{1,0:T(8,128)(2,1)S(1)}, bf16[512,4608]{1,0:T(8,128)(2,1)}, u32[]{:S(2)}) %copy-start.1) | copy-done | bytes 4718616
  36.4 0.7 load.1
  37.1 1.2 %front.4 = (f32[128,512]{1,0:T(8,128)S(1)}, bf16[128,512]{1,0:T(8,128)(2,1)S(1)}, bf16[128,2304]{1,0:T(8,128)(2,1)S(1)}) custom-call(f32[1,512]{1,0:T(1,128)S(1)} %bitcast.19, bf16[2304,512]{1,0:T(8,128)(2,1)S(1)} %get-tuple-element.55.enc_own, bf16[2304,512]{1,0:T(8,128)(2,1)S(1)} %get-tuple-element.56.enc_oth, ...), custom_call_target="tpu_custom_call" | custom-call | flops 905969664 | bytes 9437184 | tf_op jit(solution)/shard_map/front/pallas_call | solution.py:168
  38.3 0.5 parts.4
  38.8 0.1 collective-permute-done.1.refs_0_.refs_10_
  39.0 1.8 %collective-permute-start.12 = (bf16[128,2304]{1,0:T(8,128)(2,1)S(1)}, bf16[128,2304]{1,0:T(8,128)(2,1)S(1)}, u32[]{:S(2)}, u32[]{:S(2)}) collective-permute-start(bf16[128,2304]{1,0:T(8,128)(2,1)S(1)} %collective-permute-done.3.refs_0_.refs_12_), channel_id=1, source_target_pairs={{0,1},{1,0},{2,3},{3,2},{4,5},{5,4},{6,7},{7,6},{8,9},{9,8},{10,11... | collective-permute-start | bytes 1769480 | tf_op jit(solution)/shard_map/ppermute | solution.py:66
  40.8 0.5 collective-permute-start.6
  41.3 1.1 collective-permute-done.12.refs_1_.refs_16_
  42.4 1.2 front.7
  43.7 0.5 collective-permute-start.13
  44.1 0.1 collective-permute-start.5
  44.3 1.2 front.6
  45.5 0.5 collective-permute-start.10
  46.0 1.2 front.5
  47.2 0.2 collective-permute-start.7
  47.4 0.5 parts.7
  47.9 0.5 parts.6
  48.4 0.5 parts.5
  48.9 0.1 add_convert_fusion.1
  49.0 3.0 %collective-permute-start.14 = (bf16[128,2304]{1,0:T(8,128)(2,1)S(1)}, bf16[128,2304]{1,0:T(8,128)(2,1)S(1)}, u32[]{:S(2)}, u32[]{:S(2)}) collective-permute-start(bf16[128,2304]{1,0:T(8,128)(2,1)S(1)} %add_convert_fusion.1), channel_id=1, source_target_pairs={{0,32},{1,97},{2,34},{3,99},{4,36},{5,101},{6,38},{7,103},{8,40},{... | collective-permute-start | bytes 1769480 | tf_op jit(solution)/shard_map/ppermute | solution.py:456
  52.1 0.1 add_convert_fusion.2
  52.2 2.4 %collective-permute-start.11 = (bf16[128,2304]{1,0:T(8,128)(2,1)S(1)}, bf16[128,2304]{1,0:T(8,128)(2,1)S(1)}, u32[]{:S(2)}, u32[]{:S(2)}) collective-permute-start(bf16[128,2304]{1,0:T(8,128)(2,1)S(1)} %add_convert_fusion.2), channel_id=1, source_target_pairs={{0,2},{1,7},{2,4},{3,1},{4,6},{5,3},{6,0},{7,5},{8,10},{9,15},{10,... | collective-permute-start | bytes 1769480 | tf_op jit(solution)/shard_map/ppermute | solution.py:456
  54.6 0.1 add_convert_fusion.3
  54.7 0.5 collective-permute-start.8
  55.2 1.9 %side.1 = (bf16[528,512]{1,0:T(8,128)(2,1)S(1)}, f32[512,1]{1,0:T(8,128)S(1)}, f32[1,512]{1,0:T(1,128)S(1)}) custom-call(s32[512]{0:T(512)S(1)} %copy-done.3, bf16[128,512]{1,0:T(8,128)(2,1)S(1)} %get-tuple-element.68.act_ref.refs_0_, bf16[128,512]{1,0:T(8,128)(2,1)S(1)} %get-tuple-element.59.act_ref.refs_1_, ...), custom_call_target="tpu_custom_call" | custom-call | flops 9437184 | bytes 4718592 | tf_op jit(solution)/shard_map/side/pallas_call | solution.py:238
  57.2 1.7 %collective-permute-done.14 = bf16[128,2304]{1,0:T(8,128)(2,1)S(1)} collective-permute-done((bf16[128,2304]{1,0:T(8,128)(2,1)S(1)}, bf16[128,2304]{1,0:T(8,128)(2,1)S(1)}, u32[]{:S(2)}, u32[]{:S(2)}) %collective-permute-start.14) | collective-permute-done | bytes 589856 | tf_op jit(solution)/shard_map/ppermute | solution.py:456
  58.9 2.5 %collective-permute-done.11 = bf16[128,2304]{1,0:T(8,128)(2,1)S(1)} collective-permute-done((bf16[128,2304]{1,0:T(8,128)(2,1)S(1)}, bf16[128,2304]{1,0:T(8,128)(2,1)S(1)}, u32[]{:S(2)}, u32[]{:S(2)}) %collective-permute-start.11) | collective-permute-done | bytes 589856 | tf_op jit(solution)/shard_map/ppermute | solution.py:456
  61.4 2.3 %collective-permute-done.8 = bf16[128,2304]{1,0:T(8,128)(2,1)S(1)} collective-permute-done((bf16[128,2304]{1,0:T(8,128)(2,1)S(1)}, bf16[128,2304]{1,0:T(8,128)(2,1)S(1)}, u32[]{:S(2)}, u32[]{:S(2)}) %collective-permute-start.8) | collective-permute-done | bytes 589856 | tf_op jit(solution)/shard_map/ppermute | solution.py:456
  63.7 0.4 fusion
  64.1 15.0 %all_to_all.16 = bf16[16,8,2304]{2,1,0:T(8,128)(2,1)S(1)} all-to-all(bf16[16,8,2304]{2,1,0:T(8,128)(2,1)S(1)} %fusion), channel_id=1, replica_groups={{0,4,16,20,42,46,58,62,64,68,80,84,106,110,122,126},{8,12,24,28,34,38,5..., dimensions={0} | all-to-all | bytes 1179648 | tf_op jit(solution)/shard_map/all_to_all | solution.py:460
  79.1 0.1 convert_reduce_fusion
  79.3 15.2 %all_to_all.17 = bf16[16,8,2304]{2,1,0:T(8,128)(2,1)S(1)} all-to-all(bf16[16,8,2304]{2,1,0:T(8,128)(2,1)S(1)} %broadcast_in_dim.11), channel_id=1, replica_groups={{0,4,16,20,42,46,58,62,64,68,80,84,106,110,122,126},{8,12,24,28,34,38,5..., dimensions={0} | all-to-all | bytes 1179648 | tf_op jit(solution)/shard_map/all_to_all | solution.py:57
  94.5 1.6 %collective-permute-start.16 = (bf16[128,2304]{1,0:T(8,128)(2,1)S(1)}, bf16[128,2304]{1,0:T(8,128)(2,1)S(1)}, u32[]{:S(2)}, u32[]{:S(2)}) collective-permute-start(bf16[128,2304]{1,0:T(8,128)(2,1)S(1)} %bitcast.15), channel_id=1, source_target_pairs={{0,2},{1,7},{2,4},{3,1},{4,6},{5,3},{6,0},{7,5},{8,10},{9,15},{10,... | collective-permute-start | bytes 1769480 | tf_op jit(solution)/shard_map/ppermute | solution.py:62
  96.1 0.7 collective-permute-start.15
  96.8 6.2 %collective-permute-start.18 = (bf16[128,2304]{1,0:T(8,128)(2,1)S(1)}, bf16[128,2304]{1,0:T(8,128)(2,1)S(1)}, u32[]{:S(2)}, u32[]{:S(2)}) collective-permute-start(bf16[128,2304]{1,0:T(8,128)(2,1)S(1)} %bitcast.17), channel_id=1, source_target_pairs={{0,1},{1,0},{2,3},{3,2},{4,5},{5,4},{6,7},{7,6},{8,9},{9,8},{10,11... | collective-permute-start | bytes 1769480 | tf_op jit(solution)/shard_map/ppermute | solution.py:66
  103.0 0.3 collective-permute-done.17.refs_3_
  103.3 8.6 %collective-permute-start.21 = (bf16[128,2304]{1,0:T(8,128)(2,1)S(1)}, bf16[128,2304]{1,0:T(8,128)(2,1)S(1)}, u32[]{:S(2)}, u32[]{:S(2)}) collective-permute-start(bf16[128,2304]{1,0:T(8,128)(2,1)S(1)} %collective-permute-done.17.refs_3_), channel_id=1, source_target_pairs={{0,1},{1,0},{2,3},{3,2},{4,5},{5,4},{6,7},{7,6},{8,9},{9,8},{10,11... | collective-permute-start | bytes 1769480 | tf_op jit(solution)/shard_map/ppermute | solution.py:66
  111.9 0.5 collective-permute-start.19
  112.4 3.3 %grad.1 = (f32[512,512]{1,0:T(8,128)S(1)}, f32[4,2304]{1,0:T(4,128)S(1)}, bf16[512,4608]{1,0:T(8,128)(2,1)}) custom-call(s32[1]{0:T(128)} %bitcast.core_ref, bf16[528,512]{1,0:T(8,128)(2,1)S(1)} %get-tuple-element.72.left_ref, f32[512,1]{1,0:T(8,128)S(1)} %get-tuple-element.73.scale_ref, bf16[512,2304]{1,0:T(8,128)(2,1)S(1)} %get-tuple-element.60.dec_ref.refs_4_, ...), custom_call_target="tpu_custom_call" | custom-call | flops 2415919104 | bytes 4718592 | tf_op jit(solution)/shard_map/grad/pallas_call | solution.py:306
  115.7 7.1 %tail.1 = (bf16[512,4608]{1,0:T(8,128)(2,1)}, bf16[4608,512]{1,0:T(8,128)(2,1)}, f32[1,512]{1,0:T(1,128)}, f32[4,4608]{1,0:T(4,128)}) custom-call(s32[1]{0:T(128)} %bitcast.core_ref, bf16[528,512]{1,0:T(8,128)(2,1)S(1)} %get-tuple-element.72.left_ref, f32[512,1]{1,0:T(8,128)S(1)} %get-tuple-element.73.scale_ref, ...), custom_call_target="tpu_custom_call", output_to_operand_aliasing={{0}: (23, {})} | custom-call | flops 3623878656 | bytes 9437184 | tf_op jit(solution)/shard_map/tail/pallas_call | solution.py:396
  (30 shorter events, 0.2 us)
Async XLA Ops:
  0.6 2.6 %collective-permute-start = (bf16[4,4608]{1,0:T(4,128)(2,1)}, bf16[4,4608]{1,0:T(4,128)(2,1)S(1)}, u32[]{:S(2)}, u32[]{:S(2)}) collective-permute-start(bf16[4,4608]{1,0:T(4,128)(2,1)} %param.5), channel_id=1, source_target_pairs={{0,1},{1,0},{2,3},{3,2},{4,5},{5,4},{6,7},{7,6},{8,9},{9,8},{10,11... | collective-permute-start | bytes 110600 | tf_op jit(solution)/shard_map/ppermute | solution.py:66
  27.4 9.6 %collective-permute-start.4 = (bf16[128,2304]{1,0:T(8,128)(2,1)S(1)}, bf16[128,2304]{1,0:T(8,128)(2,1)S(1)}, u32[]{:S(2)}, u32[]{:S(2)}) collective-permute-start(bf16[128,2304]{1,0:T(8,128)(2,1)S(1)} %bitcast.7), channel_id=1, source_target_pairs={{0,1},{1,0},{2,3},{3,2},{4,5},{5,4},{6,7},{7,6},{8,9},{9,8},{10,11... | collective-permute-start | bytes 1769480 | tf_op jit(solution)/shard_map/ppermute | solution.py:66
  29.0 9.8 %collective-permute-start.3 = (bf16[128,2304]{1,0:T(8,128)(2,1)S(1)}, bf16[128,2304]{1,0:T(8,128)(2,1)S(1)}, u32[]{:S(2)}, u32[]{:S(2)}) collective-permute-start(bf16[128,2304]{1,0:T(8,128)(2,1)S(1)} %bitcast.8), channel_id=1, source_target_pairs={{0,32},{1,97},{2,34},{3,99},{4,36},{5,101},{6,38},{7,103},{8,40},{... | collective-permute-start | bytes 1769480 | tf_op jit(solution)/shard_map/ppermute | solution.py:62
  29.0 9.8 %collective-permute-start.2 = (bf16[128,2304]{1,0:T(8,128)(2,1)S(1)}, bf16[128,2304]{1,0:T(8,128)(2,1)S(1)}, u32[]{:S(2)}, u32[]{:S(2)}) collective-permute-start(bf16[128,2304]{1,0:T(8,128)(2,1)S(1)} %bitcast.9), channel_id=1, source_target_pairs={{0,2},{1,7},{2,4},{3,1},{4,6},{5,3},{6,0},{7,5},{8,10},{9,15},{10,... | collective-permute-start | bytes 1769480 | tf_op jit(solution)/shard_map/ppermute | solution.py:62
  29.9 9.0 %collective-permute-start.1 = (bf16[128,2304]{1,0:T(8,128)(2,1)S(1)}, bf16[128,2304]{1,0:T(8,128)(2,1)S(1)}, u32[]{:S(2)}, u32[]{:S(2)}) collective-permute-start(bf16[128,2304]{1,0:T(8,128)(2,1)S(1)} %bitcast.10), channel_id=1, source_target_pairs={{0,8},{1,25},{2,10},{3,27},{4,12},{5,29},{6,14},{7,31},{8,16},{9,1... | collective-permute-start | bytes 1769480 | tf_op jit(solution)/shard_map/ppermute | solution.py:62
  31.7 2.3 %copy-start = (bf16[4608,512]{1,0:T(8,128)(2,1)S(1)}, bf16[4608,512]{1,0:T(8,128)(2,1)}, u32[]{:S(2)}) copy-start(bf16[4608,512]{1,0:T(8,128)(2,1)} %enc_ref.1) | copy-start | bytes 14155780
  34.0 2.3 %copy-start.1 = (bf16[512,4608]{1,0:T(8,128)(2,1)S(1)}, bf16[512,4608]{1,0:T(8,128)(2,1)}, u32[]{:S(2)}) copy-start(bf16[512,4608]{1,0:T(8,128)(2,1)} %dec_ref.1) | copy-start | bytes 14155780
  36.4 0.7 copy-start.2
  39.0 3.5 %collective-permute-start.12 = (bf16[128,2304]{1,0:T(8,128)(2,1)S(1)}, bf16[128,2304]{1,0:T(8,128)(2,1)S(1)}, u32[]{:S(2)}, u32[]{:S(2)}) collective-permute-start(bf16[128,2304]{1,0:T(8,128)(2,1)S(1)} %collective-permute-done.3.refs_0_.refs_12_), channel_id=1, source_target_pairs={{0,1},{1,0},{2,3},{3,2},{4,5},{5,4},{6,7},{7,6},{8,9},{9,8},{10,11... | collective-permute-start | bytes 1769480 | tf_op jit(solution)/shard_map/ppermute | solution.py:66
  40.8 3.5 %collective-permute-start.9 = (bf16[128,2304]{1,0:T(8,128)(2,1)S(1)}, bf16[128,2304]{1,0:T(8,128)(2,1)S(1)}, u32[]{:S(2)}, u32[]{:S(2)}) collective-permute-start(bf16[128,2304]{1,0:T(8,128)(2,1)S(1)} %collective-permute-done.2.refs_0_.refs_11_), channel_id=1, source_target_pairs={{0,1},{1,0},{2,3},{3,2},{4,5},{5,4},{6,7},{7,6},{8,9},{9,8},{10,11... | collective-permute-start | bytes 1769480 | tf_op jit(solution)/shard_map/ppermute | solution.py:66
  40.8 5.1 %collective-permute-start.6 = (bf16[128,2304]{1,0:T(8,128)(2,1)S(1)}, bf16[128,2304]{1,0:T(8,128)(2,1)S(1)}, u32[]{:S(2)}, u32[]{:S(2)}) collective-permute-start(bf16[128,2304]{1,0:T(8,128)(2,1)S(1)} %collective-permute-done.1.refs_0_.refs_10_), channel_id=1, source_target_pairs={{0,1},{1,0},{2,3},{3,2},{4,5},{5,4},{6,7},{7,6},{8,9},{9,8},{10,11... | collective-permute-start | bytes 1769480 | tf_op jit(solution)/shard_map/ppermute | solution.py:66
  43.7 5.2 %collective-permute-start.13 = (bf16[128,2304]{1,0:T(8,128)(2,1)S(1)}, bf16[128,2304]{1,0:T(8,128)(2,1)S(1)}, u32[]{:S(2)}, u32[]{:S(2)}) collective-permute-start(bf16[128,2304]{1,0:T(8,128)(2,1)S(1)} %get-tuple-element.67), channel_id=1, source_target_pairs={{0,1},{1,0},{2,3},{3,2},{4,5},{5,4},{6,7},{7,6},{8,9},{9,8},{10,11... | collective-permute-start | bytes 1769480 | tf_op jit(solution)/shard_map/ppermute | solution.py:66
  44.1 13.1 %collective-permute-start.5 = (bf16[128,2304]{1,0:T(8,128)(2,1)S(1)}, bf16[128,2304]{1,0:T(8,128)(2,1)S(1)}, u32[]{:S(2)}, u32[]{:S(2)}) collective-permute-start(bf16[128,2304]{1,0:T(8,128)(2,1)S(1)} %get-tuple-element.54), channel_id=1, source_target_pairs={{0,1},{1,0},{2,3},{3,2},{4,5},{5,4},{6,7},{7,6},{8,9},{9,8},{10,11... | collective-permute-start | bytes 1769480 | tf_op jit(solution)/shard_map/ppermute | solution.py:66
  45.5 6.6 %collective-permute-start.10 = (bf16[128,2304]{1,0:T(8,128)(2,1)S(1)}, bf16[128,2304]{1,0:T(8,128)(2,1)S(1)}, u32[]{:S(2)}, u32[]{:S(2)}) collective-permute-start(bf16[128,2304]{1,0:T(8,128)(2,1)S(1)} %get-tuple-element.64), channel_id=1, source_target_pairs={{0,1},{1,0},{2,3},{3,2},{4,5},{5,4},{6,7},{7,6},{8,9},{9,8},{10,11... | collective-permute-start | bytes 1769480 | tf_op jit(solution)/shard_map/ppermute | solution.py:66
  47.2 7.4 %collective-permute-start.7 = (bf16[128,2304]{1,0:T(8,128)(2,1)S(1)}, bf16[128,2304]{1,0:T(8,128)(2,1)S(1)}, u32[]{:S(2)}, u32[]{:S(2)}) collective-permute-start(bf16[128,2304]{1,0:T(8,128)(2,1)S(1)} %get-tuple-element.61), channel_id=1, source_target_pairs={{0,1},{1,0},{2,3},{3,2},{4,5},{5,4},{6,7},{7,6},{8,9},{9,8},{10,11... | collective-permute-start | bytes 1769480 | tf_op jit(solution)/shard_map/ppermute | solution.py:66
  49.0 9.9 %collective-permute-start.14 = (bf16[128,2304]{1,0:T(8,128)(2,1)S(1)}, bf16[128,2304]{1,0:T(8,128)(2,1)S(1)}, u32[]{:S(2)}, u32[]{:S(2)}) collective-permute-start(bf16[128,2304]{1,0:T(8,128)(2,1)S(1)} %add_convert_fusion.1), channel_id=1, source_target_pairs={{0,32},{1,97},{2,34},{3,99},{4,36},{5,101},{6,38},{7,103},{8,40},{... | collective-permute-start | bytes 1769480 | tf_op jit(solution)/shard_map/ppermute | solution.py:456
  52.2 3.0 %copy-start.3 = (s32[512]{0:T(512)S(1)}, s32[512]{0:T(512)}, u32[]{:S(2)}) copy-start(s32[512]{0:T(512)} %order_ref.1) | copy-start | bytes 6148
  52.2 9.2 %collective-permute-start.11 = (bf16[128,2304]{1,0:T(8,128)(2,1)S(1)}, bf16[128,2304]{1,0:T(8,128)(2,1)S(1)}, u32[]{:S(2)}, u32[]{:S(2)}) collective-permute-start(bf16[128,2304]{1,0:T(8,128)(2,1)S(1)} %add_convert_fusion.2), channel_id=1, source_target_pairs={{0,2},{1,7},{2,4},{3,1},{4,6},{5,3},{6,0},{7,5},{8,10},{9,15},{10,... | collective-permute-start | bytes 1769480 | tf_op jit(solution)/shard_map/ppermute | solution.py:456
  54.7 9.0 %collective-permute-start.8 = (bf16[128,2304]{1,0:T(8,128)(2,1)S(1)}, bf16[128,2304]{1,0:T(8,128)(2,1)S(1)}, u32[]{:S(2)}, u32[]{:S(2)}) collective-permute-start(bf16[128,2304]{1,0:T(8,128)(2,1)S(1)} %add_convert_fusion.3), channel_id=1, source_target_pairs={{0,8},{1,25},{2,10},{3,27},{4,12},{5,29},{6,14},{7,31},{8,16},{9,1... | collective-permute-start | bytes 1769480 | tf_op jit(solution)/shard_map/ppermute | solution.py:456
  94.5 8.8 %collective-permute-start.17 = (bf16[128,2304]{1,0:T(8,128)(2,1)S(1)}, bf16[128,2304]{1,0:T(8,128)(2,1)S(1)}, u32[]{:S(2)}, u32[]{:S(2)}) collective-permute-start(bf16[128,2304]{1,0:T(8,128)(2,1)S(1)} %bitcast.14), channel_id=1, source_target_pairs={{0,32},{1,97},{2,34},{3,99},{4,36},{5,101},{6,38},{7,103},{8,40},{... | collective-permute-start | bytes 1769480 | tf_op jit(solution)/shard_map/ppermute | solution.py:62
  94.5 17.4 %collective-permute-start.16 = (bf16[128,2304]{1,0:T(8,128)(2,1)S(1)}, bf16[128,2304]{1,0:T(8,128)(2,1)S(1)}, u32[]{:S(2)}, u32[]{:S(2)}) collective-permute-start(bf16[128,2304]{1,0:T(8,128)(2,1)S(1)} %bitcast.15), channel_id=1, source_target_pairs={{0,2},{1,7},{2,4},{3,1},{4,6},{5,3},{6,0},{7,5},{8,10},{9,15},{10,... | collective-permute-start | bytes 1769480 | tf_op jit(solution)/shard_map/ppermute | solution.py:62
  96.1 15.8 %collective-permute-start.15 = (bf16[128,2304]{1,0:T(8,128)(2,1)S(1)}, bf16[128,2304]{1,0:T(8,128)(2,1)S(1)}, u32[]{:S(2)}, u32[]{:S(2)}) collective-permute-start(bf16[128,2304]{1,0:T(8,128)(2,1)S(1)} %bitcast.16), channel_id=1, source_target_pairs={{0,8},{1,25},{2,10},{3,27},{4,12},{5,29},{6,14},{7,31},{8,16},{9,1... | collective-permute-start | bytes 1769480 | tf_op jit(solution)/shard_map/ppermute | solution.py:62
  96.8 18.9 %collective-permute-start.18 = (bf16[128,2304]{1,0:T(8,128)(2,1)S(1)}, bf16[128,2304]{1,0:T(8,128)(2,1)S(1)}, u32[]{:S(2)}, u32[]{:S(2)}) collective-permute-start(bf16[128,2304]{1,0:T(8,128)(2,1)S(1)} %bitcast.17), channel_id=1, source_target_pairs={{0,1},{1,0},{2,3},{3,2},{4,5},{5,4},{6,7},{7,6},{8,9},{9,8},{10,11... | collective-permute-start | bytes 1769480 | tf_op jit(solution)/shard_map/ppermute | solution.py:66
  103.3 12.4 %collective-permute-start.21 = (bf16[128,2304]{1,0:T(8,128)(2,1)S(1)}, bf16[128,2304]{1,0:T(8,128)(2,1)S(1)}, u32[]{:S(2)}, u32[]{:S(2)}) collective-permute-start(bf16[128,2304]{1,0:T(8,128)(2,1)S(1)} %collective-permute-done.17.refs_3_), channel_id=1, source_target_pairs={{0,1},{1,0},{2,3},{3,2},{4,5},{5,4},{6,7},{7,6},{8,9},{9,8},{10,11... | collective-permute-start | bytes 1769480 | tf_op jit(solution)/shard_map/ppermute | solution.py:66
  111.8 3.9 %collective-permute-start.20 = (bf16[128,2304]{1,0:T(8,128)(2,1)S(1)}, bf16[128,2304]{1,0:T(8,128)(2,1)S(1)}, u32[]{:S(2)}, u32[]{:S(2)}) collective-permute-start(bf16[128,2304]{1,0:T(8,128)(2,1)S(1)} %collective-permute-done.16.refs_2_), channel_id=1, source_target_pairs={{0,1},{1,0},{2,3},{3,2},{4,5},{5,4},{6,7},{7,6},{8,9},{9,8},{10,11... | collective-permute-start | bytes 1769480 | tf_op jit(solution)/shard_map/ppermute | solution.py:66
  111.9 3.9 %collective-permute-start.19 = (bf16[128,2304]{1,0:T(8,128)(2,1)S(1)}, bf16[128,2304]{1,0:T(8,128)(2,1)S(1)}, u32[]{:S(2)}, u32[]{:S(2)}) collective-permute-start(bf16[128,2304]{1,0:T(8,128)(2,1)S(1)} %collective-permute-done.15.refs_1_), channel_id=1, source_target_pairs={{0,1},{1,0},{2,3},{3,2},{4,5},{5,4},{6,7},{7,6},{8,9},{9,8},{10,11... | collective-permute-start | bytes 1769480 | tf_op jit(solution)/shard_map/ppermute | solution.py:66

commit v5 on v4

--- a/solution.py
+++ b/solution.py
@@ -49,7 +49,7 @@
 
 CLASSES = chip_classes()
 SHIFTS = neighbour_shifts()
-GROUPS = ((0,), (1,), (2,), (3,))
+GROUPS = ((0,), (1,), (2, 3))
 
 
 def near_copies(block):

time: 123 us -> 122 us (level)
  starting transfers between devices: 32.9 us -> 29.7 us
  blocking collectives: 54.3 us -> 56.7 us
    ppermute x13, starting transfers between devices: 22 us -> 17.3 us  [swap_cores(): return lax.ppermute(a, 'c', SWAP)]
    ppermute x6, waiting for transfers between devices: 0.41 us -> 2.44 us  [spread(): return [near] + [lax.ppermute(near, NAMES, pairs) for pairs in SHIFTS]]
    all_to_all x1, blocking collectives: 15 us -> 17 us  [per_device(): pieces = lax.all_to_all(total, CHIPS, 0, 0, axis_index_groups=CLASSES)]
    ppermute x3, waiting for transfers between devices: 6.48 us -> 4.86 us  [per_device(): total = total + lax.ppermute(sent, NAMES, SHIFTS[k - 1]).astype(jnp.float32)]
    pallas_call x4 -> x3, Pallas kernels: 4.92 us -> 4.59 us  [front(): pl.pallas_call(functools.partial(front_kernel, count), out_shape=[jax.Sha...]
where the time goes in v5:
time: 122 us
  blocking collectives  56.7 us (46%)
  starting transfers between devices  29.7 us (24%)
  Pallas kernels  19.3 us (16%)
  waiting for transfers between devices  8.77 us (7%)
  local copies, waits for them, and re-layouts  5.53 us (5%)
    all_to_all x2, blocking collectives, near_copies(): near = lax.all_to_all(copies, CHIPS, 0, 0, axis_index_groups=CLASSES)  39.7 us
    ppermute x13, starting transfers between devices, swap_cores(): return lax.ppermute(a, 'c', SWAP)  17.3 us
    all_to_all x1, blocking collectives, per_device(): pieces = lax.all_to_all(total, CHIPS, 0, 0, axis_index_groups=CLASSES)  17 us
    pallas_call x1, Pallas kernels, tail(): pl.pallas_call(functools.partial(tail_kernel, widths, row_scale, len(prea...  7.08 us
    ppermute x3, starting transfers between devices, per_device(): total = total + lax.ppermute(sent, NAMES, SHIFTS[k - 1]).astype(jnp.float32)  6.45 us
    ppermute x6, starting transfers between devices, spread(): return [near] + [lax.ppermute(near, NAMES, pairs) for pairs in SHIFTS]  6 us
    ppermute x3, waiting for transfers between devices, per_device(): total = total + lax.ppermute(sent, NAMES, SHIFTS[k - 1]).astype(jnp.float32)  4.86 us
    unnamed x8, local copies, waits for them, and re-layouts  4.68 us
  transfers between devices with their start and end apart: 22, of which 7 were waited for; matrix products, arithmetic and copies ran while one was open for 1% of the time, Pallas kernels for 10%

profile of v5, /device:TPU:1, one launch (start us, length us, event | category | flops | bytes accessed | tf_op | source)
XLA Modules:
  0.0 122.0 jit_solution(16208662884273895961)
XLA Ops:
  0.6 1.5 %collective-permute-start = (bf16[4,4608]{1,0:T(4,128)(2,1)}, bf16[4,4608]{1,0:T(4,128)(2,1)S(1)}, u32[]{:S(2)}, u32[]{:S(2)}) collective-permute-start(bf16[4,4608]{1,0:T(4,128)(2,1)} %param.5), channel_id=1, source_target_pairs={{0,1},{1,0},{2,3},{3,2},{4,5},{5,4},{6,7},{7,6},{8,9},{9,8},{10,11... | collective-permute-start | bytes 110600 | tf_op jit(solution)/shard_map/ppermute | solution.py:66
  2.1 0.8 fusion.2
  2.9 0.3 collective-permute-done
  3.3 24.1 %all_to_all.15 = bf16[16,8,2304]{2,1,0:T(8,128)(2,1)S(1)} all-to-all(bf16[16,8,2304]{2,1,0:T(8,128)(2,1)S(1)} %broadcast_in_dim.9), channel_id=1, replica_groups={{0,4,16,20,42,46,58,62,64,68,80,84,106,110,122,126},{8,12,24,28,34,38,5..., dimensions={0} | all-to-all | bytes 1179648 | tf_op jit(solution)/shard_map/all_to_all | solution.py:57
  27.4 1.6 %collective-permute-start.4 = (bf16[128,2304]{1,0:T(8,128)(2,1)S(1)}, bf16[128,2304]{1,0:T(8,128)(2,1)S(1)}, u32[]{:S(2)}, u32[]{:S(2)}) collective-permute-start(bf16[128,2304]{1,0:T(8,128)(2,1)S(1)} %bitcast.7), channel_id=1, source_target_pairs={{0,1},{1,0},{2,3},{3,2},{4,5},{5,4},{6,7},{7,6},{8,9},{9,8},{10,11... | collective-permute-start | bytes 1769480 | tf_op jit(solution)/shard_map/ppermute | solution.py:66
  29.0 0.9 collective-permute-start.2
  29.9 1.8 %collective-permute-start.1 = (bf16[128,2304]{1,0:T(8,128)(2,1)S(1)}, bf16[128,2304]{1,0:T(8,128)(2,1)S(1)}, u32[]{:S(2)}, u32[]{:S(2)}) collective-permute-start(bf16[128,2304]{1,0:T(8,128)(2,1)S(1)} %bitcast.10), channel_id=1, source_target_pairs={{0,8},{1,25},{2,10},{3,27},{4,12},{5,29},{6,14},{7,31},{8,16},{9,1... | collective-permute-start | bytes 1769480 | tf_op jit(solution)/shard_map/ppermute | solution.py:62
  31.7 2.3 %copy-done = bf16[4608,512]{1,0:T(8,128)(2,1)S(1)} copy-done((bf16[4608,512]{1,0:T(8,128)(2,1)S(1)}, bf16[4608,512]{1,0:T(8,128)(2,1)}, u32[]{:S(2)}) %copy-start) | copy-done | bytes 4718616
  34.0 2.3 %copy-done.1 = bf16[512,4608]{1,0:T(8,128)(2,1)S(1)} copy-done((bf16[512,4608]{1,0:T(8,128)(2,1)S(1)}, bf16[512,4608]{1,0:T(8,128)(2,1)}, u32[]{:S(2)}) %copy-start.1) | copy-done | bytes 4718616
  36.4 0.7 load.1
  37.1 1.2 %front.3 = (f32[128,512]{1,0:T(8,128)S(1)}, bf16[128,512]{1,0:T(8,128)(2,1)S(1)}, bf16[128,2304]{1,0:T(8,128)(2,1)S(1)}) custom-call(f32[1,512]{1,0:T(1,128)S(1)} %bitcast.19, bf16[2304,512]{1,0:T(8,128)(2,1)S(1)} %get-tuple-element.55.enc_own, bf16[2304,512]{1,0:T(8,128)(2,1)S(1)} %get-tuple-element.56.enc_oth, ...), custom_call_target="tpu_custom_call" | custom-call | flops 905969664 | bytes 9437184 | tf_op jit(solution)/shard_map/front/pallas_call | solution.py:168
  38.3 0.5 parts.3
  38.8 0.2 collective-permute-done.1.refs_0_.refs_9_
  39.0 1.8 %collective-permute-start.6 = (bf16[128,2304]{1,0:T(8,128)(2,1)S(1)}, bf16[128,2304]{1,0:T(8,128)(2,1)S(1)}, u32[]{:S(2)}, u32[]{:S(2)}) collective-permute-start(bf16[128,2304]{1,0:T(8,128)(2,1)S(1)} %collective-permute-done.1.refs_0_.refs_9_), channel_id=1, source_target_pairs={{0,1},{1,0},{2,3},{3,2},{4,5},{5,4},{6,7},{7,6},{8,9},{9,8},{10,11... | collective-permute-start | bytes 1769480 | tf_op jit(solution)/shard_map/ppermute | solution.py:66
  40.8 0.5 collective-permute-start.10
  41.3 1.1 collective-permute-done.6.refs_1_.refs_13_
  42.4 1.2 %front.4 = (f32[128,512]{1,0:T(8,128)S(1)}, bf16[128,512]{1,0:T(8,128)(2,1)S(1)}, bf16[128,2304]{1,0:T(8,128)(2,1)S(1)}) custom-call(f32[1,512]{1,0:T(1,128)S(1)} %bitcast.20, bf16[2304,512]{1,0:T(8,128)(2,1)S(1)} %get-tuple-element.55.enc_own, bf16[2304,512]{1,0:T(8,128)(2,1)S(1)} %get-tuple-element.56.enc_oth, ...), custom_call_target="tpu_custom_call" | custom-call | flops 905969664 | bytes 9437184 | tf_op jit(solution)/shard_map/front/pallas_call | solution.py:168
  43.7 0.5 collective-permute-start.7
  44.1 0.1 collective-permute-start.5
  44.3 2.1 %front.5 = (f32[256,512]{1,0:T(8,128)S(1)}, bf16[256,512]{1,0:T(8,128)(2,1)S(1)}, bf16[128,2304]{1,0:T(8,128)(2,1)S(1)}, bf16[128,2304]{1,0:T(8,128)(2,1)S(1)}) custom-call(f32[1,512]{1,0:T(1,128)S(1)} %bitcast.21, bf16[2304,512]{1,0:T(8,128)(2,1)S(1)} %get-tuple-element.55.enc_own, bf16[2304,512]{1,0:T(8,128)(2,1)S(1)} %get-tuple-element.56.enc_oth, ...), custom_call_target="tpu_custom_call" | custom-call | flops 1811939328 | bytes 9437184 | tf_op jit(solution)/shard_map/front/pallas_call | solution.py:168
  46.4 0.5 collective-permute-start.11
  46.9 0.1 collective-permute-start.13
  47.0 0.5 parts.4
  47.5 0.8 parts.5
  48.3 0.1 add_convert_fusion.3
  48.4 1.3 %collective-permute-start.8 = (bf16[128,2304]{1,0:T(8,128)(2,1)S(1)}, bf16[128,2304]{1,0:T(8,128)(2,1)S(1)}, u32[]{:S(2)}, u32[]{:S(2)}) collective-permute-start(bf16[128,2304]{1,0:T(8,128)(2,1)S(1)} %add_convert_fusion.3), channel_id=1, source_target_pairs={{0,8},{1,25},{2,10},{3,27},{4,12},{5,29},{6,14},{7,31},{8,16},{9,1... | collective-permute-start | bytes 1769480 | tf_op jit(solution)/shard_map/ppermute | solution.py:456
  49.7 0.2 add_convert_fusion.1
  49.9 0.0 copy-start.3
  49.9 2.7 %collective-permute-start.14 = (bf16[128,2304]{1,0:T(8,128)(2,1)S(1)}, bf16[128,2304]{1,0:T(8,128)(2,1)S(1)}, u32[]{:S(2)}, u32[]{:S(2)}) collective-permute-start(bf16[128,2304]{1,0:T(8,128)(2,1)S(1)} %add_convert_fusion.1), channel_id=1, source_target_pairs={{0,32},{1,97},{2,34},{3,99},{4,36},{5,101},{6,38},{7,103},{8,40},{... | collective-permute-start | bytes 1769480 | tf_op jit(solution)/shard_map/ppermute | solution.py:456
  52.6 0.1 add_convert_fusion.2
  52.7 2.5 %collective-permute-start.12 = (bf16[128,2304]{1,0:T(8,128)(2,1)S(1)}, bf16[128,2304]{1,0:T(8,128)(2,1)S(1)}, u32[]{:S(2)}, u32[]{:S(2)}) collective-permute-start(bf16[128,2304]{1,0:T(8,128)(2,1)S(1)} %add_convert_fusion.2), channel_id=1, source_target_pairs={{0,2},{1,7},{2,4},{3,1},{4,6},{5,3},{6,0},{7,5},{8,10},{9,15},{10,... | collective-permute-start | bytes 1769480 | tf_op jit(solution)/shard_map/ppermute | solution.py:456
  55.2 1.9 %side.1 = (bf16[528,512]{1,0:T(8,128)(2,1)S(1)}, f32[512,1]{1,0:T(8,128)S(1)}, f32[1,512]{1,0:T(1,128)S(1)}) custom-call(s32[512]{0:T(512)S(1)} %copy-done.3, bf16[128,512]{1,0:T(8,128)(2,1)S(1)} %get-tuple-element.69.act_ref.refs_0_, bf16[128,512]{1,0:T(8,128)(2,1)S(1)} %get-tuple-element.59.act_ref.refs_1_, ...), custom_call_target="tpu_custom_call" | custom-call | flops 9437184 | bytes 4718592 | tf_op jit(solution)/shard_map/side/pallas_call | solution.py:238
  57.2 0.3 collective-permute-done.8
  57.5 1.9 %collective-permute-done.14 = bf16[128,2304]{1,0:T(8,128)(2,1)S(1)} collective-permute-done((bf16[128,2304]{1,0:T(8,128)(2,1)S(1)}, bf16[128,2304]{1,0:T(8,128)(2,1)S(1)}, u32[]{:S(2)}, u32[]{:S(2)}) %collective-permute-start.14) | collective-permute-done | bytes 589856 | tf_op jit(solution)/shard_map/ppermute | solution.py:456
  59.4 2.7 %collective-permute-done.12 = bf16[128,2304]{1,0:T(8,128)(2,1)S(1)} collective-permute-done((bf16[128,2304]{1,0:T(8,128)(2,1)S(1)}, bf16[128,2304]{1,0:T(8,128)(2,1)S(1)}, u32[]{:S(2)}, u32[]{:S(2)}) %collective-permute-start.12) | collective-permute-done | bytes 589856 | tf_op jit(solution)/shard_map/ppermute | solution.py:456
  62.1 0.4 fusion
  62.5 17.0 %all_to_all.16 = bf16[16,8,2304]{2,1,0:T(8,128)(2,1)S(1)} all-to-all(bf16[16,8,2304]{2,1,0:T(8,128)(2,1)S(1)} %fusion), channel_id=1, replica_groups={{0,4,16,20,42,46,58,62,64,68,80,84,106,110,122,126},{8,12,24,28,34,38,5..., dimensions={0} | all-to-all | bytes 1179648 | tf_op jit(solution)/shard_map/all_to_all | solution.py:460
  79.4 0.1 convert_reduce_fusion
  79.6 15.6 %all_to_all.17 = bf16[16,8,2304]{2,1,0:T(8,128)(2,1)S(1)} all-to-all(bf16[16,8,2304]{2,1,0:T(8,128)(2,1)S(1)} %broadcast_in_dim.11), channel_id=1, replica_groups={{0,4,16,20,42,46,58,62,64,68,80,84,106,110,122,126},{8,12,24,28,34,38,5..., dimensions={0} | all-to-all | bytes 1179648 | tf_op jit(solution)/shard_map/all_to_all | solution.py:57
  95.2 1.1 collective-permute-start.16
  96.3 2.2 %collective-permute-start.15 = (bf16[128,2304]{1,0:T(8,128)(2,1)S(1)}, bf16[128,2304]{1,0:T(8,128)(2,1)S(1)}, u32[]{:S(2)}, u32[]{:S(2)}) collective-permute-start(bf16[128,2304]{1,0:T(8,128)(2,1)S(1)} %bitcast.16), channel_id=1, source_target_pairs={{0,8},{1,25},{2,10},{3,27},{4,12},{5,29},{6,14},{7,31},{8,16},{9,1... | collective-permute-start | bytes 1769480 | tf_op jit(solution)/shard_map/ppermute | solution.py:62
  98.5 3.1 %collective-permute-start.18 = (bf16[128,2304]{1,0:T(8,128)(2,1)S(1)}, bf16[128,2304]{1,0:T(8,128)(2,1)S(1)}, u32[]{:S(2)}, u32[]{:S(2)}) collective-permute-start(bf16[128,2304]{1,0:T(8,128)(2,1)S(1)} %bitcast.17), channel_id=1, source_target_pairs={{0,1},{1,0},{2,3},{3,2},{4,5},{5,4},{6,7},{7,6},{8,9},{9,8},{10,11... | collective-permute-start | bytes 1769480 | tf_op jit(solution)/shard_map/ppermute | solution.py:66
  101.6 2.3 %collective-permute-done.17.refs_3_ = bf16[128,2304]{1,0:T(8,128)(2,1)S(1)} collective-permute-done((bf16[128,2304]{1,0:T(8,128)(2,1)S(1)}, bf16[128,2304]{1,0:T(8,128)(2,1)S(1)}, u32[]{:S(2)}, u32[]{:S(2)}) %collective-permute-start.17) | collective-permute-done | bytes 589856 | tf_op jit(solution)/shard_map/ppermute | solution.py:62
  103.9 7.0 %collective-permute-start.21 = (bf16[128,2304]{1,0:T(8,128)(2,1)S(1)}, bf16[128,2304]{1,0:T(8,128)(2,1)S(1)}, u32[]{:S(2)}, u32[]{:S(2)}) collective-permute-start(bf16[128,2304]{1,0:T(8,128)(2,1)S(1)} %collective-permute-done.17.refs_3_), channel_id=1, source_target_pairs={{0,1},{1,0},{2,3},{3,2},{4,5},{5,4},{6,7},{7,6},{8,9},{9,8},{10,11... | collective-permute-start | bytes 1769480 | tf_op jit(solution)/shard_map/ppermute | solution.py:66
  110.9 0.0 collective-permute-start.20
  110.9 0.5 collective-permute-start.19
  111.4 3.3 %grad.1 = (f32[512,512]{1,0:T(8,128)S(1)}, f32[4,2304]{1,0:T(4,128)S(1)}, bf16[512,4608]{1,0:T(8,128)(2,1)}) custom-call(s32[1]{0:T(128)} %bitcast.core_ref, bf16[528,512]{1,0:T(8,128)(2,1)S(1)} %get-tuple-element.73.left_ref, f32[512,1]{1,0:T(8,128)S(1)} %get-tuple-element.74.scale_ref, bf16[512,2304]{1,0:T(8,128)(2,1)S(1)} %get-tuple-element.60.dec_ref.refs_3_, ...), custom_call_target="tpu_custom_call" | custom-call | flops 2415919104 | bytes 4718592 | tf_op jit(solution)/shard_map/grad/pallas_call | solution.py:306
  114.8 7.1 %tail.1 = (bf16[512,4608]{1,0:T(8,128)(2,1)}, bf16[4608,512]{1,0:T(8,128)(2,1)}, f32[1,512]{1,0:T(1,128)}, f32[4,4608]{1,0:T(4,128)}) custom-call(s32[1]{0:T(128)} %bitcast.core_ref, bf16[528,512]{1,0:T(8,128)(2,1)S(1)} %get-tuple-element.73.left_ref, f32[512,1]{1,0:T(8,128)S(1)} %get-tuple-element.74.scale_ref, ...), custom_call_target="tpu_custom_call", output_to_operand_aliasing={{0}: (22, {})} | custom-call | flops 3623878656 | bytes 9437184 | tf_op jit(solution)/shard_map/tail/pallas_call | solution.py:396
  (28 shorter events, 0.2 us)
Async XLA Ops:
  0.6 2.6 %collective-permute-start = (bf16[4,4608]{1,0:T(4,128)(2,1)}, bf16[4,4608]{1,0:T(4,128)(2,1)S(1)}, u32[]{:S(2)}, u32[]{:S(2)}) collective-permute-start(bf16[4,4608]{1,0:T(4,128)(2,1)} %param.5), channel_id=1, source_target_pairs={{0,1},{1,0},{2,3},{3,2},{4,5},{5,4},{6,7},{7,6},{8,9},{9,8},{10,11... | collective-permute-start | bytes 110600 | tf_op jit(solution)/shard_map/ppermute | solution.py:66
  27.4 9.6 %collective-permute-start.4 = (bf16[128,2304]{1,0:T(8,128)(2,1)S(1)}, bf16[128,2304]{1,0:T(8,128)(2,1)S(1)}, u32[]{:S(2)}, u32[]{:S(2)}) collective-permute-start(bf16[128,2304]{1,0:T(8,128)(2,1)S(1)} %bitcast.7), channel_id=1, source_target_pairs={{0,1},{1,0},{2,3},{3,2},{4,5},{5,4},{6,7},{7,6},{8,9},{9,8},{10,11... | collective-permute-start | bytes 1769480 | tf_op jit(solution)/shard_map/ppermute | solution.py:66
  29.0 9.8 %collective-permute-start.3 = (bf16[128,2304]{1,0:T(8,128)(2,1)S(1)}, bf16[128,2304]{1,0:T(8,128)(2,1)S(1)}, u32[]{:S(2)}, u32[]{:S(2)}) collective-permute-start(bf16[128,2304]{1,0:T(8,128)(2,1)S(1)} %bitcast.8), channel_id=1, source_target_pairs={{0,32},{1,97},{2,34},{3,99},{4,36},{5,101},{6,38},{7,103},{8,40},{... | collective-permute-start | bytes 1769480 | tf_op jit(solution)/shard_map/ppermute | solution.py:62
  29.0 9.8 %collective-permute-start.2 = (bf16[128,2304]{1,0:T(8,128)(2,1)S(1)}, bf16[128,2304]{1,0:T(8,128)(2,1)S(1)}, u32[]{:S(2)}, u32[]{:S(2)}) collective-permute-start(bf16[128,2304]{1,0:T(8,128)(2,1)S(1)} %bitcast.9), channel_id=1, source_target_pairs={{0,2},{1,7},{2,4},{3,1},{4,6},{5,3},{6,0},{7,5},{8,10},{9,15},{10,... | collective-permute-start | bytes 1769480 | tf_op jit(solution)/shard_map/ppermute | solution.py:62
  29.9 9.0 %collective-permute-start.1 = (bf16[128,2304]{1,0:T(8,128)(2,1)S(1)}, bf16[128,2304]{1,0:T(8,128)(2,1)S(1)}, u32[]{:S(2)}, u32[]{:S(2)}) collective-permute-start(bf16[128,2304]{1,0:T(8,128)(2,1)S(1)} %bitcast.10), channel_id=1, source_target_pairs={{0,8},{1,25},{2,10},{3,27},{4,12},{5,29},{6,14},{7,31},{8,16},{9,1... | collective-permute-start | bytes 1769480 | tf_op jit(solution)/shard_map/ppermute | solution.py:62
  31.7 2.3 %copy-start = (bf16[4608,512]{1,0:T(8,128)(2,1)S(1)}, bf16[4608,512]{1,0:T(8,128)(2,1)}, u32[]{:S(2)}) copy-start(bf16[4608,512]{1,0:T(8,128)(2,1)} %enc_ref.1) | copy-start | bytes 14155780
  34.0 2.3 %copy-start.1 = (bf16[512,4608]{1,0:T(8,128)(2,1)S(1)}, bf16[512,4608]{1,0:T(8,128)(2,1)}, u32[]{:S(2)}) copy-start(bf16[512,4608]{1,0:T(8,128)(2,1)} %dec_ref.1) | copy-start | bytes 14155780
  36.4 0.7 copy-start.2
  39.0 3.5 %collective-permute-start.6 = (bf16[128,2304]{1,0:T(8,128)(2,1)S(1)}, bf16[128,2304]{1,0:T(8,128)(2,1)S(1)}, u32[]{:S(2)}, u32[]{:S(2)}) collective-permute-start(bf16[128,2304]{1,0:T(8,128)(2,1)S(1)} %collective-permute-done.1.refs_0_.refs_9_), channel_id=1, source_target_pairs={{0,1},{1,0},{2,3},{3,2},{4,5},{5,4},{6,7},{7,6},{8,9},{9,8},{10,11... | collective-permute-start | bytes 1769480 | tf_op jit(solution)/shard_map/ppermute | solution.py:66
  40.8 3.5 %collective-permute-start.9 = (bf16[128,2304]{1,0:T(8,128)(2,1)S(1)}, bf16[128,2304]{1,0:T(8,128)(2,1)S(1)}, u32[]{:S(2)}, u32[]{:S(2)}) collective-permute-start(bf16[128,2304]{1,0:T(8,128)(2,1)S(1)} %collective-permute-done.2.refs_0_.refs_10_), channel_id=1, source_target_pairs={{0,1},{1,0},{2,3},{3,2},{4,5},{5,4},{6,7},{7,6},{8,9},{9,8},{10,11... | collective-permute-start | bytes 1769480 | tf_op jit(solution)/shard_map/ppermute | solution.py:66
  40.8 3.5 %collective-permute-start.10 = (bf16[128,2304]{1,0:T(8,128)(2,1)S(1)}, bf16[128,2304]{1,0:T(8,128)(2,1)S(1)}, u32[]{:S(2)}, u32[]{:S(2)}) collective-permute-start(bf16[128,2304]{1,0:T(8,128)(2,1)S(1)} %collective-permute-done.3.refs_1_.refs_11_), channel_id=1, source_target_pairs={{0,1},{1,0},{2,3},{3,2},{4,5},{5,4},{6,7},{7,6},{8,9},{9,8},{10,11... | collective-permute-start | bytes 1769480 | tf_op jit(solution)/shard_map/ppermute | solution.py:66
  43.7 4.6 %collective-permute-start.7 = (bf16[128,2304]{1,0:T(8,128)(2,1)S(1)}, bf16[128,2304]{1,0:T(8,128)(2,1)S(1)}, u32[]{:S(2)}, u32[]{:S(2)}) collective-permute-start(bf16[128,2304]{1,0:T(8,128)(2,1)S(1)} %get-tuple-element.61), channel_id=1, source_target_pairs={{0,1},{1,0},{2,3},{3,2},{4,5},{5,4},{6,7},{7,6},{8,9},{9,8},{10,11... | collective-permute-start | bytes 1769480 | tf_op jit(solution)/shard_map/ppermute | solution.py:66
  44.1 13.1 %collective-permute-start.5 = (bf16[128,2304]{1,0:T(8,128)(2,1)S(1)}, bf16[128,2304]{1,0:T(8,128)(2,1)S(1)}, u32[]{:S(2)}, u32[]{:S(2)}) collective-permute-start(bf16[128,2304]{1,0:T(8,128)(2,1)S(1)} %get-tuple-element.54), channel_id=1, source_target_pairs={{0,1},{1,0},{2,3},{3,2},{4,5},{5,4},{6,7},{7,6},{8,9},{9,8},{10,11... | collective-permute-start | bytes 1769480 | tf_op jit(solution)/shard_map/ppermute | solution.py:66
  46.4 6.2 %collective-permute-start.11 = (bf16[128,2304]{1,0:T(8,128)(2,1)S(1)}, bf16[128,2304]{1,0:T(8,128)(2,1)S(1)}, u32[]{:S(2)}, u32[]{:S(2)}) collective-permute-start(bf16[128,2304]{1,0:T(8,128)(2,1)S(1)} %get-tuple-element.66), channel_id=1, source_target_pairs={{0,1},{1,0},{2,3},{3,2},{4,5},{5,4},{6,7},{7,6},{8,9},{9,8},{10,11... | collective-permute-start | bytes 1769480 | tf_op jit(solution)/shard_map/ppermute | solution.py:66
  46.9 2.8 %collective-permute-start.13 = (bf16[128,2304]{1,0:T(8,128)(2,1)S(1)}, bf16[128,2304]{1,0:T(8,128)(2,1)S(1)}, u32[]{:S(2)}, u32[]{:S(2)}) collective-permute-start(bf16[128,2304]{1,0:T(8,128)(2,1)S(1)} %get-tuple-element.68), channel_id=1, source_target_pairs={{0,1},{1,0},{2,3},{3,2},{4,5},{5,4},{6,7},{7,6},{8,9},{9,8},{10,11... | collective-permute-start | bytes 1769480 | tf_op jit(solution)/shard_map/ppermute | solution.py:66
  48.4 9.1 %collective-permute-start.8 = (bf16[128,2304]{1,0:T(8,128)(2,1)S(1)}, bf16[128,2304]{1,0:T(8,128)(2,1)S(1)}, u32[]{:S(2)}, u32[]{:S(2)}) collective-permute-start(bf16[128,2304]{1,0:T(8,128)(2,1)S(1)} %add_convert_fusion.3), channel_id=1, source_target_pairs={{0,8},{1,25},{2,10},{3,27},{4,12},{5,29},{6,14},{7,31},{8,16},{9,1... | collective-permute-start | bytes 1769480 | tf_op jit(solution)/shard_map/ppermute | solution.py:456
  49.9 5.3 %copy-start.3 = (s32[512]{0:T(512)S(1)}, s32[512]{0:T(512)}, u32[]{:S(2)}) copy-start(s32[512]{0:T(512)} %order_ref.1) | copy-start | bytes 6148
  49.9 9.5 %collective-permute-start.14 = (bf16[128,2304]{1,0:T(8,128)(2,1)S(1)}, bf16[128,2304]{1,0:T(8,128)(2,1)S(1)}, u32[]{:S(2)}, u32[]{:S(2)}) collective-permute-start(bf16[128,2304]{1,0:T(8,128)(2,1)S(1)} %add_convert_fusion.1), channel_id=1, source_target_pairs={{0,32},{1,97},{2,34},{3,99},{4,36},{5,101},{6,38},{7,103},{8,40},{... | collective-permute-start | bytes 1769480 | tf_op jit(solution)/shard_map/ppermute | solution.py:456
  52.7 9.4 %collective-permute-start.12 = (bf16[128,2304]{1,0:T(8,128)(2,1)S(1)}, bf16[128,2304]{1,0:T(8,128)(2,1)S(1)}, u32[]{:S(2)}, u32[]{:S(2)}) collective-permute-start(bf16[128,2304]{1,0:T(8,128)(2,1)S(1)} %add_convert_fusion.2), channel_id=1, source_target_pairs={{0,2},{1,7},{2,4},{3,1},{4,6},{5,3},{6,0},{7,5},{8,10},{9,15},{10,... | collective-permute-start | bytes 1769480 | tf_op jit(solution)/shard_map/ppermute | solution.py:456
  95.2 8.7 %collective-permute-start.17 = (bf16[128,2304]{1,0:T(8,128)(2,1)S(1)}, bf16[128,2304]{1,0:T(8,128)(2,1)S(1)}, u32[]{:S(2)}, u32[]{:S(2)}) collective-permute-start(bf16[128,2304]{1,0:T(8,128)(2,1)S(1)} %bitcast.14), channel_id=1, source_target_pairs={{0,32},{1,97},{2,34},{3,99},{4,36},{5,101},{6,38},{7,103},{8,40},{... | collective-permute-start | bytes 1769480 | tf_op jit(solution)/shard_map/ppermute | solution.py:62
  95.2 15.7 %collective-permute-start.16 = (bf16[128,2304]{1,0:T(8,128)(2,1)S(1)}, bf16[128,2304]{1,0:T(8,128)(2,1)S(1)}, u32[]{:S(2)}, u32[]{:S(2)}) collective-permute-start(bf16[128,2304]{1,0:T(8,128)(2,1)S(1)} %bitcast.15), channel_id=1, source_target_pairs={{0,2},{1,7},{2,4},{3,1},{4,6},{5,3},{6,0},{7,5},{8,10},{9,15},{10,... | collective-permute-start | bytes 1769480 | tf_op jit(solution)/shard_map/ppermute | solution.py:62
  96.3 14.6 %collective-permute-start.15 = (bf16[128,2304]{1,0:T(8,128)(2,1)S(1)}, bf16[128,2304]{1,0:T(8,128)(2,1)S(1)}, u32[]{:S(2)}, u32[]{:S(2)}) collective-permute-start(bf16[128,2304]{1,0:T(8,128)(2,1)S(1)} %bitcast.16), channel_id=1, source_target_pairs={{0,8},{1,25},{2,10},{3,27},{4,12},{5,29},{6,14},{7,31},{8,16},{9,1... | collective-permute-start | bytes 1769480 | tf_op jit(solution)/shard_map/ppermute | solution.py:62
  98.5 16.3 %collective-permute-start.18 = (bf16[128,2304]{1,0:T(8,128)(2,1)S(1)}, bf16[128,2304]{1,0:T(8,128)(2,1)S(1)}, u32[]{:S(2)}, u32[]{:S(2)}) collective-permute-start(bf16[128,2304]{1,0:T(8,128)(2,1)S(1)} %bitcast.17), channel_id=1, source_target_pairs={{0,1},{1,0},{2,3},{3,2},{4,5},{5,4},{6,7},{7,6},{8,9},{9,8},{10,11... | collective-permute-start | bytes 1769480 | tf_op jit(solution)/shard_map/ppermute | solution.py:66
  103.9 10.9 %collective-permute-start.21 = (bf16[128,2304]{1,0:T(8,128)(2,1)S(1)}, bf16[128,2304]{1,0:T(8,128)(2,1)S(1)}, u32[]{:S(2)}, u32[]{:S(2)}) collective-permute-start(bf16[128,2304]{1,0:T(8,128)(2,1)S(1)} %collective-permute-done.17.refs_3_), channel_id=1, source_target_pairs={{0,1},{1,0},{2,3},{3,2},{4,5},{5,4},{6,7},{7,6},{8,9},{9,8},{10,11... | collective-permute-start | bytes 1769480 | tf_op jit(solution)/shard_map/ppermute | solution.py:66
  110.9 3.9 %collective-permute-start.20 = (bf16[128,2304]{1,0:T(8,128)(2,1)S(1)}, bf16[128,2304]{1,0:T(8,128)(2,1)S(1)}, u32[]{:S(2)}, u32[]{:S(2)}) collective-permute-start(bf16[128,2304]{1,0:T(8,128)(2,1)S(1)} %collective-permute-done.16.refs_2_), channel_id=1, source_target_pairs={{0,1},{1,0},{2,3},{3,2},{4,5},{5,4},{6,7},{7,6},{8,9},{9,8},{10,11... | collective-permute-start | bytes 1769480 | tf_op jit(solution)/shard_map/ppermute | solution.py:66
  110.9 3.9 %collective-permute-start.19 = (bf16[128,2304]{1,0:T(8,128)(2,1)S(1)}, bf16[128,2304]{1,0:T(8,128)(2,1)S(1)}, u32[]{:S(2)}, u32[]{:S(2)}) collective-permute-start(bf16[128,2304]{1,0:T(8,128)(2,1)S(1)} %collective-permute-done.15.refs_1_), channel_id=1, source_target_pairs={{0,1},{1,0},{2,3},{3,2},{4,5},{5,4},{6,7},{7,6},{8,9},{9,8},{10,11... | collective-permute-start | bytes 1769480 | tf_op jit(solution)/shard_map/ppermute | solution.py:66

commit v6 on v5

--- a/solution.py
+++ b/solution.py
@@ -89,14 +89,14 @@
     return found
 
 
-def load_kernel(widths, core_ref, near_ref, enc_ref, dec_ref, *refs):
+def load_kernel(widths, near_ref, enc_ref, dec_ref, *refs):
     pieces = 2 * len(widths)
     enc_refs, dec_refs, sems = refs[:pieces], refs[pieces : 2 * pieces], refs[2 * pieces]
     half = sum(widths)
     copies = []
     for k in range(pieces):
         side_index, q = divmod(k, len(widths))
-        base = jnp.where(core_ref[0] == side_index, 0, half) + sum(widths[:q])
+        base = piece_base(lax.axis_index("c"), half, side_index, sum(widths[:q]))
         base = pl.multiple_of(base, 128)
         cut = pl.ds(base, widths[q])
         copies.append(pltpu.make_async_copy(enc_ref.at[cut, :], enc_refs[k], sems.at[k, 0]))
@@ -107,20 +107,20 @@
         copy.wait()
 
 
-def load(core, near, enc_weight, dec_weight, widths):
+def load(near, enc_weight, dec_weight, widths):
     width, latents = enc_weight.shape
     both = list(widths) * 2
     out = pl.pallas_call(
         functools.partial(load_kernel, widths),
         out_shape=[jax.ShapeDtypeStruct((w, latents), jnp.bfloat16) for w in both]
         + [jax.ShapeDtypeStruct((latents, w), jnp.bfloat16) for w in both],
-        in_specs=[SMEM, ANY, HBM, HBM],
+        in_specs=[ANY, HBM, HBM],
         out_specs=[VMEM] * (2 * len(both)),
         scratch_shapes=[pltpu.SemaphoreType.DMA((len(both), 2))],
         compiler_params=params(SMALL_VMEM),
         cost_estimate=estimate(0, 8 * width * latents),
         name="load",
-    )(core, near, enc_weight, dec_weight)
+    )(near, enc_weight, dec_weight)
     return out[: len(both)], out[len(both) :]
 
 
@@ -277,11 +277,11 @@
     return jnp.where(core == side_index, 0, half) + offset
 
 
-def grad_kernel(later, side_index, offset, half, row_scale, core_ref, left_ref, scale_ref, dec_ref, *refs):
+def grad_kernel(later, side_index, offset, half, row_scale, left_ref, scale_ref, dec_ref, *refs):
     blocks, refs = refs[:4], refs[4:]
     before, refs = (refs[0], refs[2:]) if later else (None, refs)
     total_ref, recon_ref, dec_grad_ref, dec_out, sems = refs
-    base = piece_base(core_ref[0], half, side_index, offset)
+    base = piece_base(lax.axis_index("c"), half, side_index, offset)
     err = stack(blocks)
     outs = []
 
@@ -299,7 +299,7 @@
         out.wait()
 
 
-def grad(core, left, scale, dec, blocks, held, side_index, offset, half, row_scale, out_rows):
+def grad(left, scale, dec, blocks, held, side_index, offset, half, row_scale, out_rows):
     rows, wide = blocks[0].shape
     latents = dec.shape[0]
     later = held is not None
@@ -310,20 +310,20 @@
             jax.ShapeDtypeStruct((out_rows, wide), jnp.float32),
             jax.ShapeDtypeStruct((latents, 2 * half), jnp.bfloat16),
         ),
-        in_specs=[SMEM] + [VMEM] * 7 + ([VMEM, HBM] if later else []),
+        in_specs=[VMEM] * 7 + ([VMEM, HBM] if later else []),
         out_specs=(VMEM, VMEM, HBM),
         scratch_shapes=[
             pltpu.VMEM((latents, wide), jnp.bfloat16),
             pltpu.SemaphoreType.DMA((len(chunks(wide)),)),
         ],
-        input_output_aliases={9: 2} if later else {},
+        input_output_aliases={8: 2} if later else {},
         compiler_params=params(SMALL_VMEM),
         cost_estimate=estimate(16 * rows * latents * wide, 4 * latents * wide),
         name="grad",
-    )(core, left, scale, dec, *blocks, *(held if later else ()))
-
-
-def tail_kernel(widths, row_scale, groups, core_ref, left_ref, scale_ref, norm_ref, total_ref, dec_ref, *refs):
+    )(left, scale, dec, *blocks, *(held if later else ()))
+
+
+def tail_kernel(widths, row_scale, groups, left_ref, scale_ref, norm_ref, total_ref, dec_ref, *refs):
     count = len(widths)
     preacts, refs = refs[:groups], refs[groups:]
     recons, refs = refs[: 2 * count - 1], refs[2 * count - 1 :]
@@ -331,7 +331,7 @@
     x_blocks, refs = [refs[4 * k : 4 * k + 4] for k in range(2 * count)], refs[8 * count + 1 :]
     dec_grad_ref, enc_grad_ref, bias_ref, recon_ref = refs[:4]
     dec_out, enc_out, recon_last, pre_ref, dec_sems, enc_sems = refs[4:]
-    core = core_ref[0]
+    core = lax.axis_index("c")
     half = sum(widths)
     bases = []
     for k in range(2 * count):
@@ -374,7 +374,7 @@
         for at, step in chunks(widths[k % count]):
             encoder.append(encoder_task(len(encoder), row, k, at, step))
             row += step
-    tasks = [(product, use), decoder.pop(0)]
+    tasks = [decoder.pop(0), (product, use), decoder.pop(0)]
     for spot, task in enumerate(encoder):
         tasks.append(task)
         if decoder and spot % 2 == 1:
@@ -386,7 +386,7 @@
         out.wait()
 
 
-def tail(core, left, preacts, scale, norm, total, dec, recons, e_blocks, x_blocks, dec_grad, row_scale, widths):
+def tail(left, preacts, scale, norm, total, dec, recons, e_blocks, x_blocks, dec_grad, row_scale, widths):
     rows = e_blocks[0].shape[0]
     latents = dec.shape[0]
     half = sum(widths)
@@ -401,7 +401,7 @@
             jax.ShapeDtypeStruct((1, latents), jnp.float32),
             jax.ShapeDtypeStruct((out_rows, 2 * half), jnp.float32),
         ),
-        in_specs=[SMEM] + [VMEM] * len(vmem_args) + [HBM],
+        in_specs=[VMEM] * len(vmem_args) + [HBM],
         out_specs=(HBM, HBM, VMEM, VMEM),
         scratch_shapes=[
             pltpu.VMEM((latents, widths[-1]), jnp.bfloat16),
@@ -411,11 +411,11 @@
             pltpu.SemaphoreType.DMA((len(chunks(widths[-1])),)),
             pltpu.SemaphoreType.DMA((spots,)),
         ],
-        input_output_aliases={1 + len(vmem_args): 0},
+        input_output_aliases={len(vmem_args): 0},
         compiler_params=params(TAIL_VMEM),
         cost_estimate=estimate(24 * rows * latents * half, 8 * latents * half),
         name="tail",
-    )(core, *vmem_args, dec_grad)
+    )(*vmem_args, dec_grad)
 
 
 def per_device(tokens, batch_order, enc_weight, enc_bias, dec_weight):
@@ -426,7 +426,6 @@
     widths = (half,)
     block_rows = total_rows // 4
     core = lax.axis_index("c")
-    core_arg = core[None].astype(jnp.int32)
 
     got = swap_cores(tokens)
     low = jnp.concatenate([tokens[:, :half], got[:, :half]])
@@ -434,7 +433,7 @@
     block = jnp.where(core == 0, low, high)
     near = near_copies(block)
     x_own = spread(near)
-    encs, decs = load(core_arg, near, enc_weight, dec_weight, widths)
+    encs, decs = load(near, enc_weight, dec_weight, widths)
     done = []
 
     def work(group):
@@ -463,9 +462,9 @@
     near = near_copies(err_block)
     e_own = spread(near)
     e_oth = [swap_cores(a) for a in e_own]
-    act_part, recon_own, dec_grad = grad(core_arg, left, scale, decs[0], e_own, None, 0, 0, half, row_scale, rows_dev)
+    act_part, recon_own, dec_grad = grad(left, scale, decs[0], e_own, None, 0, 0, half, row_scale, rows_dev)
     dec_grad, enc_grad, bias_grad, recon_error = tail(
-        core_arg, left, preacts, scale, norm, act_part, decs[1], [recon_own], e_oth, [x_own, x_oth], dec_grad, row_scale,
+        left, preacts, scale, norm, act_part, decs[1], [recon_own], e_oth, [x_own, x_oth], dec_grad, row_scale,
         widths,
     )
     return (recon_error, enc_grad, dec_grad, bias_grad[0])

time: 122 us -> 122 us (level)
  no operation moved by 1% of the time
where the time goes in v6:
time: 122 us
  blocking collectives  56.7 us (46%)
  starting transfers between devices  29.7 us (24%)
  Pallas kernels  19.3 us (16%)
  waiting for transfers between devices  8.76 us (7%)
  local copies, waits for them, and re-layouts  5.53 us (5%)
    all_to_all x2, blocking collectives, near_copies(): near = lax.all_to_all(copies, CHIPS, 0, 0, axis_index_groups=CLASSES)  39.7 us
    ppermute x13, starting transfers between devices, swap_cores(): return lax.ppermute(a, 'c', SWAP)  17.3 us
    all_to_all x1, blocking collectives, per_device(): pieces = lax.all_to_all(total, CHIPS, 0, 0, axis_index_groups=CLASSES)  17 us
    pallas_call x1, Pallas kernels, tail(): pl.pallas_call(functools.partial(tail_kernel, widths, row_scale, len(prea...  7.04 us
    ppermute x3, starting transfers between devices, per_device(): total = total + lax.ppermute(sent, NAMES, SHIFTS[k - 1]).astype(jnp.float32)  6.47 us
    ppermute x6, starting transfers between devices, spread(): return [near] + [lax.ppermute(near, NAMES, pairs) for pairs in SHIFTS]  6 us
    ppermute x3, waiting for transfers between devices, per_device(): total = total + lax.ppermute(sent, NAMES, SHIFTS[k - 1]).astype(jnp.float32)  4.87 us
    unnamed x8, local copies, waits for them, and re-layouts  4.69 us
  transfers between devices with their start and end apart: 22, of which 7 were waited for; matrix products, arithmetic and copies ran while one was open for 1% of the time, Pallas kernels for 10%

profile of v6, /device:TPU:1, one launch (start us, length us, event | category | flops | bytes accessed | tf_op | source)
XLA Modules:
  0.0 122.0 jit_solution(6563008897771224380)
XLA Ops:
  0.6 1.5 %collective-permute-start = (bf16[4,4608]{1,0:T(4,128)(2,1)}, bf16[4,4608]{1,0:T(4,128)(2,1)S(1)}, u32[]{:S(2)}, u32[]{:S(2)}) collective-permute-start(bf16[4,4608]{1,0:T(4,128)(2,1)} %param.5), channel_id=1, source_target_pairs={{0,1},{1,0},{2,3},{3,2},{4,5},{5,4},{6,7},{7,6},{8,9},{9,8},{10,11... | collective-permute-start | bytes 110600 | tf_op jit(solution)/shard_map/ppermute | solution.py:66
  2.1 0.8 fusion.2
  2.9 0.3 collective-permute-done
  3.3 24.1 %all_to_all.15 = bf16[16,8,2304]{2,1,0:T(8,128)(2,1)S(1)} all-to-all(bf16[16,8,2304]{2,1,0:T(8,128)(2,1)S(1)} %broadcast_in_dim.6), channel_id=1, replica_groups={{0,4,16,20,42,46,58,62,64,68,80,84,106,110,122,126},{8,12,24,28,34,38,5..., dimensions={0} | all-to-all | bytes 1179648 | tf_op jit(solution)/shard_map/all_to_all | solution.py:57
  27.5 1.6 %collective-permute-start.4 = (bf16[128,2304]{1,0:T(8,128)(2,1)S(1)}, bf16[128,2304]{1,0:T(8,128)(2,1)S(1)}, u32[]{:S(2)}, u32[]{:S(2)}) collective-permute-start(bf16[128,2304]{1,0:T(8,128)(2,1)S(1)} %bitcast.6), channel_id=1, source_target_pairs={{0,1},{1,0},{2,3},{3,2},{4,5},{5,4},{6,7},{7,6},{8,9},{9,8},{10,11... | collective-permute-start | bytes 1769480 | tf_op jit(solution)/shard_map/ppermute | solution.py:66
  29.0 0.9 collective-permute-start.2
  29.9 1.8 %collective-permute-start.1 = (bf16[128,2304]{1,0:T(8,128)(2,1)S(1)}, bf16[128,2304]{1,0:T(8,128)(2,1)S(1)}, u32[]{:S(2)}, u32[]{:S(2)}) collective-permute-start(bf16[128,2304]{1,0:T(8,128)(2,1)S(1)} %bitcast.9), channel_id=1, source_target_pairs={{0,8},{1,25},{2,10},{3,27},{4,12},{5,29},{6,14},{7,31},{8,16},{9,1... | collective-permute-start | bytes 1769480 | tf_op jit(solution)/shard_map/ppermute | solution.py:62
  31.7 2.3 %copy-done = bf16[4608,512]{1,0:T(8,128)(2,1)S(1)} copy-done((bf16[4608,512]{1,0:T(8,128)(2,1)S(1)}, bf16[4608,512]{1,0:T(8,128)(2,1)}, u32[]{:S(2)}) %copy-start) | copy-done | bytes 4718616
  34.0 2.3 %copy-done.1 = bf16[512,4608]{1,0:T(8,128)(2,1)S(1)} copy-done((bf16[512,4608]{1,0:T(8,128)(2,1)S(1)}, bf16[512,4608]{1,0:T(8,128)(2,1)}, u32[]{:S(2)}) %copy-start.1) | copy-done | bytes 4718616
  36.4 0.7 load.1
  37.1 1.2 %front.3 = (f32[128,512]{1,0:T(8,128)S(1)}, bf16[128,512]{1,0:T(8,128)(2,1)S(1)}, bf16[128,2304]{1,0:T(8,128)(2,1)S(1)}) custom-call(f32[1,512]{1,0:T(1,128)S(1)} %bitcast.18, bf16[2304,512]{1,0:T(8,128)(2,1)S(1)} %get-tuple-element.55.enc_own, bf16[2304,512]{1,0:T(8,128)(2,1)S(1)} %get-tuple-element.56.enc_oth, ...), custom_call_target="tpu_custom_call" | custom-call | flops 905969664 | bytes 9437184 | tf_op jit(solution)/shard_map/front/pallas_call | solution.py:168
  38.3 0.5 parts.3
  38.8 0.1 collective-permute-done.1.refs_0_.refs_9_
  39.0 1.8 %collective-permute-start.6 = (bf16[128,2304]{1,0:T(8,128)(2,1)S(1)}, bf16[128,2304]{1,0:T(8,128)(2,1)S(1)}, u32[]{:S(2)}, u32[]{:S(2)}) collective-permute-start(bf16[128,2304]{1,0:T(8,128)(2,1)S(1)} %collective-permute-done.1.refs_0_.refs_9_), channel_id=1, source_target_pairs={{0,1},{1,0},{2,3},{3,2},{4,5},{5,4},{6,7},{7,6},{8,9},{9,8},{10,11... | collective-permute-start | bytes 1769480 | tf_op jit(solution)/shard_map/ppermute | solution.py:66
  40.8 0.5 collective-permute-start.10
  41.3 1.1 collective-permute-done.6.refs_1_.refs_13_
  42.5 1.2 %front.4 = (f32[128,512]{1,0:T(8,128)S(1)}, bf16[128,512]{1,0:T(8,128)(2,1)S(1)}, bf16[128,2304]{1,0:T(8,128)(2,1)S(1)}) custom-call(f32[1,512]{1,0:T(1,128)S(1)} %bitcast.19, bf16[2304,512]{1,0:T(8,128)(2,1)S(1)} %get-tuple-element.55.enc_own, bf16[2304,512]{1,0:T(8,128)(2,1)S(1)} %get-tuple-element.56.enc_oth, ...), custom_call_target="tpu_custom_call" | custom-call | flops 905969664 | bytes 9437184 | tf_op jit(solution)/shard_map/front/pallas_call | solution.py:168
  43.7 0.5 collective-permute-start.7
  44.1 0.1 collective-permute-start.5
  44.3 2.1 %front.5 = (f32[256,512]{1,0:T(8,128)S(1)}, bf16[256,512]{1,0:T(8,128)(2,1)S(1)}, bf16[128,2304]{1,0:T(8,128)(2,1)S(1)}, bf16[128,2304]{1,0:T(8,128)(2,1)S(1)}) custom-call(f32[1,512]{1,0:T(1,128)S(1)} %bitcast.20, bf16[2304,512]{1,0:T(8,128)(2,1)S(1)} %get-tuple-element.55.enc_own, bf16[2304,512]{1,0:T(8,128)(2,1)S(1)} %get-tuple-element.56.enc_oth, ...), custom_call_target="tpu_custom_call" | custom-call | flops 1811939328 | bytes 9437184 | tf_op jit(solution)/shard_map/front/pallas_call | solution.py:168
  46.4 0.5 collective-permute-start.11
  46.9 0.1 collective-permute-start.13
  47.0 0.5 parts.4
  47.5 0.8 parts.5
  48.3 0.1 add_convert_fusion.3
  48.4 1.3 %collective-permute-start.8 = (bf16[128,2304]{1,0:T(8,128)(2,1)S(1)}, bf16[128,2304]{1,0:T(8,128)(2,1)S(1)}, u32[]{:S(2)}, u32[]{:S(2)}) collective-permute-start(bf16[128,2304]{1,0:T(8,128)(2,1)S(1)} %add_convert_fusion.3), channel_id=1, source_target_pairs={{0,8},{1,25},{2,10},{3,27},{4,12},{5,29},{6,14},{7,31},{8,16},{9,1... | collective-permute-start | bytes 1769480 | tf_op jit(solution)/shard_map/ppermute | solution.py:455
  49.7 0.2 add_convert_fusion.1
  49.9 0.0 copy-start.3
  49.9 2.7 %collective-permute-start.14 = (bf16[128,2304]{1,0:T(8,128)(2,1)S(1)}, bf16[128,2304]{1,0:T(8,128)(2,1)S(1)}, u32[]{:S(2)}, u32[]{:S(2)}) collective-permute-start(bf16[128,2304]{1,0:T(8,128)(2,1)S(1)} %add_convert_fusion.1), channel_id=1, source_target_pairs={{0,32},{1,97},{2,34},{3,99},{4,36},{5,101},{6,38},{7,103},{8,40},{... | collective-permute-start | bytes 1769480 | tf_op jit(solution)/shard_map/ppermute | solution.py:455
  52.6 0.1 add_convert_fusion.2
  52.7 2.5 %collective-permute-start.12 = (bf16[128,2304]{1,0:T(8,128)(2,1)S(1)}, bf16[128,2304]{1,0:T(8,128)(2,1)S(1)}, u32[]{:S(2)}, u32[]{:S(2)}) collective-permute-start(bf16[128,2304]{1,0:T(8,128)(2,1)S(1)} %add_convert_fusion.2), channel_id=1, source_target_pairs={{0,2},{1,7},{2,4},{3,1},{4,6},{5,3},{6,0},{7,5},{8,10},{9,15},{10,... | collective-permute-start | bytes 1769480 | tf_op jit(solution)/shard_map/ppermute | solution.py:455
  55.3 1.9 %side.1 = (bf16[528,512]{1,0:T(8,128)(2,1)S(1)}, f32[512,1]{1,0:T(8,128)S(1)}, f32[1,512]{1,0:T(1,128)S(1)}) custom-call(s32[512]{0:T(512)S(1)} %copy-done.3, bf16[128,512]{1,0:T(8,128)(2,1)S(1)} %get-tuple-element.69.act_ref.refs_0_, bf16[128,512]{1,0:T(8,128)(2,1)S(1)} %get-tuple-element.59.act_ref.refs_1_, ...), custom_call_target="tpu_custom_call" | custom-call | flops 9437184 | bytes 4718592 | tf_op jit(solution)/shard_map/side/pallas_call | solution.py:238
  57.2 0.3 collective-permute-done.8
  57.5 1.9 %collective-permute-done.14 = bf16[128,2304]{1,0:T(8,128)(2,1)S(1)} collective-permute-done((bf16[128,2304]{1,0:T(8,128)(2,1)S(1)}, bf16[128,2304]{1,0:T(8,128)(2,1)S(1)}, u32[]{:S(2)}, u32[]{:S(2)}) %collective-permute-start.14) | collective-permute-done | bytes 589856 | tf_op jit(solution)/shard_map/ppermute | solution.py:455
  59.4 2.7 %collective-permute-done.12 = bf16[128,2304]{1,0:T(8,128)(2,1)S(1)} collective-permute-done((bf16[128,2304]{1,0:T(8,128)(2,1)S(1)}, bf16[128,2304]{1,0:T(8,128)(2,1)S(1)}, u32[]{:S(2)}, u32[]{:S(2)}) %collective-permute-start.12) | collective-permute-done | bytes 589856 | tf_op jit(solution)/shard_map/ppermute | solution.py:455
  62.1 0.4 fusion
  62.5 17.0 %all_to_all.16 = bf16[16,8,2304]{2,1,0:T(8,128)(2,1)S(1)} all-to-all(bf16[16,8,2304]{2,1,0:T(8,128)(2,1)S(1)} %fusion), channel_id=1, replica_groups={{0,4,16,20,42,46,58,62,64,68,80,84,106,110,122,126},{8,12,24,28,34,38,5..., dimensions={0} | all-to-all | bytes 1179648 | tf_op jit(solution)/shard_map/all_to_all | solution.py:459
  79.5 0.1 convert_reduce_fusion
  79.6 15.6 %all_to_all.17 = bf16[16,8,2304]{2,1,0:T(8,128)(2,1)S(1)} all-to-all(bf16[16,8,2304]{2,1,0:T(8,128)(2,1)S(1)} %broadcast_in_dim.8), channel_id=1, replica_groups={{0,4,16,20,42,46,58,62,64,68,80,84,106,110,122,126},{8,12,24,28,34,38,5..., dimensions={0} | all-to-all | bytes 1179648 | tf_op jit(solution)/shard_map/all_to_all | solution.py:57
  95.2 1.1 collective-permute-start.16
  96.3 2.2 %collective-permute-start.15 = (bf16[128,2304]{1,0:T(8,128)(2,1)S(1)}, bf16[128,2304]{1,0:T(8,128)(2,1)S(1)}, u32[]{:S(2)}, u32[]{:S(2)}) collective-permute-start(bf16[128,2304]{1,0:T(8,128)(2,1)S(1)} %bitcast.15), channel_id=1, source_target_pairs={{0,8},{1,25},{2,10},{3,27},{4,12},{5,29},{6,14},{7,31},{8,16},{9,1... | collective-permute-start | bytes 1769480 | tf_op jit(solution)/shard_map/ppermute | solution.py:62
  98.5 3.1 %collective-permute-start.18 = (bf16[128,2304]{1,0:T(8,128)(2,1)S(1)}, bf16[128,2304]{1,0:T(8,128)(2,1)S(1)}, u32[]{:S(2)}, u32[]{:S(2)}) collective-permute-start(bf16[128,2304]{1,0:T(8,128)(2,1)S(1)} %bitcast.16), channel_id=1, source_target_pairs={{0,1},{1,0},{2,3},{3,2},{4,5},{5,4},{6,7},{7,6},{8,9},{9,8},{10,11... | collective-permute-start | bytes 1769480 | tf_op jit(solution)/shard_map/ppermute | solution.py:66
  101.6 2.3 %collective-permute-done.17.refs_3_ = bf16[128,2304]{1,0:T(8,128)(2,1)S(1)} collective-permute-done((bf16[128,2304]{1,0:T(8,128)(2,1)S(1)}, bf16[128,2304]{1,0:T(8,128)(2,1)S(1)}, u32[]{:S(2)}, u32[]{:S(2)}) %collective-permute-start.17) | collective-permute-done | bytes 589856 | tf_op jit(solution)/shard_map/ppermute | solution.py:62
  103.9 7.0 %collective-permute-start.21 = (bf16[128,2304]{1,0:T(8,128)(2,1)S(1)}, bf16[128,2304]{1,0:T(8,128)(2,1)S(1)}, u32[]{:S(2)}, u32[]{:S(2)}) collective-permute-start(bf16[128,2304]{1,0:T(8,128)(2,1)S(1)} %collective-permute-done.17.refs_3_), channel_id=1, source_target_pairs={{0,1},{1,0},{2,3},{3,2},{4,5},{5,4},{6,7},{7,6},{8,9},{9,8},{10,11... | collective-permute-start | bytes 1769480 | tf_op jit(solution)/shard_map/ppermute | solution.py:66
  110.9 0.0 collective-permute-start.20
  111.0 0.5 collective-permute-start.19
  111.5 3.3 %grad.1 = (f32[512,512]{1,0:T(8,128)S(1)}, f32[4,2304]{1,0:T(4,128)S(1)}, bf16[512,4608]{1,0:T(8,128)(2,1)}) custom-call(bf16[528,512]{1,0:T(8,128)(2,1)S(1)} %get-tuple-element.73.left_ref, f32[512,1]{1,0:T(8,128)S(1)} %get-tuple-element.74.scale_ref, bf16[512,2304]{1,0:T(8,128)(2,1)S(1)} %get-tuple-element.60.dec_ref.refs_3_, ...), custom_call_target="tpu_custom_call" | custom-call | flops 2415919104 | bytes 4718592 | tf_op jit(solution)/shard_map/grad/pallas_call | solution.py:306
  114.8 7.0 %tail.1 = (bf16[512,4608]{1,0:T(8,128)(2,1)}, bf16[4608,512]{1,0:T(8,128)(2,1)}, f32[1,512]{1,0:T(1,128)}, f32[4,4608]{1,0:T(4,128)}) custom-call(bf16[528,512]{1,0:T(8,128)(2,1)S(1)} %get-tuple-element.73.left_ref, f32[512,1]{1,0:T(8,128)S(1)} %get-tuple-element.74.scale_ref, ...), custom_call_target="tpu_custom_call", output_to_operand_aliasing={{0}: (21, {})} | custom-call | flops 3623878656 | bytes 9437184 | tf_op jit(solution)/shard_map/tail/pallas_call | solution.py:396
  (28 shorter events, 0.2 us)
Async XLA Ops:
  0.6 2.6 %collective-permute-start = (bf16[4,4608]{1,0:T(4,128)(2,1)}, bf16[4,4608]{1,0:T(4,128)(2,1)S(1)}, u32[]{:S(2)}, u32[]{:S(2)}) collective-permute-start(bf16[4,4608]{1,0:T(4,128)(2,1)} %param.5), channel_id=1, source_target_pairs={{0,1},{1,0},{2,3},{3,2},{4,5},{5,4},{6,7},{7,6},{8,9},{9,8},{10,11... | collective-permute-start | bytes 110600 | tf_op jit(solution)/shard_map/ppermute | solution.py:66
  3.3 33.8 %copy-start.2 = (f32[512]{0:T(512)S(1)}, f32[512]{0:T(512)}, u32[]{:S(2)}) copy-start(f32[512]{0:T(512)} %param.8) | copy-start | bytes 6148
  27.5 9.6 %collective-permute-start.4 = (bf16[128,2304]{1,0:T(8,128)(2,1)S(1)}, bf16[128,2304]{1,0:T(8,128)(2,1)S(1)}, u32[]{:S(2)}, u32[]{:S(2)}) collective-permute-start(bf16[128,2304]{1,0:T(8,128)(2,1)S(1)} %bitcast.6), channel_id=1, source_target_pairs={{0,1},{1,0},{2,3},{3,2},{4,5},{5,4},{6,7},{7,6},{8,9},{9,8},{10,11... | collective-permute-start | bytes 1769480 | tf_op jit(solution)/shard_map/ppermute | solution.py:66
  29.0 9.8 %collective-permute-start.3 = (bf16[128,2304]{1,0:T(8,128)(2,1)S(1)}, bf16[128,2304]{1,0:T(8,128)(2,1)S(1)}, u32[]{:S(2)}, u32[]{:S(2)}) collective-permute-start(bf16[128,2304]{1,0:T(8,128)(2,1)S(1)} %bitcast.7), channel_id=1, source_target_pairs={{0,32},{1,97},{2,34},{3,99},{4,36},{5,101},{6,38},{7,103},{8,40},{... | collective-permute-start | bytes 1769480 | tf_op jit(solution)/shard_map/ppermute | solution.py:62
  29.0 9.8 %collective-permute-start.2 = (bf16[128,2304]{1,0:T(8,128)(2,1)S(1)}, bf16[128,2304]{1,0:T(8,128)(2,1)S(1)}, u32[]{:S(2)}, u32[]{:S(2)}) collective-permute-start(bf16[128,2304]{1,0:T(8,128)(2,1)S(1)} %bitcast.8), channel_id=1, source_target_pairs={{0,2},{1,7},{2,4},{3,1},{4,6},{5,3},{6,0},{7,5},{8,10},{9,15},{10,... | collective-permute-start | bytes 1769480 | tf_op jit(solution)/shard_map/ppermute | solution.py:62
  29.9 9.0 %collective-permute-start.1 = (bf16[128,2304]{1,0:T(8,128)(2,1)S(1)}, bf16[128,2304]{1,0:T(8,128)(2,1)S(1)}, u32[]{:S(2)}, u32[]{:S(2)}) collective-permute-start(bf16[128,2304]{1,0:T(8,128)(2,1)S(1)} %bitcast.9), channel_id=1, source_target_pairs={{0,8},{1,25},{2,10},{3,27},{4,12},{5,29},{6,14},{7,31},{8,16},{9,1... | collective-permute-start | bytes 1769480 | tf_op jit(solution)/shard_map/ppermute | solution.py:62
  31.7 2.3 %copy-start = (bf16[4608,512]{1,0:T(8,128)(2,1)S(1)}, bf16[4608,512]{1,0:T(8,128)(2,1)}, u32[]{:S(2)}) copy-start(bf16[4608,512]{1,0:T(8,128)(2,1)} %enc_ref.1) | copy-start | bytes 14155780
  34.0 2.3 %copy-start.1 = (bf16[512,4608]{1,0:T(8,128)(2,1)S(1)}, bf16[512,4608]{1,0:T(8,128)(2,1)}, u32[]{:S(2)}) copy-start(bf16[512,4608]{1,0:T(8,128)(2,1)} %dec_ref.1) | copy-start | bytes 14155780
  39.0 3.5 %collective-permute-start.6 = (bf16[128,2304]{1,0:T(8,128)(2,1)S(1)}, bf16[128,2304]{1,0:T(8,128)(2,1)S(1)}, u32[]{:S(2)}, u32[]{:S(2)}) collective-permute-start(bf16[128,2304]{1,0:T(8,128)(2,1)S(1)} %collective-permute-done.1.refs_0_.refs_9_), channel_id=1, source_target_pairs={{0,1},{1,0},{2,3},{3,2},{4,5},{5,4},{6,7},{7,6},{8,9},{9,8},{10,11... | collective-permute-start | bytes 1769480 | tf_op jit(solution)/shard_map/ppermute | solution.py:66
  40.8 3.5 %collective-permute-start.9 = (bf16[128,2304]{1,0:T(8,128)(2,1)S(1)}, bf16[128,2304]{1,0:T(8,128)(2,1)S(1)}, u32[]{:S(2)}, u32[]{:S(2)}) collective-permute-start(bf16[128,2304]{1,0:T(8,128)(2,1)S(1)} %collective-permute-done.2.refs_0_.refs_10_), channel_id=1, source_target_pairs={{0,1},{1,0},{2,3},{3,2},{4,5},{5,4},{6,7},{7,6},{8,9},{9,8},{10,11... | collective-permute-start | bytes 1769480 | tf_op jit(solution)/shard_map/ppermute | solution.py:66
  40.8 3.5 %collective-permute-start.10 = (bf16[128,2304]{1,0:T(8,128)(2,1)S(1)}, bf16[128,2304]{1,0:T(8,128)(2,1)S(1)}, u32[]{:S(2)}, u32[]{:S(2)}) collective-permute-start(bf16[128,2304]{1,0:T(8,128)(2,1)S(1)} %collective-permute-done.3.refs_1_.refs_11_), channel_id=1, source_target_pairs={{0,1},{1,0},{2,3},{3,2},{4,5},{5,4},{6,7},{7,6},{8,9},{9,8},{10,11... | collective-permute-start | bytes 1769480 | tf_op jit(solution)/shard_map/ppermute | solution.py:66
  43.7 4.6 %collective-permute-start.7 = (bf16[128,2304]{1,0:T(8,128)(2,1)S(1)}, bf16[128,2304]{1,0:T(8,128)(2,1)S(1)}, u32[]{:S(2)}, u32[]{:S(2)}) collective-permute-start(bf16[128,2304]{1,0:T(8,128)(2,1)S(1)} %get-tuple-element.61), channel_id=1, source_target_pairs={{0,1},{1,0},{2,3},{3,2},{4,5},{5,4},{6,7},{7,6},{8,9},{9,8},{10,11... | collective-permute-start | bytes 1769480 | tf_op jit(solution)/shard_map/ppermute | solution.py:66
  44.1 13.1 %collective-permute-start.5 = (bf16[128,2304]{1,0:T(8,128)(2,1)S(1)}, bf16[128,2304]{1,0:T(8,128)(2,1)S(1)}, u32[]{:S(2)}, u32[]{:S(2)}) collective-permute-start(bf16[128,2304]{1,0:T(8,128)(2,1)S(1)} %get-tuple-element.54), channel_id=1, source_target_pairs={{0,1},{1,0},{2,3},{3,2},{4,5},{5,4},{6,7},{7,6},{8,9},{9,8},{10,11... | collective-permute-start | bytes 1769480 | tf_op jit(solution)/shard_map/ppermute | solution.py:66
  46.4 6.2 %collective-permute-start.11 = (bf16[128,2304]{1,0:T(8,128)(2,1)S(1)}, bf16[128,2304]{1,0:T(8,128)(2,1)S(1)}, u32[]{:S(2)}, u32[]{:S(2)}) collective-permute-start(bf16[128,2304]{1,0:T(8,128)(2,1)S(1)} %get-tuple-element.66), channel_id=1, source_target_pairs={{0,1},{1,0},{2,3},{3,2},{4,5},{5,4},{6,7},{7,6},{8,9},{9,8},{10,11... | collective-permute-start | bytes 1769480 | tf_op jit(solution)/shard_map/ppermute | solution.py:66
  46.9 2.8 %collective-permute-start.13 = (bf16[128,2304]{1,0:T(8,128)(2,1)S(1)}, bf16[128,2304]{1,0:T(8,128)(2,1)S(1)}, u32[]{:S(2)}, u32[]{:S(2)}) collective-permute-start(bf16[128,2304]{1,0:T(8,128)(2,1)S(1)} %get-tuple-element.68), channel_id=1, source_target_pairs={{0,1},{1,0},{2,3},{3,2},{4,5},{5,4},{6,7},{7,6},{8,9},{9,8},{10,11... | collective-permute-start | bytes 1769480 | tf_op jit(solution)/shard_map/ppermute | solution.py:66
  48.4 9.1 %collective-permute-start.8 = (bf16[128,2304]{1,0:T(8,128)(2,1)S(1)}, bf16[128,2304]{1,0:T(8,128)(2,1)S(1)}, u32[]{:S(2)}, u32[]{:S(2)}) collective-permute-start(bf16[128,2304]{1,0:T(8,128)(2,1)S(1)} %add_convert_fusion.3), channel_id=1, source_target_pairs={{0,8},{1,25},{2,10},{3,27},{4,12},{5,29},{6,14},{7,31},{8,16},{9,1... | collective-permute-start | bytes 1769480 | tf_op jit(solution)/shard_map/ppermute | solution.py:455
  49.9 5.3 %copy-start.3 = (s32[512]{0:T(512)S(1)}, s32[512]{0:T(512)}, u32[]{:S(2)}) copy-start(s32[512]{0:T(512)} %order_ref.1) | copy-start | bytes 6148
  49.9 9.5 %collective-permute-start.14 = (bf16[128,2304]{1,0:T(8,128)(2,1)S(1)}, bf16[128,2304]{1,0:T(8,128)(2,1)S(1)}, u32[]{:S(2)}, u32[]{:S(2)}) collective-permute-start(bf16[128,2304]{1,0:T(8,128)(2,1)S(1)} %add_convert_fusion.1), channel_id=1, source_target_pairs={{0,32},{1,97},{2,34},{3,99},{4,36},{5,101},{6,38},{7,103},{8,40},{... | collective-permute-start | bytes 1769480 | tf_op jit(solution)/shard_map/ppermute | solution.py:455
  52.7 9.4 %collective-permute-start.12 = (bf16[128,2304]{1,0:T(8,128)(2,1)S(1)}, bf16[128,2304]{1,0:T(8,128)(2,1)S(1)}, u32[]{:S(2)}, u32[]{:S(2)}) collective-permute-start(bf16[128,2304]{1,0:T(8,128)(2,1)S(1)} %add_convert_fusion.2), channel_id=1, source_target_pairs={{0,2},{1,7},{2,4},{3,1},{4,6},{5,3},{6,0},{7,5},{8,10},{9,15},{10,... | collective-permute-start | bytes 1769480 | tf_op jit(solution)/shard_map/ppermute | solution.py:455
  95.2 8.7 %collective-permute-start.17 = (bf16[128,2304]{1,0:T(8,128)(2,1)S(1)}, bf16[128,2304]{1,0:T(8,128)(2,1)S(1)}, u32[]{:S(2)}, u32[]{:S(2)}) collective-permute-start(bf16[128,2304]{1,0:T(8,128)(2,1)S(1)} %bitcast.13), channel_id=1, source_target_pairs={{0,32},{1,97},{2,34},{3,99},{4,36},{5,101},{6,38},{7,103},{8,40},{... | collective-permute-start | bytes 1769480 | tf_op jit(solution)/shard_map/ppermute | solution.py:62
  95.2 15.7 %collective-permute-start.16 = (bf16[128,2304]{1,0:T(8,128)(2,1)S(1)}, bf16[128,2304]{1,0:T(8,128)(2,1)S(1)}, u32[]{:S(2)}, u32[]{:S(2)}) collective-permute-start(bf16[128,2304]{1,0:T(8,128)(2,1)S(1)} %bitcast.14), channel_id=1, source_target_pairs={{0,2},{1,7},{2,4},{3,1},{4,6},{5,3},{6,0},{7,5},{8,10},{9,15},{10,... | collective-permute-start | bytes 1769480 | tf_op jit(solution)/shard_map/ppermute | solution.py:62
  96.3 14.6 %collective-permute-start.15 = (bf16[128,2304]{1,0:T(8,128)(2,1)S(1)}, bf16[128,2304]{1,0:T(8,128)(2,1)S(1)}, u32[]{:S(2)}, u32[]{:S(2)}) collective-permute-start(bf16[128,2304]{1,0:T(8,128)(2,1)S(1)} %bitcast.15), channel_id=1, source_target_pairs={{0,8},{1,25},{2,10},{3,27},{4,12},{5,29},{6,14},{7,31},{8,16},{9,1... | collective-permute-start | bytes 1769480 | tf_op jit(solution)/shard_map/ppermute | solution.py:62
  98.5 16.2 %collective-permute-start.18 = (bf16[128,2304]{1,0:T(8,128)(2,1)S(1)}, bf16[128,2304]{1,0:T(8,128)(2,1)S(1)}, u32[]{:S(2)}, u32[]{:S(2)}) collective-permute-start(bf16[128,2304]{1,0:T(8,128)(2,1)S(1)} %bitcast.16), channel_id=1, source_target_pairs={{0,1},{1,0},{2,3},{3,2},{4,5},{5,4},{6,7},{7,6},{8,9},{9,8},{10,11... | collective-permute-start | bytes 1769480 | tf_op jit(solution)/shard_map/ppermute | solution.py:66
  103.9 10.9 %collective-permute-start.21 = (bf16[128,2304]{1,0:T(8,128)(2,1)S(1)}, bf16[128,2304]{1,0:T(8,128)(2,1)S(1)}, u32[]{:S(2)}, u32[]{:S(2)}) collective-permute-start(bf16[128,2304]{1,0:T(8,128)(2,1)S(1)} %collective-permute-done.17.refs_3_), channel_id=1, source_target_pairs={{0,1},{1,0},{2,3},{3,2},{4,5},{5,4},{6,7},{7,6},{8,9},{9,8},{10,11... | collective-permute-start | bytes 1769480 | tf_op jit(solution)/shard_map/ppermute | solution.py:66
  110.9 3.9 %collective-permute-start.20 = (bf16[128,2304]{1,0:T(8,128)(2,1)S(1)}, bf16[128,2304]{1,0:T(8,128)(2,1)S(1)}, u32[]{:S(2)}, u32[]{:S(2)}) collective-permute-start(bf16[128,2304]{1,0:T(8,128)(2,1)S(1)} %collective-permute-done.16.refs_2_), channel_id=1, source_target_pairs={{0,1},{1,0},{2,3},{3,2},{4,5},{5,4},{6,7},{7,6},{8,9},{9,8},{10,11... | collective-permute-start | bytes 1769480 | tf_op jit(solution)/shard_map/ppermute | solution.py:66
  111.0 3.9 %collective-permute-start.19 = (bf16[128,2304]{1,0:T(8,128)(2,1)S(1)}, bf16[128,2304]{1,0:T(8,128)(2,1)S(1)}, u32[]{:S(2)}, u32[]{:S(2)}) collective-permute-start(bf16[128,2304]{1,0:T(8,128)(2,1)S(1)} %collective-permute-done.15.refs_1_), channel_id=1, source_target_pairs={{0,1},{1,0},{2,3},{3,2},{4,5},{5,4},{6,7},{7,6},{8,9},{9,8},{10,11... | collective-permute-start | bytes 1769480 | tf_op jit(solution)/shard_map/ppermute | solution.py:66
